TPU v7x, 32 devices: a whole 2x2x4 slice. The times are simulated.
32 devices in a mesh: dp: 16 (over z, y, core), tensor: 2 (over x).
Axes of the slice: x: 2, y: 2, z: 4, core: 2. Of those that a mesh axis runs over, the one named last changes fastest.
Arguments:
- tokens: bfloat16 [8192, 2048], P(('dp', 'tensor')), may hold values from -6 to 6
- segments: int32 [16, 512], P('dp'), may hold values from 0 to 7, never falling along the last dimension, each value on 1 to 256 neighbouring positions
- gain_attn: bfloat16 [2048], P('dp'), may hold values from 0.5 to 1.5
- gain_ffn: bfloat16 [2048], P('dp'), may hold values from 0.5 to 1.5
- w_query: bfloat16 [2048, 2048], P('dp', 'tensor'), may hold values from -0.125 to 0.125
- w_key: bfloat16 [2048, 2048], P('dp', 'tensor'), may hold values from -0.125 to 0.125
- w_value: bfloat16 [2048, 2048], P('dp', 'tensor'), may hold values from -0.125 to 0.125
- w_out: bfloat16 [2048, 2048], P('dp', 'tensor'), may hold values from -3 to 3
- w_gate: bfloat16 [2048, 8192], P('dp', 'tensor'), may hold values from -0.125 to 0.125
- w_up: bfloat16 [2048, 8192], P('dp', 'tensor'), may hold values from -0.125 to 0.125
- w_down: bfloat16 [2048, 8192], P('dp', 'tensor'), may hold values from -0.0625 to 0.0625
- cotangent: bfloat16 [8192, 2048], P(('dp', 'tensor')), may hold values from -6 to 6
Outputs:
- output: bfloat16 [8192, 2048], P(('dp', 'tensor'))
- grad_tokens: float32 [8192, 2048], P(('dp', 'tensor'))
- grad_gain_attn: float32 [2048], P('dp')
- grad_gain_ffn: float32 [2048], P('dp')
- grad_query: float32 [2048, 2048], P('dp', 'tensor')
- grad_key: float32 [2048, 2048], P('dp', 'tensor')
- grad_value: float32 [2048, 2048], P('dp', 'tensor')
- grad_out: float32 [2048, 2048], P('dp', 'tensor')
- grad_gate: float32 [2048, 8192], P('dp', 'tensor')
- grad_up: float32 [2048, 8192], P('dp', 'tensor')
- grad_down: float32 [2048, 8192], P('dp', 'tensor')
Inputs may be any that keep to these rules, and one draw needn't show every extreme that they name: `segments`: in each row, document numbers never fall; a document holds 1 to 256 tokens, and some document holds exactly 256.
All inputs are finite; a program needn't handle non-finite values.
Results may differ from a plain program's by a relative error of at most 0.014.
Values may be sent and summed in bfloat16 or wider, within the bound.
No kernel may reach another device: no remote copies, remote signals or barrier semaphores. Data moves between devices by JAX's collectives and lax.ppermute only.
A program may use at most 320 MiB of HBM per device.

v0:
```python
import math

import jax
import jax.numpy as jnp
from jax import lax
from jax.sharding import PartitionSpec as P

HEAD_DIM = 128
SEQ_LEN = 512


epsilon = 1e-05
theta = 10000.0


def positions_of(segment_row):
    length = segment_row.shape[-1]
    places = jnp.arange(length, dtype=jnp.int32)
    starts = jnp.concatenate([jnp.ones((1,), jnp.bool_), segment_row[1:] != segment_row[:-1]])
    begins = lax.cummax(jnp.where(starts, places, 0), axis=0)
    return places - begins


def rotary_tables(positions, half):
    freqs = theta ** (-(jnp.arange(half, dtype=jnp.float32) * 2.0 / (2 * half)))
    angles = positions.astype(jnp.float32)[..., None] * freqs
    return (jnp.cos(angles), jnp.sin(angles))


def rotate(values, cosine, sine):
    half = values.shape[-1] // 2
    first = values[..., :half]
    second = values[..., half:]
    cosine = cosine[:, None, :]
    sine = sine[:, None, :]
    return jnp.concatenate(
        [first * cosine - second * sine, second * cosine + first * sine], axis=-1
    )


def unrotate(values, cosine, sine):
    half = values.shape[-1] // 2
    first = values[..., :half]
    second = values[..., half:]
    cosine = cosine[:, None, :]
    sine = sine[:, None, :]
    return jnp.concatenate(
        [first * cosine + second * sine, second * cosine - first * sine], axis=-1
    )


def normalize(rows):
    scale = lax.rsqrt(jnp.mean(rows * rows, axis=-1, keepdims=True) + epsilon)
    return (rows * scale, scale)


def norm_back(grad_normed, unit_rows, scale, gain):
    inner = grad_normed * gain
    mean_term = jnp.mean(inner * unit_rows, axis=-1, keepdims=True)
    return (scale * (inner - unit_rows * mean_term), jnp.sum(grad_normed * unit_rows, axis=0))


def matmul(left, right):
    return jnp.dot(left, right, preferred_element_type=jnp.float32)


def with_right_turned(left, right):
    return lax.dot_general(
        left, right, (((1,), (1,)), ((), ())), preferred_element_type=jnp.float32
    )


def with_left_turned(left, right):
    return lax.dot_general(
        left, right, (((0,), (0,)), ((), ())), preferred_element_type=jnp.float32
    )


def local(
    tokens,
    segments,
    gain_attn,
    gain_ffn,
    w_query,
    w_key,
    w_value,
    w_out,
    w_gate,
    w_up,
    w_down,
    cotangent,
):
    seq_len = segments.shape[1]
    head_dim = HEAD_DIM
    heads_width = w_query.shape[1]
    local_heads = heads_width // head_dim
    scale_dot = 1.0 / math.sqrt(head_dim)
    shift = -math.log(SEQ_LEN)
    block_rows = math.gcd(seq_len, 512)
    block_starts = jnp.arange(seq_len // block_rows, dtype=jnp.int32) * block_rows
    wq_all, wk_all, wv_all, wo_all, gain_first = (
        lax.all_gather(w_query, "dp", axis=0, tiled=True),
        lax.all_gather(w_key, "dp", axis=0, tiled=True),
        lax.all_gather(w_value, "dp", axis=0, tiled=True),
        lax.all_gather(w_out, "dp", axis=0, tiled=True),
        lax.all_gather(gain_attn, "dp", axis=0, tiled=True),
    )
    gain_first = gain_first.astype(jnp.float32)
    inputs = tokens.astype(jnp.float32)
    unit_one, scale_one = normalize(inputs)
    rows_one = lax.all_gather(
        (unit_one * gain_first).astype(jnp.bfloat16), "tensor", axis=0, tiled=True
    )
    row_segments = segments[0]
    cosine, sine = rotary_tables(positions_of(row_segments), head_dim // 2)
    places = jnp.arange(seq_len, dtype=jnp.int32)

    def split_heads(flat):
        return flat.reshape(seq_len, local_heads, head_dim)

    queries = rotate(split_heads(matmul(rows_one, wq_all)), cosine, sine).astype(jnp.bfloat16)
    keys_rot = rotate(split_heads(matmul(rows_one, wk_all)), cosine, sine).astype(jnp.bfloat16)
    values = split_heads(matmul(rows_one, wv_all)).astype(jnp.bfloat16)

    def block_weights(start):
        row_places = start + jnp.arange(block_rows, dtype=jnp.int32)
        live = (row_segments[:, None] == row_segments[None, :]) & (
            places[None, :] <= row_places[:, None]
        )
        dots = (
            jnp.einsum("qhd,khd->hqk", queries, keys_rot, preferred_element_type=jnp.float32)
            * scale_dot
        )
        return (queries, jnp.where(live[None], jax.nn.sigmoid(dots + shift), 0.0))

    def forward_block(start):
        unused, probs = block_weights(start)
        return jnp.einsum(
            "hqk,khd->qhd", probs.astype(jnp.bfloat16), values, preferred_element_type=jnp.float32
        )

    mixed = lax.map(forward_block, block_starts)
    mixed_low = mixed.reshape(seq_len, heads_width).astype(jnp.bfloat16)
    middle = inputs + lax.psum_scatter(
        with_right_turned(mixed_low, wo_all), "tensor", scatter_dimension=0, tiled=True
    )
    wg_all, wu_all, wd_all, gain_second = (
        lax.all_gather(w_gate, "dp", axis=0, tiled=True),
        lax.all_gather(w_up, "dp", axis=0, tiled=True),
        lax.all_gather(w_down, "dp", axis=0, tiled=True),
        lax.all_gather(gain_ffn, "dp", axis=0, tiled=True),
    )
    gain_second = gain_second.astype(jnp.float32)
    unit_two, scale_two = normalize(middle)
    rows_two = lax.all_gather(
        (unit_two * gain_second).astype(jnp.bfloat16), "tensor", axis=0, tiled=True
    )
    gate = matmul(rows_two, wg_all)
    upward = matmul(rows_two, wu_all)
    hidden = (jax.nn.silu(gate) * upward).astype(jnp.bfloat16)
    output = (
        middle
        + lax.psum_scatter(
            with_right_turned(hidden, wd_all).astype(jnp.bfloat16),
            "tensor",
            scatter_dimension=0,
            tiled=True,
        ).astype(jnp.float32)
    ).astype(jnp.bfloat16)
    wq_back, wk_back, wv_back, wo_back, wg_back, wu_back, wd_back = (
        lax.all_gather(w_query, "dp", axis=0, tiled=True),
        lax.all_gather(w_key, "dp", axis=0, tiled=True),
        lax.all_gather(w_value, "dp", axis=0, tiled=True),
        lax.all_gather(w_out, "dp", axis=0, tiled=True),
        lax.all_gather(w_gate, "dp", axis=0, tiled=True),
        lax.all_gather(w_up, "dp", axis=0, tiled=True),
        lax.all_gather(w_down, "dp", axis=0, tiled=True),
    )
    grad_rows = lax.all_gather(cotangent, "tensor", axis=0, tiled=True)
    grad_hidden = matmul(grad_rows, wd_back)
    grad_down = with_left_turned(grad_rows, hidden)
    gate_sig = jax.nn.sigmoid(gate)
    grad_gate_act = (grad_hidden * upward * gate_sig * (1.0 + gate * (1.0 - gate_sig))).astype(
        jnp.bfloat16
    )
    grad_up_act = (grad_hidden * gate * gate_sig).astype(jnp.bfloat16)
    grad_gate = with_left_turned(rows_two, grad_gate_act)
    grad_up = with_left_turned(rows_two, grad_up_act)
    grad_gate, grad_up, grad_down = (
        lax.psum_scatter(grad_gate, "dp", scatter_dimension=0, tiled=True),
        lax.psum_scatter(grad_up, "dp", scatter_dimension=0, tiled=True),
        lax.psum_scatter(grad_down, "dp", scatter_dimension=0, tiled=True),
    )
    grad_normed_two = lax.psum_scatter(
        with_right_turned(grad_gate_act, wg_back) + with_right_turned(grad_up_act, wu_back),
        "tensor",
        scatter_dimension=0,
        tiled=True,
    )
    grad_unit_two, gain_two_part = norm_back(grad_normed_two, unit_two, scale_two, gain_second)
    grad_middle = cotangent.astype(jnp.float32) + grad_unit_two
    grad_branch = lax.all_gather(grad_middle.astype(jnp.bfloat16), "tensor", axis=0, tiled=True)
    grad_mixed = split_heads(matmul(grad_branch, wo_back)).astype(jnp.bfloat16)
    grad_out = with_left_turned(grad_branch, mixed_low)

    def backward_block(carry, start):
        key_total, value_total = carry
        query_block, probs = block_weights(start)
        grad_probs = jnp.einsum(
            "qhd,khd->hqk", grad_mixed, values, preferred_element_type=jnp.float32
        )
        grad_dots = (grad_probs * probs * (1.0 - probs)).astype(jnp.bfloat16)
        query_grad = (
            jnp.einsum("hqk,khd->qhd", grad_dots, keys_rot, preferred_element_type=jnp.float32)
            * scale_dot
        )
        key_total = (
            key_total
            + jnp.einsum("hqk,qhd->khd", grad_dots, query_block, preferred_element_type=jnp.float32)
            * scale_dot
        )
        value_total = value_total + jnp.einsum(
            "hqk,qhd->khd",
            probs.astype(jnp.bfloat16),
            grad_mixed,
            preferred_element_type=jnp.float32,
        )
        return ((key_total, value_total), query_grad)

    empty = jnp.zeros((seq_len, local_heads, head_dim), jnp.float32)
    (grad_keys, grad_values), grad_queries = lax.scan(backward_block, (empty, empty), block_starts)
    grad_queries = grad_queries.reshape(seq_len, local_heads, head_dim)
    grad_queries = (
        unrotate(grad_queries, cosine, sine).reshape(seq_len, heads_width).astype(jnp.bfloat16)
    )
    grad_keys = unrotate(grad_keys, cosine, sine).reshape(seq_len, heads_width).astype(jnp.bfloat16)
    grad_values = grad_values.reshape(seq_len, heads_width).astype(jnp.bfloat16)
    grad_query = with_left_turned(rows_one, grad_queries)
    grad_key = with_left_turned(rows_one, grad_keys)
    grad_value = with_left_turned(rows_one, grad_values)
    total = with_right_turned(grad_queries, wq_back)
    total = total + with_right_turned(grad_keys, wk_back)
    grad_normed_one = lax.psum_scatter(
        total + with_right_turned(grad_values, wv_back), "tensor", scatter_dimension=0, tiled=True
    )
    grad_unit_one, gain_one_part = norm_back(grad_normed_one, unit_one, scale_one, gain_first)
    grad_tokens = grad_middle + grad_unit_one
    gain_one_sum, gain_two_sum = lax.psum((gain_one_part, gain_two_part), "tensor")
    grad_query, grad_key, grad_value, grad_out, grad_gain_one, grad_gain_two = (
        lax.psum_scatter(grad_query, "dp", scatter_dimension=0, tiled=True),
        lax.psum_scatter(grad_key, "dp", scatter_dimension=0, tiled=True),
        lax.psum_scatter(grad_value, "dp", scatter_dimension=0, tiled=True),
        lax.psum_scatter(grad_out, "dp", scatter_dimension=0, tiled=True),
        lax.psum_scatter(gain_one_sum, "dp", scatter_dimension=0, tiled=True),
        lax.psum_scatter(gain_two_sum, "dp", scatter_dimension=0, tiled=True),
    )
    return (
        output,
        grad_tokens,
        grad_gain_one,
        grad_gain_two,
        grad_query,
        grad_key,
        grad_value,
        grad_out,
        grad_gate,
        grad_up,
        grad_down,
    )


def solution(mesh):
    placed = (
        P(("dp", "tensor"), None),
        P("dp", None),
        P("dp"),
        P("dp"),
        P("dp", "tensor"),
        P("dp", "tensor"),
        P("dp", "tensor"),
        P("dp", "tensor"),
        P("dp", "tensor"),
        P("dp", "tensor"),
        P("dp", "tensor"),
        P(("dp", "tensor"), None),
    )
    return jax.shard_map(
        local,
        mesh=mesh,
        in_specs=placed,
        out_specs=(
            P(("dp", "tensor"), None),
            P(("dp", "tensor"), None),
            P("dp"),
            P("dp"),
            P("dp", "tensor"),
            P("dp", "tensor"),
            P("dp", "tensor"),
            P("dp", "tensor"),
            P("dp", "tensor"),
            P("dp", "tensor"),
            P("dp", "tensor"),
        ),
        check_vma=False,
    )
```

profile of v0, /device:TPU:0, one launch (start us, length us, event | category | flops | bytes accessed | tf_op | source)
XLA Modules:
  0.0 2506.8 jit_solution(13471755629542058284)
XLA Ops:
  7.2 23.2 all-gather
  41.2 24.4 all-gather.14.cloned.1.call-done
  65.5 52.8 %all-gather.18.cloned.1.call-done = bf16[2048,1024]{1,0:T(8,128)(2,1)} async-done(((bf16[128,1024]{1,0:T(8,128)(2,1)}), bf16[2048,1024]{1,0:T(8,128)(2,1)}) %all-gather.18.cloned.1.call-update) | async-done | bytes 4194320 | tf_op jit(solution)/shard_map/all_gather | solution.py:102
  123.9 45.6 %all-gather.20.cloned.1.call-done = bf16[2048,1024]{1,0:T(8,128)(2,1)} async-done(((bf16[128,1024]{1,0:T(8,128)(2,1)}), bf16[2048,1024]{1,0:T(8,128)(2,1)}) %all-gather.20.cloned.1.call-update) | async-done | bytes 4194320 | tf_op jit(solution)/shard_map/all_gather | solution.py:103
  179.4 41.4 %all-gather.16.cloned.1.call-done = bf16[2048,1024]{1,0:T(8,128)(2,1)} async-done(((bf16[128,1024]{1,0:T(8,128)(2,1)}), bf16[2048,1024]{1,0:T(8,128)(2,1)}) %all-gather.16.cloned.1.call-update) | async-done | bytes 4194320 | tf_op jit(solution)/shard_map/all_gather | solution.py:104
  234.9 37.3 %all-gather.22.cloned.1.call-done = bf16[2048,1024]{1,0:T(8,128)(2,1)} async-done(((bf16[128,1024]{1,0:T(8,128)(2,1)}), bf16[2048,1024]{1,0:T(8,128)(2,1)}) %all-gather.22.cloned.1.call-update) | async-done | bytes 4194320 | tf_op jit(solution)/shard_map/all_gather | solution.py:105
  279.4 18.8 all-gather.1
  298.2 33.5 %reduce-scatter.12.cloned.1.call-done = f32[256,2048]{1,0:T(8,128)} async-done(((f32[512,2048]{1,0:T(8,128)}), f32[256,2048]{1,0:T(8,128)}) %reduce-scatter.12.cloned.1.call-update) | async-done | bytes 2097168 | tf_op jit(solution)/shard_map/reduce_scatter | solution.py:144
  338.0 30.4 %all-gather.24.cloned.1.call-done = bf16[512,2048]{1,0:T(8,128)(2,1)} async-done(((bf16[256,2048]{1,0:T(8,128)(2,1)}), bf16[512,2048]{1,0:T(8,128)(2,1)}) %all-gather.24.cloned.1.call-update) | async-done | bytes 2097168 | tf_op jit(solution)/shard_map/all_gather | solution.py:155
  368.4 129.3 %all-gather.26.cloned.1.call-done = bf16[2048,4096]{1,0:T(8,128)(2,1)} async-done(((bf16[128,4096]{1,0:T(8,128)(2,1)}), bf16[2048,4096]{1,0:T(8,128)(2,1)}) %all-gather.26.cloned.1.call-update) | async-done | bytes 16777232 | tf_op jit(solution)/shard_map/all_gather | solution.py:148
  497.7 14.9 fusion.35
  512.6 112.5 %all-gather.28.cloned.1.call-done = bf16[2048,4096]{1,0:T(8,128)(2,1)} async-done(((bf16[128,4096]{1,0:T(8,128)(2,1)}), bf16[2048,4096]{1,0:T(8,128)(2,1)}) %all-gather.28.cloned.1.call-update) | async-done | bytes 16777232 | tf_op jit(solution)/shard_map/all_gather | solution.py:149
  625.1 15.0 fusion.36
  640.1 17.8 all-gather.32.cloned.1.call-done
  657.9 129.3 %all-gather.30.cloned.1.call-done = bf16[2048,4096]{1,0:T(8,128)(2,1)} async-done(((bf16[128,4096]{1,0:T(8,128)(2,1)}), bf16[2048,4096]{1,0:T(8,128)(2,1)}) %all-gather.30.cloned.1.call-update) | async-done | bytes 16777232 | tf_op jit(solution)/shard_map/all_gather | solution.py:150
  787.3 22.1 multiply_convert_fusion.1
  809.3 15.3 fusion.37
  824.6 14.4 convolution_add_fusion
  839.1 52.6 %reduce-scatter.16.cloned.1.call-done = f32[256,2048]{1,0:T(8,128)} async-done(((f32[512,2048]{1,0:T(8,128)}), f32[256,2048]{1,0:T(8,128)}) %reduce-scatter.16.cloned.1.call-update) | async-done | bytes 2097168 | tf_op jit(solution)/shard_map/reduce_scatter | solution.py:194
  896.8 33.2 %all-gather.34.cloned.1.call-done = bf16[512,2048]{1,0:T(8,128)(2,1)} async-done(((bf16[256,2048]{1,0:T(8,128)(2,1)}), bf16[512,2048]{1,0:T(8,128)(2,1)}) %all-gather.34.cloned.1.call-update) | async-done | bytes 2097168 | tf_op jit(solution)/shard_map/all_gather | solution.py:202
  964.6 14.6 convolution_convert_fusion
  979.3 18.6 convolution_bitcast_fusion
  1030.4 17.6 fusion.44
  1048.1 19.2 fusion.45
  1072.3 61.6 %all-reduce.2 = (f32[2048]{0:T(1024)S(1)}, f32[2048]{0:T(1024)S(1)}) all-reduce(f32[2048]{0:T(1024)S(1)} %get-tuple-element.97, f32[2048]{0:T(1024)S(1)} %copy-done.31), channel_id=6, replica_groups=mesh['dp'=16,'tensor'=2] {'dp'}, use_global_device_ids=true, to_apply=%region_12.13.clone | all-reduce | flops 4096 | bytes 32768
  1145.2 245.2 %reduce-scatter.32.cloned.1.call-done = f32[128,4096]{0,1:T(8,128)} async-done(((f32[2048,4096]{0,1:T(8,128)}), f32[128,4096]{0,1:T(8,128)}) %reduce-scatter.32.cloned.1.call-update) | async-done | bytes 2097168 | tf_op jit(solution)/shard_map/reduce_scatter | solution.py:192
  1393.3 105.4 %reduce-scatter.20.cloned.1.call-done = f32[128,1024]{1,0:T(8,128)} async-done(((f32[2048,1024]{1,0:T(8,128)}), f32[128,1024]{1,0:T(8,128)}) %reduce-scatter.20.cloned.1.call-update) | async-done | bytes 524304 | tf_op jit(solution)/shard_map/reduce_scatter | solution.py:250
  1498.7 108.9 %reduce-scatter.22.cloned.1.call-done = f32[128,1024]{1,0:T(8,128)} async-done(((f32[2048,1024]{1,0:T(8,128)}), f32[128,1024]{1,0:T(8,128)}) %reduce-scatter.22.cloned.1.call-update) | async-done | bytes 524304 | tf_op jit(solution)/shard_map/reduce_scatter | solution.py:251
  1607.7 109.0 %reduce-scatter.24.cloned.1.call-done = f32[128,1024]{1,0:T(8,128)} async-done(((f32[2048,1024]{1,0:T(8,128)}), f32[128,1024]{1,0:T(8,128)}) %reduce-scatter.24.cloned.1.call-update) | async-done | bytes 524304 | tf_op jit(solution)/shard_map/reduce_scatter | solution.py:252
  1716.7 108.8 %reduce-scatter.26.cloned.1.call-done = f32[128,1024]{1,0:T(8,128)} async-done(((f32[2048,1024]{1,0:T(8,128)}), f32[128,1024]{1,0:T(8,128)}) %reduce-scatter.26.cloned.1.call-update) | async-done | bytes 524304 | tf_op jit(solution)/shard_map/reduce_scatter | solution.py:253
  1825.5 337.4 %reduce-scatter.28.cloned.1.call-done = f32[128,4096]{1,0:T(8,128)} async-done(((f32[2048,4096]{1,0:T(8,128)}), f32[128,4096]{1,0:T(8,128)}) %reduce-scatter.28.cloned.1.call-update) | async-done | bytes 2097168 | tf_op jit(solution)/shard_map/reduce_scatter | solution.py:190
  2162.9 336.6 %reduce-scatter.30.cloned.1.call-done = f32[128,4096]{1,0:T(8,128)} async-done(((f32[2048,4096]{1,0:T(8,128)}), f32[128,4096]{1,0:T(8,128)}) %reduce-scatter.30.cloned.1.call-update) | async-done | bytes 2097168 | tf_op jit(solution)/shard_map/reduce_scatter | solution.py:191
  (202 shorter events, 143.5 us)
Async XLA Ops:
  7.2 58.3 %all-gather.14.cloned.1.call-start = ((), (), s32[]{:S(2)}) async-start(), calls=%async_computation.11 | async-start | bytes 3145728 | tf_op jit(solution)/shard_map/all_gather | solution.py:111
  35.0 83.3 %all-gather.18.cloned.1.call-start = ((), (), s32[]{:S(2)}) async-start(), calls=%async_computation.13 | async-start | bytes 4456448 | tf_op jit(solution)/shard_map/all_gather | solution.py:102
  35.7 133.8 %all-gather.20.cloned.1.call-start = ((), (), s32[]{:S(2)}) async-start(), calls=%async_computation.14 | async-start | bytes 4456448 | tf_op jit(solution)/shard_map/all_gather | solution.py:103
  36.5 184.3 %all-gather.16.cloned.1.call-start = ((), (), s32[]{:S(2)}) async-start(), calls=%async_computation.12 | async-start | bytes 4456448 | tf_op jit(solution)/shard_map/all_gather | solution.py:104
  37.1 235.1 %all-gather.22.cloned.1.call-start = ((), (), s32[]{:S(2)}) async-start(), calls=%async_computation.15 | async-start | bytes 4456448 | tf_op jit(solution)/shard_map/all_gather | solution.py:105
  37.6 294.1 %reduce-scatter.12.cloned.1.call-start = ((), (), s32[]{:S(2)}) async-start(), calls=%async_computation.16 | async-start | bytes 6291456 | tf_op jit(solution)/shard_map/reduce_scatter | solution.py:144
  41.1 135.6 %copy-start.17 = (f32[512,64]{1,0:T(8,128)}, f32[512,64]{1,0:T(8,128)S(1)}, u32[]{:S(2)}) copy-start(f32[512,64]{1,0:T(8,128)S(1)} %get-tuple-element.126) | copy-start | bytes 393220
  278.8 53.0 %copy-start.3 = (bf16[256,2048]{1,0:T(8,128)(2,1)S(1)}, bf16[256,2048]{1,0:T(8,128)(2,1)}, u32[]{:S(2)}) copy-start(bf16[256,2048]{1,0:T(8,128)(2,1)} %param.12) | copy-start | bytes 3145732
  278.8 89.6 %all-gather.24.cloned.1.call-start = ((), (), s32[]{:S(2)}) async-start(), calls=%async_computation.17 | async-start | bytes 3145728 | tf_op jit(solution)/shard_map/all_gather | solution.py:155
  298.2 596.4 %copy-start.27 = (f32[16,1,128]{2,1,0:T(1,128)}, f32[16,1,128]{2,1,0:T(1,128)S(1)}, u32[]{:S(2)}) copy-start(f32[16,1,128]{2,1,0:T(1,128)S(1)} %convert_element_type.125) | copy-start | bytes 24580
  333.7 560.9 %copy-start.1 = (f32[256,2048]{1,0:T(8,128)}, f32[256,2048]{1,0:T(8,128)S(1)}, u32[]{:S(2)}) copy-start(f32[256,2048]{1,0:T(8,128)S(1)} %get-tuple-element.104) | copy-start | bytes 6291460
  333.7 560.9 %copy-start.33 = (f32[256]{0:T(256)}, f32[256]{0:T(256)S(1)}, u32[]{:S(2)}) copy-start(f32[256]{0:T(256)S(1)} %add_rsqrt_fusion) | copy-start | bytes 3076
  335.1 162.6 %all-gather.26.cloned.1.call-start = ((), (), s32[]{:S(2)}) async-start(), calls=%async_computation.18 | async-start | bytes 17825792 | tf_op jit(solution)/shard_map/all_gather | solution.py:148
  335.8 289.3 %all-gather.28.cloned.1.call-start = ((), (), s32[]{:S(2)}) async-start(), calls=%async_computation.19 | async-start | bytes 17825792 | tf_op jit(solution)/shard_map/all_gather | solution.py:149
  336.6 321.3 %all-gather.32.cloned.1.call-start = ((), (), s32[]{:S(2)}) async-start(), calls=%async_computation.22 | async-start | bytes 3145728 | tf_op jit(solution)/shard_map/all_gather | solution.py:179
  337.2 450.1 %all-gather.30.cloned.1.call-start = ((), (), s32[]{:S(2)}) async-start(), calls=%async_computation.20 | async-start | bytes 17825792 | tf_op jit(solution)/shard_map/all_gather | solution.py:150
  337.9 553.8 %reduce-scatter.16.cloned.1.call-start = ((), (), s32[]{:S(2)}) async-start(), calls=%async_computation.23 | async-start | bytes 6291456 | tf_op jit(solution)/shard_map/reduce_scatter | solution.py:194
  839.1 56.1 %copy-start.6 = (bf16[256,2048]{1,0:T(8,128)(2,1)S(1)}, bf16[256,2048]{1,0:T(8,128)(2,1)}, u32[]{:S(2)}) copy-start(bf16[256,2048]{1,0:T(8,128)(2,1)} %param.23) | copy-start | bytes 3145732
  839.1 91.0 %all-gather.34.cloned.1.call-start = ((), (), s32[]{:S(2)}) async-start(), calls=%async_computation.24 | async-start | bytes 3145728 | tf_op jit(solution)/shard_map/all_gather | solution.py:202
  896.8 172.8 %reduce-scatter.18.cloned.1.call-start = ((), (), s32[]{:S(2)}) async-start(), calls=%async_computation.25 | async-start | bytes 6291456 | tf_op jit(solution)/shard_map/reduce_scatter | solution.py:243
  964.6 174.9 %reduce-scatter.14.cloned.1.call-start = ((), (), s32[]{:S(2)}) async-start(), calls=%async_computation.21 | async-start | bytes 3145728 | tf_op jit(solution)/shard_map/reduce_scatter | solution.py:163
  979.3 411.2 %reduce-scatter.32.cloned.1.call-start = ((), (), s32[]{:S(2)}) async-start(), calls=%async_computation.32 | async-start | bytes 35651584 | tf_op jit(solution)/shard_map/reduce_scatter | solution.py:192
  997.9 500.8 %reduce-scatter.20.cloned.1.call-start = ((), (), s32[]{:S(2)}) async-start(), calls=%async_computation.26 | async-start | bytes 8912896 | tf_op jit(solution)/shard_map/reduce_scatter | solution.py:250
  1006.4 601.3 %reduce-scatter.22.cloned.1.call-start = ((), (), s32[]{:S(2)}) async-start(), calls=%async_computation.27 | async-start | bytes 8912896 | tf_op jit(solution)/shard_map/reduce_scatter | solution.py:251
  1013.7 703.0 %reduce-scatter.24.cloned.1.call-start = ((), (), s32[]{:S(2)}) async-start(), calls=%async_computation.28 | async-start | bytes 8912896 | tf_op jit(solution)/shard_map/reduce_scatter | solution.py:252
  1021.0 804.5 %reduce-scatter.26.cloned.1.call-start = ((), (), s32[]{:S(2)}) async-start(), calls=%async_computation.29 | async-start | bytes 8912896 | tf_op jit(solution)/shard_map/reduce_scatter | solution.py:253
  1028.8 1134.1 %reduce-scatter.28.cloned.1.call-start = ((), (), s32[]{:S(2)}) async-start(), calls=%async_computation.30 | async-start | bytes 35651584 | tf_op jit(solution)/shard_map/reduce_scatter | solution.py:190
  1048.0 1451.5 %reduce-scatter.30.cloned.1.call-start = ((), (), s32[]{:S(2)}) async-start(), calls=%async_computation.31 | async-start | bytes 35651584 | tf_op jit(solution)/shard_map/reduce_scatter | solution.py:191
  1067.3 72.2 %copy-start.2 = (f32[256,2048]{1,0:T(8,128)S(1)}, f32[256,2048]{1,0:T(8,128)}, u32[]{:S(2)}) copy-start(f32[256,2048]{1,0:T(8,128)} %copy-done.1) | copy-start | bytes 6291460
  1067.3 72.2 %copy-start.28 = (f32[16,1,128]{2,1,0:T(1,128)S(1)}, f32[16,1,128]{2,1,0:T(1,128)}, u32[]{:S(2)}) copy-start(f32[16,1,128]{2,1,0:T(1,128)} %copy-done.27) | copy-start | bytes 24580
  1067.3 72.1 %copy-start.34 = (f32[256]{0:T(256)S(1)}, f32[256]{0:T(256)}, u32[]{:S(2)}) copy-start(f32[256]{0:T(256)} %copy-done.33) | copy-start | bytes 3076
  1067.3 72.1 %copy-start.38 = (f32[256]{0:T(256)S(1)}, f32[256]{0:T(256)}, u32[]{:S(2)}) copy-start(f32[256]{0:T(256)} %copy-done.37) | copy-start | bytes 3076
  (39 other events, 327.2 us)
Sparse Core Ops, SparseCore 0:
  35.1 30.3 all-gather.13
  67.7 50.5 all-gather.17
  120.4 49.0 all-gather.19
  171.6 49.1 all-gather.15
  222.8 49.3 all-gather.21
  278.9 52.7 reduce-scatter.11
  335.2 33.1 all-gather.23
  370.8 126.8 all-gather.25
  500.1 124.9 all-gather.27
  626.6 31.2 all-gather.31
  660.3 126.8 all-gather.29
  839.2 52.4 reduce-scatter.15
  896.9 33.1 all-gather.33
  964.7 54.2 reduce-scatter.17
  1021.8 31.8 reduce-scatter.13
  1057.7 332.6 reduce-scatter.31
  1394.9 103.7 reduce-scatter.19
  1503.2 104.4 reduce-scatter.21
  1612.3 104.3 reduce-scatter.23
  1721.2 104.3 reduce-scatter.25
  1830.4 332.5 reduce-scatter.27
  2167.8 331.7 reduce-scatter.29
where the time goes:
time: 2520 us; the launch traced here: 2510 us
  waiting for transfers between devices  2100 us (83%)
  matrix products  232 us (9%)
  blocking collectives  109 us (4%)
  other arithmetic  28.7 us (1%)
    reduce_scatter x1, waiting for transfers between devices, local(): lax.psum_scatter(grad_gate, 'dp', scatter_dimension=0, tiled=True)  337 us
    reduce_scatter x1, waiting for transfers between devices, local(): lax.psum_scatter(grad_up, 'dp', scatter_dimension=0, tiled=True)  337 us
    reduce_scatter x1, waiting for transfers between devices, local(): lax.psum_scatter(grad_down, 'dp', scatter_dimension=0, tiled=True)  245 us
    all_gather x1, waiting for transfers between devices, local(): lax.all_gather(w_down, 'dp', axis=0, tiled=True)  129 us
    all_gather x1, waiting for transfers between devices, local(): lax.all_gather(w_gate, 'dp', axis=0, tiled=True)  129 us
    all_gather x1, waiting for transfers between devices, local(): lax.all_gather(w_up, 'dp', axis=0, tiled=True)  112 us
    reduce_scatter x1, waiting for transfers between devices, local(): lax.psum_scatter(grad_value, 'dp', scatter_dimension=0, tiled=True)  109 us
    reduce_scatter x1, waiting for transfers between devices, local(): lax.psum_scatter(grad_key, 'dp', scatter_dimension=0, tiled=True)  109 us
  transfers between devices with their start and end apart: 22, of which 20 were waited for; matrix products, arithmetic and copies ran while one was open for 7% of the time, Pallas kernels for 0%

commit v1 on v0

v1 whole, which is shorter than its diff:
```python
import math

import jax
import jax.numpy as jnp
from jax import lax
from jax.sharding import PartitionSpec as P

HEAD_DIM = 128
SEQ_LEN = 512
PLANE = 4
CHUNKS = 4

epsilon = 1e-05
theta = 10000.0
low = jnp.bfloat16
f32 = jnp.float32


def dot(left, right):
    return jnp.dot(left, right, preferred_element_type=f32)


def dot_rt(left, right):
    return lax.dot_general(left, right, (((1,), (1,)), ((), ())), preferred_element_type=f32)


def dot_lt(left, right):
    return lax.dot_general(left, right, (((0,), (0,)), ((), ())), preferred_element_type=f32)


def after(value, *earlier):
    return lax.optimization_barrier((value,) + earlier)[0]


def swap_x(value):
    return lax.ppermute(value, "tensor", [(0, 1), (1, 0)])


def swap_dp(value, flip):
    count = lax.axis_size("dp")
    return lax.ppermute(value, "dp", [(i, i ^ flip) for i in range(count)])


def swap_c(value):
    return swap_dp(value, 1)


def swap_y(value):
    return swap_dp(value, 2)


def line_shift(value, planes, way):
    pairs = []
    for p in planes:
        pairs += [(p * PLANE + j, (p + way) * PLANE + j) for j in range(PLANE)]
    return lax.ppermute(value, "dp", pairs)


def gather_plane(own):
    half = own.shape[0] // 2
    from_c = swap_c(own)
    from_x = swap_x(own)
    from_y = swap_y(own)
    from_xy = jnp.concatenate([swap_y(from_x[:half]), swap_x(from_y[half:])], axis=0)
    from_cx = swap_c(from_x)
    from_cy = swap_c(from_y)
    from_cxy = swap_c(from_xy)
    return jnp.concatenate(
        [own, from_x, from_c, from_cx, from_y, from_xy, from_cy, from_cxy], axis=0
    )


def scatter_plane(partial):
    rows = partial.shape[0] // 8
    half = rows // 2
    width = partial.shape[1]
    blocks = partial.reshape(2, 2, 2, rows, width)
    other = swap_c(blocks[:, 1].astype(low))
    both = blocks[:, 0].astype(f32) + other.astype(f32)
    top, bottom = both[:, :, :half], both[:, :, half:]
    top_x = swap_x(top[:, 1].astype(low))
    bottom_y = swap_y(bottom[1].astype(low))
    top = top[:, 0] + top_x.astype(f32)
    bottom = bottom[0] + bottom_y.astype(f32)
    top_y = swap_y(top[1].astype(low))
    bottom_x = swap_x(bottom[1].astype(low))
    return jnp.concatenate([top[0] + top_y.astype(f32), bottom[0] + bottom_x.astype(f32)], axis=0)


def to_columns(parts, place):
    rows, _, width = parts.shape
    result = jnp.zeros((PLANE, rows, width), parts.dtype)
    for flip in range(PLANE):
        piece = lax.dynamic_index_in_dim(parts, place ^ flip, 1, keepdims=False)
        if flip:
            piece = swap_dp(piece, flip)
        result = lax.dynamic_update_index_in_dim(result, piece, place ^ flip, 0)
    return result.reshape(PLANE * rows, width)


def to_rows(block, place):
    width = block.shape[1]
    parts = block.reshape(PLANE, block.shape[0] // PLANE, width)
    result = jnp.zeros((parts.shape[1], PLANE, width), parts.dtype)
    for flip in range(PLANE):
        piece = lax.dynamic_index_in_dim(parts, place ^ flip, 0, keepdims=False)
        if flip:
            piece = swap_dp(piece, flip)
        result = lax.dynamic_update_index_in_dim(result, piece, place ^ flip, 1)
    return result


def gather_line(own, depth, level, count):
    up, down = own, own
    ups, downs = [], []
    for step in range(1, count):
        up = line_shift(up, range(step - 1, count - 1), 1)
        down = line_shift(down, range(1, count + 1 - step), -1)
        ups.append(up)
        downs.append(down)
    result = jnp.zeros((count,) + own.shape, own.dtype)
    result = lax.dynamic_update_index_in_dim(result, own, level, 0)
    for step in range(1, count):
        piece = jnp.where(level >= step, ups[step - 1], downs[count - step - 1])
        result = lax.dynamic_update_index_in_dim(
            result, piece, lax.rem(level - step + count, count), 0
        )
    mark = (ups[max(count - 3, 0)], downs[max(count - 3, 0)]) if count > 1 else (own,)
    return result.reshape((count * own.shape[0],) + own.shape[1:]), mark


def scatter_line(blocks, level, count, wait):
    if count == 1:
        return blocks[0].astype(f32), ()
    got_up = got_down = None
    ups = []
    for step in range(1, count):
        send_up = lax.dynamic_index_in_dim(
            blocks, lax.rem(level - step + count, count), 0, keepdims=False
        )
        send_down = lax.dynamic_index_in_dim(
            blocks, lax.rem(level + step, count), 0, keepdims=False
        )
        if got_up is None:
            send_up, send_down = send_up.astype(low), send_down.astype(low)
            if wait:
                send_up = after(send_up, *wait)
                send_down = after(send_down, *wait)
        else:
            send_up = (send_up.astype(f32) + got_up.astype(f32)).astype(low)
            send_down = (send_down.astype(f32) + got_down.astype(f32)).astype(low)
        got_up = line_shift(send_up, range(0, min(step, count - 1)), 1)
        got_down = line_shift(send_down, range(max(count - step, 1), count), -1)
        ups.append((got_up, got_down))
    own = lax.dynamic_index_in_dim(blocks, level, 0, keepdims=False)
    total = own.astype(f32) + got_up.astype(f32) + got_down.astype(f32)
    return total, ups[max(count - 3, 0)]


def normalize(rows):
    scale = lax.rsqrt(jnp.mean(rows * rows, axis=-1, keepdims=True) + epsilon)
    return rows * scale, scale


def norm_back(grad_normed, unit_rows, scale, gain):
    inner = grad_normed * gain
    mean_term = jnp.mean(inner * unit_rows, axis=-1, keepdims=True)
    return scale * (inner - unit_rows * mean_term), jnp.sum(grad_normed * unit_rows, axis=0)


def rotate(values, cosine, sine):
    half = values.shape[-1] // 2
    first, second = values[..., :half], values[..., half:]
    return jnp.concatenate(
        [first * cosine - second * sine, second * cosine + first * sine], axis=-1
    )


def unrotate(values, cosine, sine):
    half = values.shape[-1] // 2
    first, second = values[..., :half], values[..., half:]
    return jnp.concatenate(
        [first * cosine + second * sine, second * cosine - first * sine], axis=-1
    )


def gather_gains(gains, place, level, count):
    plane = jnp.zeros((PLANE,) + gains.shape, gains.dtype)
    for flip in range(PLANE):
        piece = swap_dp(gains, flip) if flip else gains
        plane = lax.dynamic_update_index_in_dim(plane, piece, place ^ flip, 0)
    whole = jnp.zeros((count,) + plane.shape, gains.dtype)
    whole = lax.dynamic_update_index_in_dim(whole, plane, level, 0)
    total = count * PLANE
    for step in range(1, count):
        pairs = [(i, (i + step * PLANE) % total) for i in range(total)]
        piece = lax.ppermute(plane, "dp", pairs)
        whole = lax.dynamic_update_index_in_dim(
            whole, piece, lax.rem(level - step + count, count), 0
        )
    return jnp.moveaxis(whole, 2, 0).reshape(gains.shape[0], -1)


def scatter_gain(part, place, level, count):
    part = part + swap_x(part)
    blocks = part.reshape(count, PLANE, -1)
    mine = lax.dynamic_index_in_dim(blocks, place, 1, keepdims=False)
    for flip in range(1, PLANE):
        mine = mine + swap_dp(
            lax.dynamic_index_in_dim(blocks, place ^ flip, 1, keepdims=False), flip
        )
    result = lax.dynamic_index_in_dim(mine, level, 0, keepdims=False)
    total = count * PLANE
    for step in range(1, count):
        pairs = [(i, (i + step * PLANE) % total) for i in range(total)]
        result = result + lax.ppermute(
            lax.dynamic_index_in_dim(mine, lax.rem(level + step, count), 0, keepdims=False),
            "dp",
            pairs,
        )
    return result


def local(
    tokens,
    segments,
    gain_attn,
    gain_ffn,
    w_query,
    w_key,
    w_value,
    w_out,
    w_gate,
    w_up,
    w_down,
    cotangent,
):
    seq_len = segments.shape[1]
    shard = w_query.shape[0]
    model = tokens.shape[1]
    count = lax.axis_size("dp") // PLANE
    me = lax.axis_index("dp")
    side = lax.axis_index("tensor")
    level, place = me // PLANE, lax.rem(me, PLANE)
    scale_dot = 1.0 / math.sqrt(HEAD_DIM)
    shift = -math.log(SEQ_LEN)
    width = w_query.shape[1] // PLANE
    heads = width // HEAD_DIM
    units = w_gate.shape[1] // PLANE
    chunk = units // CHUNKS

    attn_parts = jnp.concatenate(
        [w.reshape(shard, PLANE, width) for w in (w_query, w_key, w_value, w_out)], axis=2
    )
    attn_block = to_columns(attn_parts, place)
    attn_weights, mark = gather_line(attn_block, shard, level, count)
    w_qkv, w_o = attn_weights[:, : 3 * width], attn_weights[:, 3 * width :]
    chunk_weights = []
    wide = [w.reshape(shard, PLANE, units) for w in (w_gate, w_up, w_down)]
    for k in range(CHUNKS):
        parts = jnp.concatenate([w[:, :, k * chunk : (k + 1) * chunk] for w in wide], axis=2)
        block = after(to_columns(parts, place), *mark)
        gathered, mark = gather_line(block, shard, level, count)
        chunk_weights.append(gathered)

    gains = gather_gains(jnp.stack([gain_attn, gain_ffn]), place, level, count).astype(f32)
    gain_first, gain_second = gains[0], gains[1]
    inputs = tokens.astype(f32)
    unit_one, scale_one = normalize(inputs)
    rows_one = gather_plane((unit_one * gain_first).astype(low))
    grad_rows = gather_plane(after(cotangent, rows_one))
    seg = jnp.concatenate([segments] + [swap_dp(segments, flip) for flip in range(1, PLANE)], axis=0)
    places = lax.rem(jnp.arange(seq_len, dtype=jnp.int32) + side * (seq_len // 2), seq_len)
    seg = jnp.where(side == 0, seg, jnp.roll(seg, seq_len // 2, axis=1))
    same = seg[:, :, None] == seg[:, None, :]
    live = same & (places[None, None, :] <= places[None, :, None])
    positions = jnp.sum(live.astype(jnp.int32), axis=2) - 1
    freqs = theta ** (-(jnp.arange(HEAD_DIM // 2, dtype=f32) * 2.0 / HEAD_DIM))
    angles = positions.astype(f32)[..., None] * freqs
    cosine, sine = jnp.cos(angles)[:, :, None, :], jnp.sin(angles)[:, :, None, :]

    qkv = dot(rows_one, w_qkv).reshape(PLANE, seq_len, 3, heads, HEAD_DIM)
    queries = rotate(qkv[:, :, 0], cosine, sine).astype(low)
    keys = rotate(qkv[:, :, 1], cosine, sine).astype(low)
    values = qkv[:, :, 2].astype(low)

    def weights():
        dots = (
            jnp.einsum("nqhd,nkhd->nhqk", queries, keys, preferred_element_type=f32) * scale_dot
        )
        return jnp.where(live[:, None], jax.nn.sigmoid(dots + shift), 0.0)

    probs = weights()
    probs_low = probs.astype(low)
    mixed = jnp.einsum("nhqk,nkhd->nqhd", probs_low, values, preferred_element_type=f32)
    mixed = mixed.reshape(PLANE * seq_len, width).astype(low)
    middle = inputs + scatter_plane(dot_rt(mixed, w_o))
    unit_two, scale_two = normalize(middle)
    rows_two = gather_plane((unit_two * gain_second).astype(low))

    hiddens, grad_acts, ffn_grads = [], [], []
    wait = ()
    for k in range(CHUNKS):
        part = chunk_weights[k]
        wg, wu, wd = part[:, :chunk], part[:, chunk : 2 * chunk], part[:, 2 * chunk :]
        gate = dot(rows_two, wg)
        upward = dot(rows_two, wu)
        grad_hidden = dot(grad_rows, wd)
        gate_sig = jax.nn.sigmoid(gate)
        silu = gate * gate_sig
        hidden = (silu * upward).astype(low)
        grad_gate = (grad_hidden * upward * gate_sig * (1.0 + gate * (1.0 - gate_sig))).astype(low)
        grad_up = (grad_hidden * silu).astype(low)
        hiddens.append(hidden)
        grad_acts.append((grad_gate, grad_up))
        grads = jnp.concatenate(
            [
                dot_lt(rows_two, grad_gate).astype(low),
                dot_lt(rows_two, grad_up).astype(low),
                dot_lt(grad_rows, hidden).astype(low),
            ],
            axis=1,
        ).reshape(count, PLANE * shard, 3 * chunk)
        total, wait = scatter_line(grads, level, count, wait)
        ffn_grads.append(to_rows(total.astype(low), place))
    grad_normed_two = None
    for (grad_gate, grad_up), part in zip(grad_acts, chunk_weights):
        term = dot_rt(jnp.concatenate([grad_gate, grad_up], axis=1), part[:, : 2 * chunk])
        grad_normed_two = term if grad_normed_two is None else grad_normed_two + term
    grad_normed_two = scatter_plane(grad_normed_two)
    grad_unit_two, gain_two_part = norm_back(grad_normed_two, unit_two, scale_two, gain_second)
    grad_middle = cotangent.astype(f32) + grad_unit_two
    grad_branch = gather_plane(grad_middle.astype(low))
    down_all = jnp.concatenate([part[:, 2 * chunk :] for part in chunk_weights], axis=1)
    output = (middle + scatter_plane(dot_rt(jnp.concatenate(hiddens, axis=1), down_all))).astype(low)

    grad_mixed = dot(grad_branch, w_o).astype(low).reshape(PLANE, seq_len, heads, HEAD_DIM)
    grad_out = dot_lt(grad_branch, mixed).astype(low).reshape(count, PLANE * shard, width)
    grad_out, wait = scatter_line(grad_out, level, count, wait)
    grad_probs = jnp.einsum("nqhd,nkhd->nhqk", grad_mixed, values, preferred_element_type=f32)
    grad_dots = (grad_probs * probs * (1.0 - probs)).astype(low)
    grad_q = jnp.einsum("nhqk,nkhd->nqhd", grad_dots, keys, preferred_element_type=f32) * scale_dot
    grad_k = jnp.einsum("nhqk,nqhd->nkhd", grad_dots, queries, preferred_element_type=f32) * scale_dot
    grad_v = jnp.einsum("nhqk,nqhd->nkhd", probs_low, grad_mixed, preferred_element_type=f32)
    grad_qkv = jnp.concatenate(
        [
            unrotate(grad_q, cosine, sine).astype(low).reshape(PLANE * seq_len, width),
            unrotate(grad_k, cosine, sine).astype(low).reshape(PLANE * seq_len, width),
            grad_v.astype(low).reshape(PLANE * seq_len, width),
        ],
        axis=1,
    )
    grad_proj = dot_lt(rows_one, grad_qkv).astype(low).reshape(count, PLANE * shard, 3 * width)
    grad_proj, wait = scatter_line(grad_proj, level, count, wait)
    grad_normed_one = scatter_plane(dot_rt(grad_qkv, w_qkv))
    grad_unit_one, gain_one_part = norm_back(grad_normed_one, unit_one, scale_one, gain_first)
    grad_tokens = grad_middle + grad_unit_one

    out_rows = to_rows(grad_out.astype(low), place).astype(f32).reshape(shard, PLANE * width)
    proj_rows = to_rows(grad_proj.astype(low), place).astype(f32)
    proj = [
        proj_rows[:, :, k * width : (k + 1) * width].reshape(shard, PLANE * width) for k in range(3)
    ]
    ffn = [
        jnp.concatenate(
            [g[:, :, k * chunk : (k + 1) * chunk] for g in ffn_grads], axis=2
        )
        .astype(f32)
        .reshape(shard, PLANE * units)
        for k in range(3)
    ]
    return (
        output,
        grad_tokens,
        scatter_gain(gain_one_part, place, level, count),
        scatter_gain(gain_two_part, place, level, count),
        proj[0],
        proj[1],
        proj[2],
        out_rows,
        ffn[0],
        ffn[1],
        ffn[2],
    )


def solution(mesh):
    rows, grid = P(("dp", "tensor"), None), P("dp", "tensor")
    return jax.shard_map(
        local,
        mesh=mesh,
        in_specs=(rows, P("dp", None), P("dp"), P("dp")) + (grid,) * 7 + (rows,),
        out_specs=(rows, rows, P("dp"), P("dp")) + (grid,) * 7,
        check_vma=False,
    )
```

time: 2520 us -> 1360 us (0.54)
  waiting for transfers between devices: 2100 us -> 385 us
  starting transfers between devices: 1.1 us -> 357 us
  local copies, waits for them, and re-layouts: 22.6 us -> 254 us
  blocking collectives: 109 us -> 0 us
  other arithmetic: 28.7 us -> 113 us
    reduce_scatter x11 -> x0, waiting for transfers between devices: 1440 us -> none  [the longest x1 337 us: local(): lax.psum_scatter(grad_gate, 'dp', scatter_dimension=0, tiled=True)]
    all_gather x11 -> x0, waiting for transfers between devices: 654 us -> none  [the longest x1 129 us: local(): lax.all_gather(w_down, 'dp', axis=0, tiled=True)]
    ppermute x0 -> x174, waiting for transfers between devices: none -> 385 us  [the longest x66 191 us: line_shift(): return lax.ppermute(value, 'dp', pairs)]
    ppermute x0 -> x174, starting transfers between devices: none -> 357 us  [the longest x66 264 us: line_shift(): return lax.ppermute(value, 'dp', pairs)]
    dynamic_update_slice x0 -> x56, local copies, waits for them, and re-layouts: none -> 68.2 us  [the longest x24 53 us: to_rows(): result = lax.dynamic_update_index_in_dim(result, piece, place ^ flip, 1)]
    unnamed x1 -> x0, blocking collectives: 61.6 us -> none
    all_gather x2 -> x0, blocking collectives: 41.9 us -> none  [the longest x1 23.2 us: local(): lax.all_gather(gain_attn, 'dp', axis=0, tiled=True)]
    unnamed x104 -> x328, local copies, waits for them, and re-layouts: 17.8 us -> 58.1 us
  transfers between devices with their start and end apart: 22 -> 174, of which waited for: 20 -> 56; matrix products, arithmetic and copies ran while one was open for 7% -> 37% of each run, Pallas kernels for 0% -> 0%
where the time goes in v1:
time: 1360 us; the launch traced here: 1350 us
  waiting for transfers between devices  385 us (28%)
  starting transfers between devices  357 us (26%)
  local copies, waits for them, and re-layouts  254 us (19%)
  matrix products  240 us (18%)
  other arithmetic  113 us (8%)
    ppermute x66, starting transfers between devices, line_shift(): return lax.ppermute(value, 'dp', pairs)  264 us
    ppermute x66, waiting for transfers between devices, line_shift(): return lax.ppermute(value, 'dp', pairs)  191 us
    ppermute x81, waiting for transfers between devices, swap_dp(): return lax.ppermute(value, 'dp', [(i, i ^ flip) for i in range(count)])  129 us
    dot_general x14, matrix products, dot(): return jnp.dot(left, right, preferred_element_type=f32)  84.1 us
    dot_general x7, matrix products, dot_rt(): lax.dot_general(left, right, (((1,), (1,)), ((), ())), preferred_element_...  78 us
    dot_general x14, matrix products, dot_lt(): lax.dot_general(left, right, (((0,), (0,)), ((), ())), preferred_element_...  62.1 us
    unnamed x328, local copies, waits for them, and re-layouts  58.1 us
    dynamic_update_slice x24, local copies, waits for them, and re-layouts, to_rows(): result = lax.dynamic_update_index_in_dim(result, piece, place ^ flip, 1)  53 us
  transfers between devices with their start and end apart: 174, of which 56 were waited for; matrix products, arithmetic and copies ran while one was open for 37% of the time, Pallas kernels for 0%

profile of v1, /device:TPU:0, one launch (start us, length us, event | category | flops | bytes accessed | tf_op | source)
XLA Modules:
  0.0 1353.4 jit_solution(15226164533445061309)
XLA Ops:
  73.6 11.4 collective-permute-done.49
  104.0 27.1 %collective-permute-done.67 = bf16[128,768]{1,0:T(8,128)(2,1)S(1)} collective-permute-done((bf16[128,768]{1,0:T(8,128)(2,1)S(1)}, bf16[128,768]{1,0:T(8,128)(2,1)S(1)}, u32[]{:S(2)}, u32[]{:S(2)}) %collective-permute-start.67) | collective-permute-done | bytes 196640 | tf_op jit(solution)/shard_map/ppermute | solution.py:41
  142.3 15.2 %collective-permute-done.18 = bf16[512,1024]{1,0:T(8,128)(2,1)S(1)} collective-permute-done((bf16[512,1024]{1,0:T(8,128)(2,1)S(1)}, bf16[512,1024]{1,0:T(8,128)(2,1)S(1)}, u32[]{:S(2)}, u32[]{:S(2)}) %collective-permute-start.18) | collective-permute-done | bytes 1048608 | tf_op jit(solution)/shard_map/ppermute | solution.py:56
  162.5 20.3 %collective-permute-done.19 = bf16[512,1024]{1,0:T(8,128)(2,1)S(1)} collective-permute-done((bf16[512,1024]{1,0:T(8,128)(2,1)S(1)}, bf16[512,1024]{1,0:T(8,128)(2,1)S(1)}, u32[]{:S(2)}, u32[]{:S(2)}) %collective-permute-start.19) | collective-permute-done | bytes 1048608 | tf_op jit(solution)/shard_map/ppermute | solution.py:56
  185.6 9.1 collective-permute-start.42
  200.3 10.5 collective-permute-done.20
  211.7 12.5 collective-permute-done.43
  289.2 11.1 collective-permute-start.45
  309.2 9.7 collective-permute-done.45
  328.9 10.9 collective-permute-done.52
  351.1 12.7 collective-permute-done.53
  365.1 18.6 %collective-permute-start.60 = (bf16[512,768]{1,0:T(8,128)(2,1)}, bf16[512,768]{1,0:T(8,128)(2,1)S(1)}, u32[]{:S(2)}, u32[]{:S(2)}) collective-permute-start(bf16[512,768]{1,0:T(8,128)(2,1)} %bitcast.82), channel_id=1, source_target_pairs={{0,8},{2,10},{4,12},{6,14},{8,16},{10,18},{12,20},{14,22},{16,24},... | collective-permute-start | bytes 2359304 | tf_op jit(solution)/shard_map/ppermute | solution.py:56
  403.2 14.0 %collective-permute-done.54 = bf16[512,768]{1,0:T(8,128)(2,1)S(1)} collective-permute-done((bf16[512,768]{1,0:T(8,128)(2,1)S(1)}, bf16[512,768]{1,0:T(8,128)(2,1)S(1)}, u32[]{:S(2)}, u32[]{:S(2)}) %collective-permute-start.54) | collective-permute-done | bytes 786464 | tf_op jit(solution)/shard_map/ppermute | solution.py:56
  450.8 16.1 %collective-permute-done.63 = bf16[512,768]{1,0:T(8,128)(2,1)S(1)} collective-permute-done((bf16[512,768]{1,0:T(8,128)(2,1)S(1)}, bf16[512,768]{1,0:T(8,128)(2,1)S(1)}, u32[]{:S(2)}, u32[]{:S(2)}) %collective-permute-start.63) | collective-permute-done | bytes 786464 | tf_op jit(solution)/shard_map/ppermute | solution.py:56
  472.7 20.2 %collective-permute-done.29 = bf16[2,128,2048]{2,1,0:T(8,128)(2,1)S(1)} collective-permute-done((bf16[2,128,2048]{2,1,0:T(8,128)(2,1)S(1)}, bf16[2,128,2048]{2,1,0:T(8,128)(2,1)S(1)}, u32[]{:S(2)}, u32[]{:S(2)}) %collective-permute-start.29) | collective-permute-done | bytes 1048608 | tf_op jit(solution)/shard_map/ppermute | solution.py:41
  631.3 15.5 %fusion.8 = f32[2048,2048]{1,0:T(8,128)} fusion(bf16[2048,256]{0,1:T(8,128)(2,1)} %get-tuple-element.82, bf16[2048,256]{0,1:T(8,128)(2,1)} %get-tuple-element.91, bf16[2048,256]{0,1:T(8,128)(2,1)} %get-tuple-element.85, bf16[2048,256]{0,1:T(8,128)(2,1)} %get-tuple-element.88, bf16[2048,256]{1,0:T(8,128)(2,1)} %slice.535, bf16[2048,256]{1,0:T(8,128)(2,1)} %slice.534, ...), kind=kOutput, calls=%fused_computation.22 | convolution fusion | flops 8623489024 | bytes 25165824 | tf_op jit(solution)/shard_map/dot_general | solution.py:24
  661.2 23.6 %add_add_fusion = f32[2048,2048]{1,0:T(8,128)} fusion(f32[2048,2048]{1,0:T(8,128)} %fusion.43, f32[2048,2048]{1,0:T(8,128)} %fusion.47, f32[2048,2048]{1,0:T(8,128)} %fusion.45, bf16[2048,768]{1,0:T(8,128)(2,1)S(1)} %bitcast.613, bf16[2048,256]{0,1:T(8,128)(2,1)S(1)} %copy-done.57, bf16[2048,256]{0,1:T(8,128)(2,1)S(1)} %copy-done.59), kind=kOutput, calls=%fused_computation | convolution fusion | flops 4311744512 | bytes 71303168 | tf_op jit(solution)/shard_map/dot_general | solution.py:24
  736.5 20.9 %collective-permute-start.124 = (bf16[512,768]{1,0:T(8,128)(2,1)S(1)}, bf16[512,768]{1,0:T(8,128)(2,1)S(1)}, u32[]{:S(2)}, u32[]{:S(2)}) collective-permute-start(bf16[512,768]{1,0:T(8,128)(2,1)S(1)} %dynamic-slice_bitcast_fusion.5), channel_id=1, source_target_pairs={{0,8},{2,10},{4,12},{6,14},{1,9},{3,11},{5,13},{7,15}} | collective-permute-start | bytes 2359304 | tf_op jit(solution)/shard_map/ppermute | solution.py:56
  762.8 9.7 collective-permute-done.124
  800.4 11.1 collective-permute-done.76
  820.3 13.7 %collective-permute-done.89 = bf16[2,128,2048]{2,1,0:T(8,128)(2,1)S(1)} collective-permute-done((bf16[2,128,2048]{2,1,0:T(8,128)(2,1)S(1)}, bf16[2,128,2048]{2,1,0:T(8,128)(2,1)S(1)}, u32[]{:S(2)}, u32[]{:S(2)}) %collective-permute-start.89) | collective-permute-done | bytes 1048608 | tf_op jit(solution)/shard_map/ppermute | solution.py:36
  870.3 11.4 collective-permute-done.113
  956.3 14.1 %collective-permute-done.129 = bf16[512,768]{1,0:T(8,128)(2,1)S(1)} collective-permute-done((bf16[512,768]{1,0:T(8,128)(2,1)S(1)}, bf16[512,768]{1,0:T(8,128)(2,1)S(1)}, u32[]{:S(2)}, u32[]{:S(2)}) %collective-permute-start.129) | collective-permute-done | bytes 786464 | tf_op jit(solution)/shard_map/ppermute | solution.py:56
  1019.0 21.6 %collective-permute-start.132 = (bf16[512,768]{1,0:T(8,128)(2,1)S(1)}, bf16[512,768]{1,0:T(8,128)(2,1)S(1)}, u32[]{:S(2)}, u32[]{:S(2)}) collective-permute-start(bf16[512,768]{1,0:T(8,128)(2,1)S(1)} %copy-done.85), channel_id=1, source_target_pairs={{0,8},{2,10},{4,12},{6,14},{1,9},{3,11},{5,13},{7,15}} | collective-permute-start | bytes 2359304 | tf_op jit(solution)/shard_map/ppermute | solution.py:56
  1040.6 10.1 fusion.27
  1060.3 9.4 convolution_convert_fusion
  1098.1 23.4 %collective-permute-start.136 = (bf16[512,256]{1,0:T(8,128)(2,1)}, bf16[512,256]{1,0:T(8,128)(2,1)S(1)}, u32[]{:S(2)}, u32[]{:S(2)}) collective-permute-start(bf16[512,256]{1,0:T(8,128)(2,1)} %dynamic-slice_bitcast_fusion.11), channel_id=1, source_target_pairs={{0,8},{2,10},{4,12},{6,14},{1,9},{3,11},{5,13},{7,15}} | collective-permute-start | bytes 786440 | tf_op jit(solution)/shard_map/ppermute | solution.py:56
  1154.1 10.2 collective-permute-done.167
  1167.7 10.7 collective-permute-start.149
  1215.7 10.4 collective-permute-done.140
  1266.3 29.5 %collective-permute-start.142 = (bf16[512,768]{1,0:T(8,128)(2,1)S(1)}, bf16[512,768]{1,0:T(8,128)(2,1)S(1)}, u32[]{:S(2)}, u32[]{:S(2)}) collective-permute-start(bf16[512,768]{1,0:T(8,128)(2,1)S(1)} %get-tuple-element.55), channel_id=1, source_target_pairs={{0,8},{2,10},{4,12},{6,14},{8,16},{10,18},{12,20},{14,22},{16,24},... | collective-permute-start | bytes 2359304 | tf_op jit(solution)/shard_map/ppermute | solution.py:56
  1303.9 13.9 %collective-permute-done.117 = f32[128]{0:T(128)S(1)} collective-permute-done((f32[128]{0:T(128)S(1)}, f32[128]{0:T(128)S(1)}, u32[]{:S(2)}, u32[]{:S(2)}) %collective-permute-start.117) | collective-permute-done | bytes 544 | tf_op jit(solution)/shard_map/ppermute | solution.py:216
  (995 shorter events, 869.9 us)
Async XLA Ops:
  1.5 44.7 %collective-permute-start = (bf16[2,128]{1,0:T(2,128)(2,1)S(1)}, bf16[2,128]{1,0:T(2,128)(2,1)S(1)}, u32[]{:S(2)}, u32[]{:S(2)}) collective-permute-start(bf16[2,128]{1,0:T(2,128)(2,1)S(1)} %get-tuple-element.67), channel_id=1, source_target_pairs={{0,2},{2,0},{4,6},{6,4},{8,10},{10,8},{12,14},{14,12},{16,18},{18,... | collective-permute-start | bytes 1544 | tf_op jit(solution)/shard_map/ppermute | solution.py:41
  2.0 44.3 %collective-permute-start.1 = (bf16[2,128]{1,0:T(2,128)(2,1)S(1)}, bf16[2,128]{1,0:T(2,128)(2,1)S(1)}, u32[]{:S(2)}, u32[]{:S(2)}) collective-permute-start(bf16[2,128]{1,0:T(2,128)(2,1)S(1)} %get-tuple-element.67), channel_id=1, source_target_pairs={{0,4},{2,6},{4,0},{6,2},{8,12},{10,14},{12,8},{14,10},{16,20},{18,... | collective-permute-start | bytes 1544 | tf_op jit(solution)/shard_map/ppermute | solution.py:41
  4.5 41.9 %collective-permute-start.2 = (bf16[2,128]{1,0:T(2,128)(2,1)S(1)}, bf16[2,128]{1,0:T(2,128)(2,1)S(1)}, u32[]{:S(2)}, u32[]{:S(2)}) collective-permute-start(bf16[2,128]{1,0:T(2,128)(2,1)S(1)} %get-tuple-element.67), channel_id=1, source_target_pairs={{0,6},{2,4},{4,2},{6,0},{8,14},{10,12},{12,10},{14,8},{16,22},{18,... | collective-permute-start | bytes 1544 | tf_op jit(solution)/shard_map/ppermute | solution.py:41
  4.6 43.8 %collective-permute-start.23 = (s32[1,512]{1,0:T(1,128)}, s32[1,512]{1,0:T(1,128)S(1)}, u32[]{:S(2)}, u32[]{:S(2)}) collective-permute-start(s32[1,512]{1,0:T(1,128)} %param.13), channel_id=1, source_target_pairs={{0,2},{2,0},{4,6},{6,4},{8,10},{10,8},{12,14},{14,12},{16,18},{18,... | collective-permute-start | bytes 6152 | tf_op jit(solution)/shard_map/ppermute | solution.py:41
  4.8 43.7 %collective-permute-start.24 = (s32[1,512]{1,0:T(1,128)}, s32[1,512]{1,0:T(1,128)S(1)}, u32[]{:S(2)}, u32[]{:S(2)}) collective-permute-start(s32[1,512]{1,0:T(1,128)} %param.13), channel_id=1, source_target_pairs={{0,4},{2,6},{4,0},{6,2},{8,12},{10,14},{12,8},{14,10},{16,20},{18,... | collective-permute-start | bytes 6152 | tf_op jit(solution)/shard_map/ppermute | solution.py:41
  48.5 52.4 %collective-permute-start.14 = (bf16[128,1024]{1,0:T(8,128)(2,1)}, bf16[128,1024]{1,0:T(8,128)(2,1)S(1)}, u32[]{:S(2)}, u32[]{:S(2)}) collective-permute-start(bf16[128,1024]{1,0:T(8,128)(2,1)} %bitcast.689), channel_id=1, source_target_pairs={{0,2},{2,0},{4,6},{6,4},{8,10},{10,8},{12,14},{14,12},{16,18},{18,... | collective-permute-start | bytes 786440 | tf_op jit(solution)/shard_map/ppermute | solution.py:41
  98.7 40.1 %collective-permute-start.6 = (bf16[256,2048]{1,0:T(8,128)(2,1)S(1)}, bf16[256,2048]{1,0:T(8,128)(2,1)S(1)}, u32[]{:S(2)}, u32[]{:S(2)}) collective-permute-start(bf16[256,2048]{1,0:T(8,128)(2,1)S(1)} %get-tuple-element.65), channel_id=1, source_target_pairs={{0,1},{1,0},{2,3},{3,2},{4,5},{5,4},{6,7},{7,6},{8,9},{9,8},{10,11... | collective-permute-start | bytes 3145736 | tf_op jit(solution)/shard_map/ppermute | solution.py:36
  195.8 89.8 %collective-permute-start.80 = (bf16[256,2048]{1,0:T(8,128)(2,1)}, bf16[256,2048]{1,0:T(8,128)(2,1)}, u32[]{:S(2)}, u32[]{:S(2)}) collective-permute-start(bf16[256,2048]{1,0:T(8,128)(2,1)} %param.23), channel_id=1, source_target_pairs={{0,1},{1,0},{2,3},{3,2},{4,5},{5,4},{6,7},{7,6},{8,9},{9,8},{10,11... | collective-permute-start | bytes 3145736 | tf_op jit(solution)/shard_map/ppermute | solution.py:36
  210.8 91.8 %collective-permute-start.81 = (bf16[256,2048]{1,0:T(8,128)(2,1)}, bf16[256,2048]{1,0:T(8,128)(2,1)}, u32[]{:S(2)}, u32[]{:S(2)}) collective-permute-start(bf16[256,2048]{1,0:T(8,128)(2,1)} %param.23), channel_id=1, source_target_pairs={{0,2},{2,0},{4,6},{6,4},{8,10},{10,8},{12,14},{14,12},{16,18},{18,... | collective-permute-start | bytes 3145736 | tf_op jit(solution)/shard_map/ppermute | solution.py:41
  224.2 63.2 %collective-permute-start.83 = (bf16[256,2048]{1,0:T(8,128)(2,1)}, bf16[256,2048]{1,0:T(8,128)(2,1)}, u32[]{:S(2)}, u32[]{:S(2)}) collective-permute-start(bf16[256,2048]{1,0:T(8,128)(2,1)} %param.23), channel_id=1, source_target_pairs={{0,4},{2,6},{4,0},{6,2},{8,12},{10,14},{12,8},{14,10},{16,20},{18,... | collective-permute-start | bytes 3145736 | tf_op jit(solution)/shard_map/ppermute | solution.py:41
  225.5 63.7 %collective-permute-start.44 = (bf16[512,768]{1,0:T(8,128)(2,1)}, bf16[512,768]{1,0:T(8,128)(2,1)}, u32[]{:S(2)}, u32[]{:S(2)}) collective-permute-start(bf16[512,768]{1,0:T(8,128)(2,1)} %collective-permute-done.43), channel_id=1, source_target_pairs={{8,0},{10,2},{12,4},{14,6},{16,8},{18,10},{20,12},{22,14},{9,1},{1... | collective-permute-start | bytes 2359304 | tf_op jit(solution)/shard_map/ppermute | solution.py:56
  226.8 78.2 %collective-permute-start.46 = (bf16[512,768]{1,0:T(8,128)(2,1)}, bf16[512,768]{1,0:T(8,128)(2,1)}, u32[]{:S(2)}, u32[]{:S(2)}) collective-permute-start(bf16[512,768]{1,0:T(8,128)(2,1)} %collective-permute-done.42), channel_id=1, source_target_pairs={{8,16},{10,18},{12,20},{14,22},{16,24},{18,26},{20,28},{22,30},{9,... | collective-permute-start | bytes 2359304 | tf_op jit(solution)/shard_map/ppermute | solution.py:56
  302.6 140.4 %collective-permute-start.26 = (bf16[2,2,256,2048]{3,2,1,0:T(8,128)(2,1)}, bf16[2,2,256,2048]{3,2,1,0:T(8,128)(2,1)}, u32[]{:S(2)}, u32[]{:S(2)}) collective-permute-start(bf16[2,2,256,2048]{3,2,1,0:T(8,128)(2,1)} %fusion.4), channel_id=1, source_target_pairs={{0,2},{2,0},{4,6},{6,4},{8,10},{10,8},{12,14},{14,12},{16,18},{18,... | collective-permute-start | bytes 12582920 | tf_op jit(solution)/shard_map/ppermute | solution.py:41
  438.4 56.5 %collective-permute-start.65 = (bf16[512,768]{1,0:T(8,128)(2,1)}, bf16[512,768]{1,0:T(8,128)(2,1)}, u32[]{:S(2)}, u32[]{:S(2)}) collective-permute-start(bf16[512,768]{1,0:T(8,128)(2,1)} %collective-permute-done.64), channel_id=1, source_target_pairs={{16,24},{18,26},{20,28},{22,30},{17,25},{19,27},{21,29},{23,31}} | collective-permute-start | bytes 2359304 | tf_op jit(solution)/shard_map/ppermute | solution.py:56
  606.7 84.2 %collective-permute-start.120 = (bf16[512,768]{1,0:T(8,128)(2,1)}, bf16[512,768]{1,0:T(8,128)(2,1)}, u32[]{:S(2)}, u32[]{:S(2)}) collective-permute-start(bf16[512,768]{1,0:T(8,128)(2,1)} %dynamic-slice_bitcast_fusion.4), channel_id=1, source_target_pairs={{0,8},{2,10},{4,12},{6,14},{1,9},{3,11},{5,13},{7,15}} | collective-permute-start | bytes 2359304 | tf_op jit(solution)/shard_map/ppermute | solution.py:56
  652.9 126.3 %collective-permute-start.75 = (bf16[2,2,256,2048]{3,2,0,1:T(8,128)(2,1)}, bf16[2,2,256,2048]{3,2,0,1:T(8,128)(2,1)}, u32[]{:S(2)}, u32[]{:S(2)}) collective-permute-start(bf16[2,2,256,2048]{3,2,0,1:T(8,128)(2,1)} %fusion.5), channel_id=1, source_target_pairs={{0,2},{2,0},{4,6},{6,4},{8,10},{10,8},{12,14},{14,12},{16,18},{18,... | collective-permute-start | bytes 12582920 | tf_op jit(solution)/shard_map/ppermute | solution.py:41
  721.2 67.7 %collective-permute-start.88 = (bf16[2,2,256,2048]{3,2,0,1:T(8,128)(2,1)}, bf16[2,2,256,2048]{3,2,0,1:T(8,128)(2,1)}, u32[]{:S(2)}, u32[]{:S(2)}) collective-permute-start(bf16[2,2,256,2048]{3,2,0,1:T(8,128)(2,1)} %fusion.6), channel_id=1, source_target_pairs={{0,2},{2,0},{4,6},{6,4},{8,10},{10,8},{12,14},{14,12},{16,18},{18,... | collective-permute-start | bytes 12582920 | tf_op jit(solution)/shard_map/ppermute | solution.py:41
  799.7 40.2 %collective-permute-start.126 = (bf16[512,768]{1,0:T(8,128)(2,1)S(1)}, bf16[512,768]{1,0:T(8,128)(2,1)S(1)}, u32[]{:S(2)}, u32[]{:S(2)}) collective-permute-start(bf16[512,768]{1,0:T(8,128)(2,1)S(1)} %get-tuple-element.32), channel_id=1, source_target_pairs={{24,16},{26,18},{28,20},{30,22},{25,17},{27,19},{29,21},{31,23}} | collective-permute-start | bytes 2359304 | tf_op jit(solution)/shard_map/ppermute | solution.py:56
  865.8 44.4 %collective-permute-start.154 = (bf16[512,768]{1,0:T(8,128)(2,1)}, bf16[512,768]{1,0:T(8,128)(2,1)}, u32[]{:S(2)}, u32[]{:S(2)}) collective-permute-start(bf16[512,768]{1,0:T(8,128)(2,1)} %get-tuple-element.45), channel_id=1, source_target_pairs={{0,8},{2,10},{4,12},{6,14},{8,16},{10,18},{12,20},{14,22},{16,24},... | collective-permute-start | bytes 2359304 | tf_op jit(solution)/shard_map/ppermute | solution.py:56
  910.2 45.5 %collective-permute-start.97 = (bf16[128,2048]{1,0:T(8,128)(2,1)S(1)}, bf16[128,2048]{1,0:T(8,128)(2,1)S(1)}, u32[]{:S(2)}, u32[]{:S(2)}) collective-permute-start(bf16[128,2048]{1,0:T(8,128)(2,1)S(1)} %slice.562), channel_id=1, source_target_pairs={{0,4},{2,6},{4,0},{6,2},{8,12},{10,14},{12,8},{14,10},{16,20},{18,... | collective-permute-start | bytes 1572872 | tf_op jit(solution)/shard_map/ppermute | solution.py:41
  911.4 44.3 %collective-permute-start.98 = (bf16[128,2048]{1,0:T(8,128)(2,1)S(1)}, bf16[128,2048]{1,0:T(8,128)(2,1)S(1)}, u32[]{:S(2)}, u32[]{:S(2)}) collective-permute-start(bf16[128,2048]{1,0:T(8,128)(2,1)S(1)} %slice.563), channel_id=1, source_target_pairs={{0,1},{1,0},{2,3},{3,2},{4,5},{5,4},{6,7},{7,6},{8,9},{9,8},{10,11... | collective-permute-start | bytes 1572872 | tf_op jit(solution)/shard_map/ppermute | solution.py:36
  913.2 42.7 %collective-permute-start.95 = (bf16[256,2048]{1,0:T(8,128)(2,1)S(1)}, bf16[256,2048]{1,0:T(8,128)(2,1)S(1)}, u32[]{:S(2)}, u32[]{:S(2)}) collective-permute-start(bf16[256,2048]{1,0:T(8,128)(2,1)S(1)} %copy-done.54), channel_id=1, source_target_pairs={{0,2},{2,0},{4,6},{6,4},{8,10},{10,8},{12,14},{14,12},{16,18},{18,... | collective-permute-start | bytes 3145736 | tf_op jit(solution)/shard_map/ppermute | solution.py:41
  915.6 40.6 %collective-permute-start.99 = (bf16[256,2048]{1,0:T(8,128)(2,1)S(1)}, bf16[256,2048]{1,0:T(8,128)(2,1)S(1)}, u32[]{:S(2)}, u32[]{:S(2)}) collective-permute-start(bf16[256,2048]{1,0:T(8,128)(2,1)S(1)} %copy-done.52), channel_id=1, source_target_pairs={{0,2},{2,0},{4,6},{6,4},{8,10},{10,8},{12,14},{14,12},{16,18},{18,... | collective-permute-start | bytes 3145736 | tf_op jit(solution)/shard_map/ppermute | solution.py:41
  971.9 44.4 %collective-permute-start.130 = (bf16[512,768]{1,0:T(8,128)(2,1)}, bf16[512,768]{1,0:T(8,128)(2,1)}, u32[]{:S(2)}, u32[]{:S(2)}) collective-permute-start(bf16[512,768]{1,0:T(8,128)(2,1)} %get-tuple-element.34), channel_id=1, source_target_pairs={{24,16},{26,18},{28,20},{30,22},{25,17},{27,19},{29,21},{31,23}} | collective-permute-start | bytes 2359304 | tf_op jit(solution)/shard_map/ppermute | solution.py:56
  973.4 163.6 %collective-permute-start.164 = (bf16[512,768]{1,0:T(8,128)(2,1)}, bf16[512,768]{1,0:T(8,128)(2,1)}, u32[]{:S(2)}, u32[]{:S(2)}) collective-permute-start(bf16[512,768]{1,0:T(8,128)(2,1)} %get-tuple-element.49), channel_id=1, source_target_pairs={{0,8},{2,10},{4,12},{6,14},{8,16},{10,18},{12,20},{14,22},{16,24},... | collective-permute-start | bytes 2359304 | tf_op jit(solution)/shard_map/ppermute | solution.py:56
  1081.9 56.7 %collective-permute-start.165 = (bf16[512,768]{1,0:T(8,128)(2,1)}, bf16[512,768]{1,0:T(8,128)(2,1)S(1)}, u32[]{:S(2)}, u32[]{:S(2)}) collective-permute-start(bf16[512,768]{1,0:T(8,128)(2,1)} %add_convert_fusion.6), channel_id=1, source_target_pairs={{8,0},{10,2},{12,4},{14,6},{16,8},{18,10},{20,12},{22,14},{24,16},... | collective-permute-start | bytes 2359304 | tf_op jit(solution)/shard_map/ppermute | solution.py:56
  1083.2 56.8 %collective-permute-start.169 = (bf16[512,768]{1,0:T(8,128)(2,1)}, bf16[512,768]{1,0:T(8,128)(2,1)S(1)}, u32[]{:S(2)}, u32[]{:S(2)}) collective-permute-start(bf16[512,768]{1,0:T(8,128)(2,1)} %get-tuple-element.51), channel_id=1, source_target_pairs={{0,8},{2,10},{4,12},{6,14},{8,16},{10,18},{12,20},{14,22},{16,24},... | collective-permute-start | bytes 2359304 | tf_op jit(solution)/shard_map/ppermute | solution.py:56
  1134.7 74.1 %collective-permute-start.102 = (bf16[2,128,2048]{2,1,0:T(8,128)(2,1)}, bf16[2,128,2048]{2,1,0:T(8,128)(2,1)}, u32[]{:S(2)}, u32[]{:S(2)}) collective-permute-start(bf16[2,128,2048]{2,1,0:T(8,128)(2,1)} %slice_bitcast_fusion.12), channel_id=1, source_target_pairs={{0,1},{1,0},{2,3},{3,2},{4,5},{5,4},{6,7},{7,6},{8,9},{9,8},{10,11... | collective-permute-start | bytes 3145736 | tf_op jit(solution)/shard_map/ppermute | solution.py:36
  1137.0 71.8 %collective-permute-start.104 = (bf16[2,128,2048]{2,1,0:T(8,128)(2,1)}, bf16[2,128,2048]{2,1,0:T(8,128)(2,1)}, u32[]{:S(2)}, u32[]{:S(2)}) collective-permute-start(bf16[2,128,2048]{2,1,0:T(8,128)(2,1)} %slice_bitcast_fusion.10), channel_id=1, source_target_pairs={{0,4},{2,6},{4,0},{6,2},{8,12},{10,14},{12,8},{14,10},{16,20},{18,... | collective-permute-start | bytes 3145736 | tf_op jit(solution)/shard_map/ppermute | solution.py:41
  1167.7 65.0 %collective-permute-start.149 = (bf16[512,256]{1,0:T(8,128)(2,1)}, bf16[512,256]{1,0:T(8,128)(2,1)}, u32[]{:S(2)}, u32[]{:S(2)}) collective-permute-start(bf16[512,256]{1,0:T(8,128)(2,1)} %get-tuple-element.53), channel_id=1, source_target_pairs={{0,8},{2,10},{4,12},{6,14},{8,16},{10,18},{12,20},{14,22},{16,24},... | collective-permute-start | bytes 786440 | tf_op jit(solution)/shard_map/ppermute | solution.py:56
  1212.2 42.0 %collective-permute-start.103 = (bf16[128,2048]{1,0:T(8,128)(2,1)}, bf16[128,2048]{1,0:T(8,128)(2,1)}, u32[]{:S(2)}, u32[]{:S(2)}) collective-permute-start(bf16[128,2048]{1,0:T(8,128)(2,1)} %fusion.147), channel_id=1, source_target_pairs={{0,4},{2,6},{4,0},{6,2},{8,12},{10,14},{12,8},{14,10},{16,20},{18,... | collective-permute-start | bytes 1572872 | tf_op jit(solution)/shard_map/ppermute | solution.py:41
  1266.3 55.9 %collective-permute-start.142 = (bf16[512,768]{1,0:T(8,128)(2,1)S(1)}, bf16[512,768]{1,0:T(8,128)(2,1)S(1)}, u32[]{:S(2)}, u32[]{:S(2)}) collective-permute-start(bf16[512,768]{1,0:T(8,128)(2,1)S(1)} %get-tuple-element.55), channel_id=1, source_target_pairs={{0,8},{2,10},{4,12},{6,14},{8,16},{10,18},{12,20},{14,22},{16,24},... | collective-permute-start | bytes 2359304 | tf_op jit(solution)/shard_map/ppermute | solution.py:56
  (282 other events, 5261.1 us)

commit v2 on v1

v2 whole, which is shorter than its diff:
```python
import math

import jax
import jax.numpy as jnp
from jax import lax
from jax.sharding import Mesh
from jax.sharding import PartitionSpec as P

HEAD_DIM = 128
SEQ_LEN = 512
PLANE = 4
CHUNKS = 2

epsilon = 1e-05
theta = 10000.0
low = jnp.bfloat16
f32 = jnp.float32


def dot(left, right):
    return jnp.dot(left, right, preferred_element_type=f32)


def dot_rt(left, right):
    return lax.dot_general(left, right, (((1,), (1,)), ((), ())), preferred_element_type=f32)


def dot_lt(left, right):
    return lax.dot_general(left, right, (((0,), (0,)), ((), ())), preferred_element_type=f32)


def after(value, *earlier):
    return lax.optimization_barrier((value,) + earlier)[0]


def swap(value, axis):
    return lax.ppermute(value, axis, [(0, 1), (1, 0)])


def gather_plane(own):
    half = own.shape[0] // 2
    from_x = swap(own, "tensor")
    from_y = swap(own, "y")
    chip = jnp.concatenate(
        [own, from_x, from_y, swap(from_x[:half], "y"), swap(from_y[half:], "tensor")], axis=0
    )
    return jnp.concatenate([chip, swap(chip, "c")], axis=0)


def scatter_plane(partial):
    rows = partial.shape[0] // 8
    half = rows // 2
    width = partial.shape[1]
    mine, theirs = partial[: 4 * rows], partial[4 * rows :]
    both = mine.astype(f32) + swap(theirs.astype(low), "c").astype(f32)
    both = both.reshape(2, 2, rows, width)
    top, bottom = both[:, :, :half], both[:, :, half:]
    top_x = swap(top[:, 1].astype(low), "tensor")
    bottom_y = swap(bottom[1].astype(low), "y")
    top = top[:, 0] + top_x.astype(f32)
    bottom = bottom[0] + bottom_y.astype(f32)
    top_y = swap(top[1].astype(low), "y")
    bottom_x = swap(bottom[1].astype(low), "tensor")
    return jnp.concatenate([top[0] + top_y.astype(f32), bottom[0] + bottom_x.astype(f32)], axis=0)


def to_columns(parts):
    block = lax.all_to_all(parts, ("y", "c"), 0, 0, tiled=True)
    return block.reshape(-1, parts.shape[2])


def to_rows(block):
    parts = block.reshape(PLANE, block.shape[0] // PLANE, block.shape[1])
    return lax.all_to_all(parts, ("y", "c"), 0, 0, tiled=True)


def gather_line(block):
    return lax.all_gather(block, "z", axis=0, tiled=True)


def scatter_line(grads):
    return lax.psum_scatter(grads.astype(low), "z", scatter_dimension=0, tiled=True)


def quarters(weight, width):
    return jnp.swapaxes(weight.reshape(weight.shape[0], PLANE, width), 0, 1)


def shard_of(parts):
    return jnp.swapaxes(parts, 0, 1).reshape(parts.shape[1], -1).astype(f32)


def normalize(rows):
    scale = lax.rsqrt(jnp.mean(rows * rows, axis=-1, keepdims=True) + epsilon)
    return rows * scale, scale


def norm_back(grad_normed, unit_rows, scale, gain):
    inner = grad_normed * gain
    mean_term = jnp.mean(inner * unit_rows, axis=-1, keepdims=True)
    return scale * (inner - unit_rows * mean_term), jnp.sum(grad_normed * unit_rows, axis=0)


def rotate(values, cosine, sine):
    half = values.shape[-1] // 2
    first, second = values[..., :half], values[..., half:]
    return jnp.concatenate(
        [first * cosine - second * sine, second * cosine + first * sine], axis=-1
    )


def unrotate(values, cosine, sine):
    half = values.shape[-1] // 2
    first, second = values[..., :half], values[..., half:]
    return jnp.concatenate(
        [first * cosine + second * sine, second * cosine - first * sine], axis=-1
    )


def shifted(value, step):
    count = lax.axis_size("z")
    return lax.ppermute(value, "z", [(i, (i + step) % count) for i in range(count)])


def plane_flip(value, dy, dc):
    if dy and dc:
        return lax.ppermute(value, ("y", "c"), [(i, i ^ 3) for i in range(4)])
    return swap(value, "y" if dy else "c")


def gather_gains(gains, place, level):
    plane = jnp.zeros((PLANE,) + gains.shape, gains.dtype)
    for flip in range(PLANE):
        piece = plane_flip(gains, flip // 2, flip % 2) if flip else gains
        plane = lax.dynamic_update_index_in_dim(plane, piece, place ^ flip, 0)
    count = lax.axis_size("z")
    whole = jnp.zeros((count,) + plane.shape, gains.dtype)
    whole = lax.dynamic_update_index_in_dim(whole, plane, level, 0)
    for step in range(1, count):
        piece = shifted(plane, step)
        whole = lax.dynamic_update_index_in_dim(
            whole, piece, lax.rem(level - step + count, count), 0
        )
    return jnp.moveaxis(whole, 2, 0).reshape(gains.shape[0], -1)


def scatter_gain(part, place, level):
    count = lax.axis_size("z")
    part = part + swap(part, "tensor")
    blocks = part.reshape(count, PLANE, -1)
    mine = lax.dynamic_index_in_dim(blocks, place, 1, keepdims=False)
    for flip in range(1, PLANE):
        piece = lax.dynamic_index_in_dim(blocks, place ^ flip, 1, keepdims=False)
        mine = mine + plane_flip(piece, flip // 2, flip % 2)
    result = lax.dynamic_index_in_dim(mine, level, 0, keepdims=False)
    for step in range(1, count):
        piece = lax.dynamic_index_in_dim(mine, lax.rem(level + step, count), 0, keepdims=False)
        result = result + shifted(piece, step)
    return result


def local(
    tokens,
    segments,
    gain_attn,
    gain_ffn,
    w_query,
    w_key,
    w_value,
    w_out,
    w_gate,
    w_up,
    w_down,
    cotangent,
):
    seq_len = segments.shape[1]
    side = lax.axis_index("tensor")
    level, place = lax.axis_index("z"), lax.axis_index("y") * 2 + lax.axis_index("c")
    scale_dot = 1.0 / math.sqrt(HEAD_DIM)
    shift = -math.log(SEQ_LEN)
    width = w_query.shape[1] // PLANE
    heads = width // HEAD_DIM
    units = w_gate.shape[1] // PLANE
    chunk = units // CHUNKS

    attn_block = to_columns(
        jnp.concatenate([quarters(w, width) for w in (w_query, w_key, w_value, w_out)], axis=2)
    )
    attn_weights = gather_line(attn_block)
    w_qkv, w_o = attn_weights[:, : 3 * width], attn_weights[:, 3 * width :]
    chunk_weights = []
    wide = [quarters(w, units) for w in (w_gate, w_up, w_down)]
    earlier = attn_block
    for k in range(CHUNKS):
        parts = jnp.concatenate([w[:, :, k * chunk : (k + 1) * chunk] for w in wide], axis=2)
        earlier = to_columns(after(parts, earlier))
        chunk_weights.append(gather_line(earlier))

    gains = gather_gains(jnp.stack([gain_attn, gain_ffn]), place, level).astype(f32)
    gain_first, gain_second = gains[0], gains[1]
    inputs = tokens.astype(f32)
    unit_one, scale_one = normalize(inputs)
    rows_one = gather_plane((unit_one * gain_first).astype(low))
    grad_rows = gather_plane(after(cotangent, rows_one))
    seg = jnp.concatenate([segments] + [plane_flip(segments, dy, dc) for dc, dy in ((0, 1), (1, 0), (1, 1))], axis=0)
    places = lax.rem(jnp.arange(seq_len, dtype=jnp.int32) + side * (seq_len // 2), seq_len)
    seg = jnp.where(side == 0, seg, jnp.roll(seg, seq_len // 2, axis=1))
    same = seg[:, :, None] == seg[:, None, :]
    live = same & (places[None, None, :] <= places[None, :, None])
    positions = jnp.sum(live.astype(jnp.int32), axis=2) - 1
    freqs = theta ** (-(jnp.arange(HEAD_DIM // 2, dtype=f32) * 2.0 / HEAD_DIM))
    angles = positions.astype(f32)[..., None] * freqs
    cosine, sine = jnp.cos(angles)[:, :, None, :], jnp.sin(angles)[:, :, None, :]

    qkv = dot(rows_one, w_qkv).reshape(PLANE, seq_len, 3, heads, HEAD_DIM)
    queries = rotate(qkv[:, :, 0], cosine, sine).astype(low)
    keys = rotate(qkv[:, :, 1], cosine, sine).astype(low)
    values = qkv[:, :, 2].astype(low)

    def weights():
        dots = (
            jnp.einsum("nqhd,nkhd->nhqk", queries, keys, preferred_element_type=f32) * scale_dot
        )
        return jnp.where(live[:, None], jax.nn.sigmoid(dots + shift), 0.0)

    probs = weights()
    probs_low = probs.astype(low)
    mixed = jnp.einsum("nhqk,nkhd->nqhd", probs_low, values, preferred_element_type=f32)
    mixed = mixed.reshape(PLANE * seq_len, width).astype(low)
    middle = inputs + scatter_plane(dot_rt(mixed, w_o))
    unit_two, scale_two = normalize(middle)
    rows_two = gather_plane((unit_two * gain_second).astype(low))

    hiddens, grad_acts, grad_in, grad_downs = [], [], [], []
    for k in range(CHUNKS):
        part = chunk_weights[k]
        wg, wu, wd = part[:, :chunk], part[:, chunk : 2 * chunk], part[:, 2 * chunk :]
        gate = dot(rows_two, wg)
        upward = dot(rows_two, wu)
        grad_hidden = dot(grad_rows, wd)
        gate_sig = jax.nn.sigmoid(gate)
        silu = gate * gate_sig
        hidden = (silu * upward).astype(low)
        grad_gate = (grad_hidden * upward * gate_sig * (1.0 + gate * (1.0 - gate_sig))).astype(low)
        grad_up = (grad_hidden * silu).astype(low)
        hiddens.append(hidden)
        both = jnp.concatenate([grad_gate, grad_up], axis=1)
        grad_acts.append(both)
        grad_in.append(to_rows(scatter_line(dot_lt(rows_two, both))))
        grad_downs.append(to_rows(scatter_line(dot_lt(grad_rows, hidden))))
    grad_normed_two = None
    for both, part in zip(grad_acts, chunk_weights):
        term = dot_rt(both, part[:, : 2 * chunk])
        grad_normed_two = term if grad_normed_two is None else grad_normed_two + term
    grad_normed_two = scatter_plane(grad_normed_two)
    grad_unit_two, gain_two_part = norm_back(grad_normed_two, unit_two, scale_two, gain_second)
    grad_middle = cotangent.astype(f32) + grad_unit_two
    grad_branch = gather_plane(grad_middle.astype(low))
    down_all = jnp.concatenate([part[:, 2 * chunk :] for part in chunk_weights], axis=1)
    output = (middle + scatter_plane(dot_rt(jnp.concatenate(hiddens, axis=1), down_all))).astype(low)

    grad_mixed = dot(grad_branch, w_o).astype(low).reshape(PLANE, seq_len, heads, HEAD_DIM)
    grad_out = to_rows(scatter_line(dot_lt(grad_branch, mixed)))
    grad_probs = jnp.einsum("nqhd,nkhd->nhqk", grad_mixed, values, preferred_element_type=f32)
    grad_dots = (grad_probs * probs * (1.0 - probs)).astype(low)
    grad_q = jnp.einsum("nhqk,nkhd->nqhd", grad_dots, keys, preferred_element_type=f32) * scale_dot
    grad_k = jnp.einsum("nhqk,nqhd->nkhd", grad_dots, queries, preferred_element_type=f32) * scale_dot
    grad_v = jnp.einsum("nhqk,nqhd->nkhd", probs_low, grad_mixed, preferred_element_type=f32)
    grad_qkv = jnp.concatenate(
        [
            unrotate(grad_q, cosine, sine).astype(low).reshape(PLANE * seq_len, width),
            unrotate(grad_k, cosine, sine).astype(low).reshape(PLANE * seq_len, width),
            grad_v.astype(low).reshape(PLANE * seq_len, width),
        ],
        axis=1,
    )
    grad_proj = to_rows(scatter_line(dot_lt(rows_one, grad_qkv)))
    grad_normed_one = scatter_plane(dot_rt(grad_qkv, w_qkv))
    grad_unit_one, gain_one_part = norm_back(grad_normed_one, unit_one, scale_one, gain_first)
    grad_tokens = grad_middle + grad_unit_one

    proj = [shard_of(grad_proj[:, :, k * width : (k + 1) * width]) for k in range(3)]
    ffn = [
        shard_of(jnp.concatenate([g[:, :, k * chunk : (k + 1) * chunk] for g in grad_in], axis=2))
        for k in range(2)
    ]
    ffn.append(shard_of(jnp.concatenate(grad_downs, axis=2)))
    return (
        output,
        grad_tokens,
        scatter_gain(gain_one_part, place, level),
        scatter_gain(gain_two_part, place, level),
        proj[0],
        proj[1],
        proj[2],
        shard_of(grad_out),
        ffn[0],
        ffn[1],
        ffn[2],
    )


def solution(mesh):
    lines = mesh.shape["dp"] // PLANE
    finer = Mesh(
        mesh.devices.reshape(lines, 2, 2, mesh.shape["tensor"]), ("z", "y", "c", "tensor")
    )
    dp = ("z", "y", "c")
    rows, grid = P(dp + ("tensor",), None), P(dp, "tensor")
    return jax.shard_map(
        local,
        mesh=finer,
        in_specs=(rows, P(dp, None), P(dp), P(dp)) + (grid,) * 7 + (rows,),
        out_specs=(rows, rows, P(dp), P(dp)) + (grid,) * 7,
        check_vma=False,
    )
```

time: 1360 us -> 843 us (0.62)
  starting transfers between devices: 357 us -> 90.6 us
  waiting for transfers between devices: 385 us -> 265 us
  local copies, waits for them, and re-layouts: 254 us -> 158 us
  other arithmetic: 113 us -> 68.8 us
  matrix products: 240 us -> 216 us
  blocking collectives: 0 us -> 22.7 us
    ppermute x174 -> x63, starting transfers between devices: 357 us -> 61.6 us  [the longest x50 43.7 us: swap(): return lax.ppermute(value, axis, [(0, 1), (1, 0)])]
    ppermute x174 -> x63, waiting for transfers between devices: 385 us -> 225 us  [the longest x50 222 us: swap(): return lax.ppermute(value, axis, [(0, 1), (1, 0)])]
    dynamic_update_slice x49 -> x0, local copies, waits for them, and re-layouts: 68.1 us -> none  [the longest x24 53 us: to_rows(): result = lax.dynamic_update_index_in_dim(result, piece, place ^ flip, 1)]
    convert_element_type x30 -> x1, other arithmetic: 32.2 us -> 0.01 us  [local(): gather_gains(jnp.stack([gain_attn, gain_ffn]), place, level).astype(f32)]
    all_to_all x0 -> x8, starting transfers between devices: none -> 28.2 us  [the longest x6 21.1 us: to_rows(): return lax.all_to_all(parts, ('y', 'c'), 0, 0, tiled=True)]
    dynamic_slice x26 -> x1, local copies, waits for them, and re-layouts: 23.3 us -> 0.02 us  [scatter_gain(): piece = lax.dynamic_index_in_dim(blocks, place ^ flip, 1, keepdims=False)]
    all_to_all x0 -> x1, blocking collectives: none -> 22.7 us  [to_columns(): block = lax.all_to_all(parts, ('y', 'c'), 0, 0, tiled=True)]
    dot_general x7 -> x5, matrix products: 78 us -> 55.3 us  [dot_rt(): lax.dot_general(left, right, (((1,), (1,)), ((), ())), preferred_element_...]
  transfers between devices with their start and end apart: 174 -> 80, of which waited for: 56 -> 35; matrix products, arithmetic and copies ran while one was open for 37% -> 44% of each run, Pallas kernels for 0% -> 0%
where the time goes in v2:
time: 843 us; the launch traced here: 836 us
  waiting for transfers between devices  265 us (31%)
  matrix products  216 us (26%)
  local copies, waits for them, and re-layouts  158 us (19%)
  starting transfers between devices  90.6 us (11%)
  other arithmetic  68.8 us (8%)
  blocking collectives  22.7 us (3%)
  between operations  15.7 us (2%)
    ppermute x50, waiting for transfers between devices, swap(): return lax.ppermute(value, axis, [(0, 1), (1, 0)])  222 us
    dot_general x8, matrix products, dot(): return jnp.dot(left, right, preferred_element_type=f32)  80.9 us
    unnamed x152, local copies, waits for them, and re-layouts  72.1 us
    dot_general x6, matrix products, dot_lt(): lax.dot_general(left, right, (((0,), (0,)), ((), ())), preferred_element_...  61.7 us
    dot_general x5, matrix products, dot_rt(): lax.dot_general(left, right, (((1,), (1,)), ((), ())), preferred_element_...  55.3 us
    ppermute x50, starting transfers between devices, swap(): return lax.ppermute(value, axis, [(0, 1), (1, 0)])  43.7 us
    add x4, other arithmetic, scatter_plane(): both = mine.astype(f32) + swap(theirs.astype(low), 'c').astype(f32)  24.3 us
    all_to_all x1, blocking collectives, to_columns(): block = lax.all_to_all(parts, ('y', 'c'), 0, 0, tiled=True)  22.7 us
  transfers between devices with their start and end apart: 80, of which 35 were waited for; matrix products, arithmetic and copies ran while one was open for 44% of the time, Pallas kernels for 0%

profile of v2, /device:TPU:0, one launch (start us, length us, event | category | flops | bytes accessed | tf_op | source)
XLA Modules:
  0.0 836.4 jit_solution(15202267916656362627)
XLA Ops:
  36.6 17.7 %collective-permute-done.6 = bf16[256,2048]{1,0:T(8,128)(2,1)} collective-permute-done((bf16[256,2048]{1,0:T(8,128)(2,1)S(1)}, bf16[256,2048]{1,0:T(8,128)(2,1)}, u32[]{:S(2)}, u32[]{:S(2)}) %collective-permute-start.6) | collective-permute-done | bytes 1048608 | tf_op jit(solution)/shard_map/ppermute | solution.py:37
  100.3 11.5 %all-to-all-done.1 = bf16[4,128,1536]{1,2,0:T(8,128)(2,1)S(1)} async-done(((bf16[4,128,1536]{1,2,0:T(8,128)(2,1)}), bf16[4,128,1536]{1,2,0:T(8,128)(2,1)S(1)}, u32[]{:S(2)}, u32[]{:S(2)}) %all-to-all-start.1) | async-done | bytes 1572896 | tf_op jit(solution)/shard_map/all_to_all | solution.py:68
  118.3 11.7 %fusion.18 = f32[2048,768]{1,0:T(8,128)} fusion(bf16[2048,2048]{1,0:T(8,128)(2,1)} %constant_dynamic-update-slice_fusion.5, bf16[2048,1024]{1,0:T(8,128)(2,1)} %all-gather.4.cloned.1.call-done), kind=kOutput, calls=%fused_computation.49 | convolution fusion | flops 6442450944 | bytes 17825792 | tf_op jit(solution)/shard_map/dot_general | solution.py:21
  130.0 8.4 %reshape.331 = f32[4,512,3,2,128]{4,3,2,1,0:T(2,128)} reshape(f32[2048,768]{1,0:T(8,128)} %fusion.18) | data formatting | bytes 12582912 | tf_op jit(solution)/shard_map/reshape | solution.py:215
  176.0 22.7 %all_to_all.45 = bf16[4,128,1536]{1,2,0:T(8,128)(2,1)S(1)} all-to-all(bf16[4,128,1536]{1,2,0:T(8,128)(2,1)S(1)} %pad_maximum_fusion.9), channel_id=1, replica_groups=mesh['z'=4,'y'=2,'c'=2,'tensor'=2] {'y','c'}, dimensions={0} | all-to-all | bytes 3145728 | tf_op jit(solution)/shard_map/all_to_all | solution.py:68
  212.6 14.1 %collective-permute-done.29 = bf16[256,2048]{1,0:T(8,128)(2,1)S(1)} collective-permute-done((bf16[256,2048]{1,0:T(8,128)(2,1)}, bf16[256,2048]{1,0:T(8,128)(2,1)S(1)}, u32[]{:S(2)}, u32[]{:S(2)}) %collective-permute-start.29) | collective-permute-done | bytes 1048608 | tf_op jit(solution)/shard_map/ppermute | solution.py:37
  231.3 29.5 %collective-permute-done.31 = bf16[128,2048]{1,0:T(8,128)(2,1)S(1)} collective-permute-done((bf16[128,2048]{1,0:T(8,128)(2,1)S(1)}, bf16[128,2048]{1,0:T(8,128)(2,1)S(1)}, u32[]{:S(2)}, u32[]{:S(2)}) %collective-permute-start.31) | collective-permute-done | bytes 524320 | tf_op jit(solution)/shard_map/ppermute | solution.py:37
  264.4 10.7 %collective-permute-done.16 = bf16[128,2048]{1,0:T(8,128)(2,1)S(1)} collective-permute-done((bf16[128,2048]{1,0:T(8,128)(2,1)S(1)}, bf16[128,2048]{1,0:T(8,128)(2,1)S(1)}, u32[]{:S(2)}, u32[]{:S(2)}) %collective-permute-start.16) | collective-permute-done | bytes 524320 | tf_op jit(solution)/shard_map/ppermute | solution.py:37
  280.7 20.0 %collective-permute-done.19 = bf16[256,2048]{1,0:T(8,128)(2,1)S(1)} collective-permute-done((bf16[256,2048]{1,0:T(8,128)(2,1)S(1)}, bf16[256,2048]{1,0:T(8,128)(2,1)S(1)}, u32[]{:S(2)}, u32[]{:S(2)}) %collective-permute-start.19) | collective-permute-done | bytes 1048608 | tf_op jit(solution)/shard_map/ppermute | solution.py:37
  319.4 9.8 %fusion.112 = f32[2048,512]{0,1:T(8,128)} fusion(bf16[2048,2048]{1,0:T(8,128)(2,1)} %constant_dynamic-update-slice_fusion.27, bf16[2048,1536]{1,0:T(8,128)(2,1)S(1)} %bitcast.311), kind=kOutput, calls=%fused_computation.291 | convolution fusion | flops 4294967296 | bytes 14680064 | tf_op jit(solution)/shard_map/dot_general | solution.py:21
  329.2 20.5 %all-gather.8.cloned.1.call-done = bf16[2048,1536]{1,0:T(8,128)(2,1)} async-done(((bf16[512,1536]{1,0:T(8,128)(2,1)}), bf16[2048,1536]{1,0:T(8,128)(2,1)}) %all-gather.8.cloned.1.call-update) | async-done | bytes 6291472 | tf_op jit(solution)/shard_map/all_gather | solution.py:78
  352.9 10.7 %fusion.110 = f32[2048,512]{0,1:T(8,128)} fusion(bf16[2048,2048]{1,0:T(8,128)(2,1)} %constant_dynamic-update-slice_fusion.27, bf16[2048,1536]{1,0:T(8,128)(2,1)} %all-gather.8.cloned.1.call-done), kind=kOutput, calls=%fused_computation.289 | convolution fusion | flops 4294967296 | bytes 14680064 | tf_op jit(solution)/shard_map/dot_general | solution.py:21
  368.5 9.7 %fusion.33 = f32[2048,512]{0,1:T(8,128)} fusion(bf16[2048,2048]{1,0:T(8,128)(2,1)} %constant_dynamic-update-slice_fusion.16, bf16[2048,1536]{1,0:T(8,128)(2,1)S(1)} %bitcast.320), kind=kOutput, calls=%fused_computation.72 | convolution fusion | flops 4294967296 | bytes 14680064 | tf_op jit(solution)/shard_map/dot_general | solution.py:21
  378.1 13.6 %multiply_convert_fusion.2 = (bf16[2048,512]{0,1:T(8,128)(2,1)}, bf16[2048,512]{0,1:T(8,128)(2,1)}, bf16[2048,512]{0,1:T(8,128)(2,1)}) fusion(f32[2048,512]{0,1:T(8,128)} %fusion.110, f32[2048,512]{0,1:T(8,128)} %fusion.33, bf16[2048,2048]{1,0:T(8,128)(2,1)} %constant_dynamic-update-slice_fusion.16, bf16[2048,1536]{1,0:T(8,128)(2,1)S(1)} %bitcast.320), kind=kOutput, calls=%fused_computation.24 | convolution fusion | flops 4310695936 | bytes 25165824 | tf_op jit(solution)/shard_map/dot_general | solution.py:21
  391.8 7.4 convolution_convert_fusion.3
  399.3 8.0 fusion.37
  407.3 11.2 %multiply_convert_fusion.4 = (bf16[2048,512]{0,1:T(8,128)(2,1)}, bf16[2048,512]{0,1:T(8,128)(2,1)}, bf16[2048,512]{0,1:T(8,128)(2,1)}) fusion(f32[2048,512]{0,1:T(8,128)S(1)} %copy-done.49, f32[2048,512]{0,1:T(8,128)S(1)} %fusion.37, bf16[2048,2048]{1,0:T(8,128)(2,1)} %constant_dynamic-update-slice_fusion.16, ...), kind=kOutput, calls=%fused_computation.26 | convolution fusion | flops 4310695936 | bytes 25165824 | tf_op jit(solution)/shard_map/dot_general | solution.py:21
  418.5 11.4 %fusion.3 = f32[2048,2048]{1,0:T(8,128)S(1)} fusion(bf16[2048,512]{0,1:T(8,128)(2,1)} %get-tuple-element.38, bf16[2048,512]{0,1:T(8,128)(2,1)} %get-tuple-element.41, bf16[2048,512]{1,0:T(8,128)(2,1)} %slice.433, bf16[2048,512]{1,0:T(8,128)(2,1)S(1)} %slice-done.2), kind=kOutput, calls=%fused_computation.14 | convolution fusion | flops 8606711808 | bytes 25165824 | tf_op jit(solution)/shard_map/dot_general | solution.py:25
  438.5 10.0 %convolution_convert_fusion.4 = bf16[2048,512]{1,0:T(8,128)(2,1)} fusion(bf16[2048,2048]{1,0:T(8,128)(2,1)} %constant_dynamic-update-slice_fusion.27, bf16[2048,512]{0,1:T(8,128)(2,1)S(1)} %copy-done.50), kind=kOutput, calls=%fused_computation.46 | convolution fusion | flops 4296015872 | bytes 12582912 | tf_op jit(solution)/shard_map/dot_general | solution.py:29
  448.5 15.4 %fusion.1 = f32[2048,2048]{1,0:T(8,128)} fusion(bf16[2048,1536]{1,0:T(8,128)(2,1)} %all-gather.6.cloned.1.call-done, bf16[2048,512]{0,1:T(8,128)(2,1)} %get-tuple-element.40, bf16[2048,512]{0,1:T(8,128)(2,1)} %get-tuple-element.39), kind=kOutput, calls=%fused_computation.12 | convolution fusion | flops 8598323200 | bytes 25165824 | tf_op jit(solution)/shard_map/dot_general | solution.py:25
  463.9 17.4 %convolution_add_fusion = f32[2048,2048]{1,0:T(8,128)} fusion(f32[2048,2048]{1,0:T(8,128)} %fusion.1, bf16[2048,1536]{1,0:T(8,128)(2,1)} %all-gather.8.cloned.1.call-done, bf16[2048,512]{0,1:T(8,128)(2,1)} %get-tuple-element.37, bf16[2048,512]{0,1:T(8,128)(2,1)S(1)} %copy-done.51), kind=kOutput, calls=%fused_computation.10 | convolution fusion | flops 8602517504 | bytes 41943040 | tf_op jit(solution)/shard_map/dot_general | solution.py:25
  488.1 12.9 %convolution_convert_fusion.1 = bf16[2048,1024]{1,0:T(8,128)(2,1)} fusion(bf16[2048,2048]{1,0:T(8,128)(2,1)} %constant_dynamic-update-slice_fusion.16, bf16[2048,512]{0,1:T(8,128)(2,1)S(1)} %copy-done.55, bf16[2048,512]{0,1:T(8,128)(2,1)S(1)} %copy-done.54), kind=kOutput, calls=%fused_computation.36 | convolution fusion | flops 8600420352 | bytes 16777216 | tf_op jit(solution)/shard_map/dot_general | solution.py:29
  522.1 14.8 %collective-permute-done.25 = bf16[2,128,2048]{2,1,0:T(8,128)(2,1)S(1)} collective-permute-done((bf16[2,128,2048]{2,1,0:T(8,128)(2,1)S(1)}, bf16[2,128,2048]{2,1,0:T(8,128)(2,1)S(1)}, u32[]{:S(2)}, u32[]{:S(2)}) %collective-permute-start.25) | collective-permute-done | bytes 1048608 | tf_op jit(solution)/shard_map/ppermute | solution.py:37
  543.7 15.7 %collective-permute-done.35 = bf16[2,128,2048]{2,1,0:T(8,128)(2,1)S(1)} collective-permute-done((bf16[2,128,2048]{2,1,0:T(8,128)(2,1)S(1)}, bf16[2,128,2048]{2,1,0:T(8,128)(2,1)S(1)}, u32[]{:S(2)}, u32[]{:S(2)}) %collective-permute-start.35) | collective-permute-done | bytes 1048608 | tf_op jit(solution)/shard_map/ppermute | solution.py:37
  564.0 8.3 collective-permute-done.26
  572.6 9.8 %collective-permute-done.36 = bf16[128,2048]{1,0:T(8,128)(2,1)S(1)} collective-permute-done((bf16[128,2048]{1,0:T(8,128)(2,1)S(1)}, bf16[128,2048]{1,0:T(8,128)(2,1)S(1)}, u32[]{:S(2)}, u32[]{:S(2)}) %collective-permute-start.36) | collective-permute-done | bytes 524320 | tf_op jit(solution)/shard_map/ppermute | solution.py:37
  588.7 21.9 %collective-permute-done.39 = bf16[256,2048]{1,0:T(8,128)(2,1)S(1)} collective-permute-done((bf16[256,2048]{1,0:T(8,128)(2,1)S(1)}, bf16[256,2048]{1,0:T(8,128)(2,1)S(1)}, u32[]{:S(2)}, u32[]{:S(2)}) %collective-permute-start.39) | collective-permute-done | bytes 1048608 | tf_op jit(solution)/shard_map/ppermute | solution.py:37
  615.2 7.4 collective-permute-done.41
  628.1 13.1 %convolution_convert_fusion = bf16[2048,1024]{1,0:T(8,128)(2,1)} fusion(bf16[2048,2048]{1,0:T(8,128)(2,1)} %constant_dynamic-update-slice_fusion.16, bf16[2048,512]{0,1:T(8,128)(2,1)S(1)} %copy-done.53, bf16[2048,512]{0,1:T(8,128)(2,1)S(1)} %copy-done.52), kind=kOutput, calls=%fused_computation.35 | convolution fusion | flops 8600420352 | bytes 16777216 | tf_op jit(solution)/shard_map/dot_general | solution.py:29
  707.1 11.4 %convolution_convert_fusion.2 = bf16[2048,768]{1,0:T(8,128)(2,1)} fusion(bf16[2048,2048]{1,0:T(8,128)(2,1)} %constant_dynamic-update-slice_fusion.5, bf16[2048,768]{1,0:T(8,128)(2,1)} %copy-done.35), kind=kOutput, calls=%fused_computation.37 | convolution fusion | flops 6444023808 | bytes 14680064 | tf_op jit(solution)/shard_map/dot_general | solution.py:29
  748.1 20.2 %collective-permute-done.56 = f32[2048]{0:T(1024)S(1)} collective-permute-done((f32[2048]{0:T(1024)S(1)}, f32[2048]{0:T(1024)S(1)}, u32[]{:S(2)}, u32[]{:S(2)}) %collective-permute-start.56) | collective-permute-done | bytes 8224 | tf_op jit(solution)/shard_map/ppermute | solution.py:37
  786.1 10.4 %collective-permute-done.46 = bf16[128,2048]{1,0:T(8,128)(2,1)} collective-permute-done((bf16[128,2048]{1,0:T(8,128)(2,1)}, bf16[128,2048]{1,0:T(8,128)(2,1)}, u32[]{:S(2)}, u32[]{:S(2)}) %collective-permute-start.46) | collective-permute-done | bytes 524320 | tf_op jit(solution)/shard_map/ppermute | solution.py:37
  (456 shorter events, 383.5 us)
Async XLA Ops:
  20.2 98.0 %all-gather.4.cloned.1.call-start = ((), (), s32[]{:S(2)}) async-start(), calls=%async_computation.15 | async-start | bytes 5242880 | tf_op jit(solution)/shard_map/all_gather | solution.py:78
  31.6 26.2 %collective-permute-start.7 = (bf16[256,2048]{1,0:T(8,128)(2,1)S(1)}, bf16[256,2048]{1,0:T(8,128)(2,1)}, u32[]{:S(2)}, u32[]{:S(2)}) collective-permute-start(bf16[256,2048]{1,0:T(8,128)(2,1)S(1)} %get-tuple-element.29), channel_id=1, source_target_pairs={{0,4},{4,0},{1,5},{5,1},{2,6},{6,2},{3,7},{7,3},{8,12},{12,8},{9,1... | collective-permute-start | bytes 3145736 | tf_op jit(solution)/shard_map/ppermute | solution.py:37
  76.1 37.5 %collective-permute-start.10 = (bf16[1024,2048]{1,0:T(8,128)(2,1)}, bf16[1024,2048]{1,0:T(8,128)(2,1)}, u32[]{:S(2)}, u32[]{:S(2)}) collective-permute-start(bf16[1024,2048]{1,0:T(8,128)(2,1)} %get-tuple-element.104), channel_id=1, source_target_pairs={{0,2},{2,0},{1,3},{3,1},{4,6},{6,4},{5,7},{7,5},{8,10},{10,8},{9,1... | collective-permute-start | bytes 12582920 | tf_op jit(solution)/shard_map/ppermute | solution.py:37
  91.7 222.7 %all-gather.6.cloned.1.call-start = ((), (), s32[]{:S(2)}) async-start(), calls=%async_computation.16 | async-start | bytes 7864320 | tf_op jit(solution)/shard_map/all_gather | solution.py:78
  113.3 236.4 %all-gather.8.cloned.1.call-start = ((), (), s32[]{:S(2)}) async-start(), calls=%async_computation.17 | async-start | bytes 7864320 | tf_op jit(solution)/shard_map/all_gather | solution.py:78
  175.9 26.7 %collective-permute-start.14 = (bf16[1024,2048]{1,0:T(8,128)(2,1)}, bf16[1024,2048]{1,0:T(8,128)(2,1)}, u32[]{:S(2)}, u32[]{:S(2)}) collective-permute-start(bf16[1024,2048]{1,0:T(8,128)(2,1)} %slice.615), channel_id=1, source_target_pairs={{0,2},{2,0},{1,3},{3,1},{4,6},{6,4},{5,7},{7,5},{8,10},{10,8},{9,1... | collective-permute-start | bytes 12582920 | tf_op jit(solution)/shard_map/ppermute | solution.py:37
  200.3 491.0 %reduce-scatter.17.cloned.1.call-start = ((), (), s32[]{:S(2)}) async-start(), calls=%async_computation.23 | async-start | bytes 2621440 | tf_op jit(solution)/shard_map/reduce_scatter | solution.py:82
  200.4 26.3 %collective-permute-start.29 = (bf16[256,2048]{1,0:T(8,128)(2,1)}, bf16[256,2048]{1,0:T(8,128)(2,1)S(1)}, u32[]{:S(2)}, u32[]{:S(2)}) collective-permute-start(bf16[256,2048]{1,0:T(8,128)(2,1)} %param.23), channel_id=1, source_target_pairs={{0,1},{1,0},{2,3},{3,2},{4,5},{5,4},{6,7},{7,6},{8,9},{9,8},{10,11... | collective-permute-start | bytes 3145736 | tf_op jit(solution)/shard_map/ppermute | solution.py:37
  202.2 26.3 %collective-permute-start.30 = (bf16[256,2048]{1,0:T(8,128)(2,1)}, bf16[256,2048]{1,0:T(8,128)(2,1)S(1)}, u32[]{:S(2)}, u32[]{:S(2)}) collective-permute-start(bf16[256,2048]{1,0:T(8,128)(2,1)} %param.23), channel_id=1, source_target_pairs={{0,4},{4,0},{1,5},{5,1},{2,6},{6,2},{3,7},{7,3},{8,12},{12,8},{9,1... | collective-permute-start | bytes 3145736 | tf_op jit(solution)/shard_map/ppermute | solution.py:37
  209.3 52.3 %collective-permute-start.15 = (bf16[2,128,2048]{2,1,0:T(8,128)(2,1)S(1)}, bf16[2,128,2048]{2,1,0:T(8,128)(2,1)S(1)}, u32[]{:S(2)}, u32[]{:S(2)}) collective-permute-start(bf16[2,128,2048]{2,1,0:T(8,128)(2,1)S(1)} %slice_bitcast_fusion.23), channel_id=1, source_target_pairs={{0,1},{1,0},{2,3},{3,2},{4,5},{5,4},{6,7},{7,6},{8,9},{9,8},{10,11... | collective-permute-start | bytes 3145736 | tf_op jit(solution)/shard_map/ppermute | solution.py:37
  209.8 51.9 %collective-permute-start.17 = (bf16[2,128,2048]{2,1,0:T(8,128)(2,1)S(1)}, bf16[2,128,2048]{2,1,0:T(8,128)(2,1)S(1)}, u32[]{:S(2)}, u32[]{:S(2)}) collective-permute-start(bf16[2,128,2048]{2,1,0:T(8,128)(2,1)S(1)} %slice_bitcast_fusion.21), channel_id=1, source_target_pairs={{0,4},{4,0},{1,5},{5,1},{2,6},{6,2},{3,7},{7,3},{8,12},{12,8},{9,1... | collective-permute-start | bytes 3145736 | tf_op jit(solution)/shard_map/ppermute | solution.py:37
  226.7 34.0 %collective-permute-start.31 = (bf16[128,2048]{1,0:T(8,128)(2,1)S(1)}, bf16[128,2048]{1,0:T(8,128)(2,1)S(1)}, u32[]{:S(2)}, u32[]{:S(2)}) collective-permute-start(bf16[128,2048]{1,0:T(8,128)(2,1)S(1)} %slice.444), channel_id=1, source_target_pairs={{0,4},{4,0},{1,5},{5,1},{2,6},{6,2},{3,7},{7,3},{8,12},{12,8},{9,1... | collective-permute-start | bytes 1572872 | tf_op jit(solution)/shard_map/ppermute | solution.py:37
  228.5 35.0 %collective-permute-start.32 = (bf16[128,2048]{1,0:T(8,128)(2,1)S(1)}, bf16[128,2048]{1,0:T(8,128)(2,1)S(1)}, u32[]{:S(2)}, u32[]{:S(2)}) collective-permute-start(bf16[128,2048]{1,0:T(8,128)(2,1)S(1)} %slice.445), channel_id=1, source_target_pairs={{0,1},{1,0},{2,3},{3,2},{4,5},{5,4},{6,7},{7,6},{8,9},{9,8},{10,11... | collective-permute-start | bytes 1572872 | tf_op jit(solution)/shard_map/ppermute | solution.py:37
  264.4 50.0 %collective-permute-start.33 = (bf16[1024,2048]{1,0:T(8,128)(2,1)}, bf16[1024,2048]{1,0:T(8,128)(2,1)}, u32[]{:S(2)}, u32[]{:S(2)}) collective-permute-start(bf16[1024,2048]{1,0:T(8,128)(2,1)} %get-tuple-element.96), channel_id=1, source_target_pairs={{0,2},{2,0},{1,3},{3,1},{4,6},{6,4},{5,7},{7,5},{8,10},{10,8},{9,1... | collective-permute-start | bytes 12582920 | tf_op jit(solution)/shard_map/ppermute | solution.py:37
  314.4 49.3 %collective-permute-start.23 = (bf16[1024,2048]{1,0:T(8,128)(2,1)}, bf16[1024,2048]{1,0:T(8,128)(2,1)}, u32[]{:S(2)}, u32[]{:S(2)}) collective-permute-start(bf16[1024,2048]{1,0:T(8,128)(2,1)} %get-tuple-element.100), channel_id=1, source_target_pairs={{0,2},{2,0},{1,3},{3,1},{4,6},{6,4},{5,7},{7,5},{8,10},{10,8},{9,1... | collective-permute-start | bytes 12582920 | tf_op jit(solution)/shard_map/ppermute | solution.py:37
  399.2 302.8 %reduce-scatter.15.cloned.1.call-start = ((), (), s32[]{:S(2)}) async-start(), calls=%async_computation.22 | async-start | bytes 2621440 | tf_op jit(solution)/shard_map/reduce_scatter | solution.py:82
  438.4 62.6 %collective-permute-start.24 = (bf16[1024,2048]{1,0:T(8,128)(2,1)}, bf16[1024,2048]{1,0:T(8,128)(2,1)}, u32[]{:S(2)}, u32[]{:S(2)}) collective-permute-start(bf16[1024,2048]{1,0:T(8,128)(2,1)} %slice.614), channel_id=1, source_target_pairs={{0,2},{2,0},{1,3},{3,1},{4,6},{6,4},{5,7},{7,5},{8,10},{10,8},{9,1... | collective-permute-start | bytes 12582920 | tf_op jit(solution)/shard_map/ppermute | solution.py:37
  448.5 270.1 %reduce-scatter.11.cloned.1.call-start = ((), (), s32[]{:S(2)}) async-start(), calls=%async_computation.20 | async-start | bytes 5242880 | tf_op jit(solution)/shard_map/reduce_scatter | solution.py:82
  487.7 26.3 %collective-permute-start.34 = (bf16[1024,2048]{1,0:T(8,128)(2,1)}, bf16[1024,2048]{1,0:T(8,128)(2,1)}, u32[]{:S(2)}, u32[]{:S(2)}) collective-permute-start(bf16[1024,2048]{1,0:T(8,128)(2,1)} %slice.613), channel_id=1, source_target_pairs={{0,2},{2,0},{1,3},{3,1},{4,6},{6,4},{5,7},{7,5},{8,10},{10,8},{9,1... | collective-permute-start | bytes 12582920 | tf_op jit(solution)/shard_map/ppermute | solution.py:37
  501.0 233.7 %reduce-scatter.13.cloned.1.call-start = ((), (), s32[]{:S(2)}) async-start(), calls=%async_computation.21 | async-start | bytes 5242880 | tf_op jit(solution)/shard_map/reduce_scatter | solution.py:82
  510.8 26.1 %collective-permute-start.25 = (bf16[2,128,2048]{2,1,0:T(8,128)(2,1)S(1)}, bf16[2,128,2048]{2,1,0:T(8,128)(2,1)S(1)}, u32[]{:S(2)}, u32[]{:S(2)}) collective-permute-start(bf16[2,128,2048]{2,1,0:T(8,128)(2,1)S(1)} %slice_bitcast_fusion.19), channel_id=1, source_target_pairs={{0,1},{1,0},{2,3},{3,2},{4,5},{5,4},{6,7},{7,6},{8,9},{9,8},{10,11... | collective-permute-start | bytes 3145736 | tf_op jit(solution)/shard_map/ppermute | solution.py:37
  512.4 26.1 %collective-permute-start.27 = (bf16[2,128,2048]{2,1,0:T(8,128)(2,1)S(1)}, bf16[2,128,2048]{2,1,0:T(8,128)(2,1)S(1)}, u32[]{:S(2)}, u32[]{:S(2)}) collective-permute-start(bf16[2,128,2048]{2,1,0:T(8,128)(2,1)S(1)} %slice_bitcast_fusion.17), channel_id=1, source_target_pairs={{0,4},{4,0},{1,5},{5,1},{2,6},{6,2},{3,7},{7,3},{8,12},{12,8},{9,1... | collective-permute-start | bytes 3145736 | tf_op jit(solution)/shard_map/ppermute | solution.py:37
  520.8 38.6 %collective-permute-start.35 = (bf16[2,128,2048]{2,1,0:T(8,128)(2,1)S(1)}, bf16[2,128,2048]{2,1,0:T(8,128)(2,1)S(1)}, u32[]{:S(2)}, u32[]{:S(2)}) collective-permute-start(bf16[2,128,2048]{2,1,0:T(8,128)(2,1)S(1)} %slice_bitcast_fusion.15), channel_id=1, source_target_pairs={{0,1},{1,0},{2,3},{3,2},{4,5},{5,4},{6,7},{7,6},{8,9},{9,8},{10,11... | collective-permute-start | bytes 3145736 | tf_op jit(solution)/shard_map/ppermute | solution.py:37
  521.5 39.6 %collective-permute-start.37 = (bf16[2,128,2048]{2,1,0:T(8,128)(2,1)S(1)}, bf16[2,128,2048]{2,1,0:T(8,128)(2,1)S(1)}, u32[]{:S(2)}, u32[]{:S(2)}) collective-permute-start(bf16[2,128,2048]{2,1,0:T(8,128)(2,1)S(1)} %slice_bitcast_fusion.13), channel_id=1, source_target_pairs={{0,4},{4,0},{1,5},{5,1},{2,6},{6,2},{3,7},{7,3},{8,12},{12,8},{9,1... | collective-permute-start | bytes 3145736 | tf_op jit(solution)/shard_map/ppermute | solution.py:37
  541.5 30.7 %collective-permute-start.26 = (bf16[128,2048]{1,0:T(8,128)(2,1)S(1)}, bf16[128,2048]{1,0:T(8,128)(2,1)S(1)}, u32[]{:S(2)}, u32[]{:S(2)}) collective-permute-start(bf16[128,2048]{1,0:T(8,128)(2,1)S(1)} %fusion.79), channel_id=1, source_target_pairs={{0,4},{4,0},{1,5},{5,1},{2,6},{6,2},{3,7},{7,3},{8,12},{12,8},{9,1... | collective-permute-start | bytes 1572872 | tf_op jit(solution)/shard_map/ppermute | solution.py:37
  543.1 29.3 %collective-permute-start.28 = (bf16[128,2048]{1,0:T(8,128)(2,1)S(1)}, bf16[128,2048]{1,0:T(8,128)(2,1)S(1)}, u32[]{:S(2)}, u32[]{:S(2)}) collective-permute-start(bf16[128,2048]{1,0:T(8,128)(2,1)S(1)} %fusion.80), channel_id=1, source_target_pairs={{0,1},{1,0},{2,3},{3,2},{4,5},{5,4},{6,7},{7,6},{8,9},{9,8},{10,11... | collective-permute-start | bytes 1572872 | tf_op jit(solution)/shard_map/ppermute | solution.py:37
  690.9 31.2 %collective-permute-start.44 = (bf16[1024,2048]{1,0:T(8,128)(2,1)}, bf16[1024,2048]{1,0:T(8,128)(2,1)}, u32[]{:S(2)}, u32[]{:S(2)}) collective-permute-start(bf16[1024,2048]{1,0:T(8,128)(2,1)} %slice.612), channel_id=1, source_target_pairs={{0,2},{2,0},{1,3},{3,1},{4,6},{6,4},{5,7},{7,5},{8,10},{10,8},{9,1... | collective-permute-start | bytes 12582920 | tf_op jit(solution)/shard_map/ppermute | solution.py:37
  694.8 77.5 %reduce-scatter.9.cloned.1.call-start = ((), (), s32[]{:S(2)}) async-start(), calls=%async_computation.19 | async-start | bytes 1310720 | tf_op jit(solution)/shard_map/reduce_scatter | solution.py:82
  707.0 104.8 %reduce-scatter.7.cloned.1.call-start = ((), (), s32[]{:S(2)}) async-start(), calls=%async_computation.18 | async-start | bytes 3932160 | tf_op jit(solution)/shard_map/reduce_scatter | solution.py:82
  736.5 31.9 %all-to-all-start.6 = ((bf16[4,128,1024]{2,1,0:T(8,128)(2,1)}), bf16[4,128,1024]{2,1,0:T(8,128)(2,1)S(1)}, u32[]{:S(2)}, u32[]{:S(2)}) async-start(bf16[4,128,1024]{2,1,0:T(8,128)(2,1)} %bitcast.313), calls=%async_computation.10 | async-start | bytes 2097152 | tf_op jit(solution)/shard_map/all_to_all | solution.py:74
  742.4 33.5 %collective-permute-start.45 = (bf16[2,128,2048]{2,1,0:T(8,128)(2,1)}, bf16[2,128,2048]{2,1,0:T(8,128)(2,1)}, u32[]{:S(2)}, u32[]{:S(2)}) collective-permute-start(bf16[2,128,2048]{2,1,0:T(8,128)(2,1)} %slice_bitcast_fusion.11), channel_id=1, source_target_pairs={{0,1},{1,0},{2,3},{3,2},{4,5},{5,4},{6,7},{7,6},{8,9},{9,8},{10,11... | collective-permute-start | bytes 3145736 | tf_op jit(solution)/shard_map/ppermute | solution.py:37
  743.2 33.9 %collective-permute-start.47 = (bf16[2,128,2048]{2,1,0:T(8,128)(2,1)}, bf16[2,128,2048]{2,1,0:T(8,128)(2,1)}, u32[]{:S(2)}, u32[]{:S(2)}) collective-permute-start(bf16[2,128,2048]{2,1,0:T(8,128)(2,1)} %slice_bitcast_fusion.9), channel_id=1, source_target_pairs={{0,4},{4,0},{1,5},{5,1},{2,6},{6,2},{3,7},{7,3},{8,12},{12,8},{9,1... | collective-permute-start | bytes 3145736 | tf_op jit(solution)/shard_map/ppermute | solution.py:37
  (111 other events, 1341.2 us)
Sparse Core Ops, SparseCore 0:
  36.6 81.2 all-gather.3
  120.0 113.8 all-gather.5
  236.1 113.5 all-gather.7
  399.4 42.0 reduce-scatter.16
  448.6 42.1 reduce-scatter.14
  501.2 74.9 reduce-scatter.10
  641.3 74.3 reduce-scatter.12
  718.0 27.6 reduce-scatter.8
  748.1 58.8 reduce-scatter.6

commit v3 on v2

v3 whole, which is shorter than its diff:
```python
import functools
import math

import jax
import jax.numpy as jnp
from jax import lax
from jax.experimental import pallas as pl
from jax.experimental.pallas import tpu as pltpu
from jax.sharding import Mesh
from jax.sharding import PartitionSpec as P

HEAD_DIM = 128
SEQ_LEN = 512
PLANE = 4
CHUNKS = 2

epsilon = 1e-05
theta = 10000.0
low = jnp.bfloat16
f32 = jnp.float32
params = pltpu.CompilerParams(vmem_limit_bytes=56 * 2**20)


def dot(left, right):
    return jnp.dot(left, right, preferred_element_type=f32)


def dot_rt(left, right):
    return lax.dot_general(left, right, (((1,), (1,)), ((), ())), preferred_element_type=f32)


def dot_lt(left, right):
    return lax.dot_general(left, right, (((0,), (0,)), ((), ())), preferred_element_type=f32)


def after(value, *earlier):
    return lax.optimization_barrier((value,) + earlier)[0]


def whole(array):
    return pl.BlockSpec(array.shape, lambda i: (0,) * array.ndim)


def cost(flops, *arrays):
    size = sum(math.prod(a.shape) * a.dtype.itemsize for a in arrays)
    return pl.CostEstimate(flops=flops, bytes_accessed=size, transcendentals=0)


def turn(vectors, cosine, sine):
    return vectors * cosine + pltpu.roll(vectors, HEAD_DIM // 2, 1) * sine


def weights_of(query, key, live):
    dots = dot_rt(query, key) * (1.0 / math.sqrt(HEAD_DIM)) - math.log(SEQ_LEN)
    return jax.nn.sigmoid(dots) * live


def attend_kernel(width, rows_ref, w_ref, cos_ref, sin_ref, live_ref, qkv_ref, mixed_ref, part_ref):
    qkv = dot(rows_ref[...], w_ref[:, : 3 * width])
    cosine, sine = cos_ref[...], sin_ref[...]
    live = live_ref[...].astype(f32)
    for first in range(0, width, HEAD_DIM):
        at_q, at_k, at_v = (slice(g + first, g + first + HEAD_DIM) for g in (0, width, 2 * width))
        query = turn(qkv[:, at_q], cosine, sine).astype(low)
        key = turn(qkv[:, at_k], cosine, sine).astype(low)
        value = qkv[:, at_v].astype(low)
        qkv_ref[:, at_q] = query
        qkv_ref[:, at_k] = key
        qkv_ref[:, at_v] = value
        probs = weights_of(query, key, live)
        mixed_ref[:, at_q] = dot(probs.astype(low), value).astype(low)
    part_ref[...] = dot_rt(mixed_ref[...], w_ref[:, 3 * width :]).astype(low)


def attend(rows, weights, cosine, sine, live):
    total, model = rows.shape
    width, seq = weights.shape[1] // 4, live.shape[1]
    tile = lambda columns: pl.BlockSpec((seq, columns), lambda n: (n, 0))
    outs = [jax.ShapeDtypeStruct((total, c), low) for c in (3 * width, width, model)]
    return pl.pallas_call(
        functools.partial(attend_kernel, width),
        grid=(total // seq,),
        in_specs=[tile(model), whole(weights), tile(HEAD_DIM), tile(HEAD_DIM), tile(seq)],
        out_specs=[tile(3 * width), tile(width), tile(model)],
        out_shape=outs,
        compiler_params=params,
        cost_estimate=cost(8 * total * model * width + 4 * total * seq * width, rows, weights, *outs),
    )(rows, weights, cosine, sine, live)


def attend_back_kernel(
    width, grad_ref, w_ref, qkv_ref, cos_ref, sin_ref, live_ref, grads_ref, part_ref
):
    grad_mixed = dot(grad_ref[...], w_ref[:, 3 * width :]).astype(low)
    cosine, sine = cos_ref[...], -sin_ref[...]
    live = live_ref[...].astype(f32)
    scale = 1.0 / math.sqrt(HEAD_DIM)
    for first in range(0, width, HEAD_DIM):
        at_q, at_k, at_v = (slice(g + first, g + first + HEAD_DIM) for g in (0, width, 2 * width))
        query, key, value = qkv_ref[:, at_q], qkv_ref[:, at_k], qkv_ref[:, at_v]
        grad = grad_mixed[:, at_q]
        probs = weights_of(query, key, live)
        grad_dots = (dot_rt(grad, value) * probs * (1.0 - probs)).astype(low)
        grads_ref[:, at_q] = turn(dot(grad_dots, key) * scale, cosine, sine).astype(low)
        grads_ref[:, at_k] = turn(dot_lt(grad_dots, query) * scale, cosine, sine).astype(low)
        grads_ref[:, at_v] = dot_lt(probs.astype(low), grad).astype(low)
    part_ref[...] = dot_rt(grads_ref[...], w_ref[:, : 3 * width]).astype(low)


def attend_back(grad_rows, weights, qkv, cosine, sine, live):
    total, model = grad_rows.shape
    width, seq = weights.shape[1] // 4, live.shape[1]
    tile = lambda columns: pl.BlockSpec((seq, columns), lambda n: (n, 0))
    outs = [jax.ShapeDtypeStruct((total, c), low) for c in (3 * width, model)]
    return pl.pallas_call(
        functools.partial(attend_back_kernel, width),
        grid=(total // seq,),
        in_specs=[
            tile(model),
            whole(weights),
            tile(3 * width),
            tile(HEAD_DIM),
            tile(HEAD_DIM),
            tile(seq),
        ],
        out_specs=[tile(3 * width), tile(model)],
        out_shape=outs,
        compiler_params=params,
        cost_estimate=cost(
            8 * total * model * width + 10 * total * seq * width, grad_rows, weights, qkv, *outs
        ),
    )(grad_rows, weights, qkv, cosine, sine, live)


def gated_kernel(units, rows_ref, grad_ref, w_ref, both_ref, hidden_ref):
    gate = dot(rows_ref[...], w_ref[:, :units])
    upward = dot(rows_ref[...], w_ref[:, units : 2 * units])
    grad_hidden = dot(grad_ref[...], w_ref[:, 2 * units :])
    gate_sig = jax.nn.sigmoid(gate)
    silu = gate * gate_sig
    both_ref[:, :units] = (
        grad_hidden * upward * gate_sig * (1.0 + gate * (1.0 - gate_sig))
    ).astype(low)
    both_ref[:, units:] = (grad_hidden * silu).astype(low)
    hidden_ref[...] = (silu * upward).astype(low)


def gated(rows, grad_rows, weights, tile=512):
    total, model = rows.shape
    units = weights.shape[1] // 3
    tiled = lambda columns: pl.BlockSpec((tile, columns), lambda i: (i, 0))
    outs = [jax.ShapeDtypeStruct((total, c), low) for c in (2 * units, units)]
    return pl.pallas_call(
        functools.partial(gated_kernel, units),
        grid=(total // tile,),
        in_specs=[tiled(model), tiled(model), whole(weights)],
        out_specs=[tiled(2 * units), tiled(units)],
        out_shape=outs,
        compiler_params=params,
        cost_estimate=cost(6 * total * model * units, rows, grad_rows, weights, *outs),
    )(rows, grad_rows, weights)


def project_kernel(first, count, *refs):
    total = None
    for act_ref, w_ref in zip(refs[:count], refs[count : 2 * count]):
        term = dot_rt(act_ref[...], w_ref[:, first : first + act_ref.shape[1]])
        total = term if total is None else total + term
    refs[-1][...] = total.astype(low)


def project(acts, weights, first, tile=256):
    total, wide = acts[0].shape
    model = weights[0].shape[0]
    out = jax.ShapeDtypeStruct((total, model), low)
    return pl.pallas_call(
        functools.partial(project_kernel, first, len(acts)),
        grid=(total // tile,),
        in_specs=[pl.BlockSpec((tile, wide), lambda i: (i, 0))] * len(acts)
        + [whole(w) for w in weights],
        out_specs=pl.BlockSpec((tile, model), lambda i: (i, 0)),
        out_shape=out,
        compiler_params=params,
        cost_estimate=cost(2 * total * model * wide * len(acts), *acts, *weights, out),
    )(*acts, *weights)


def outer_kernel(groups, *refs):
    out_ref = refs[-1]
    refs = list(refs[:-1])
    first = 0
    for count in groups:
        total = None
        for _ in range(count):
            left_ref, right_ref = refs.pop(0), refs.pop(0)
            term = dot_lt(left_ref[...], right_ref[...])
            total = term if total is None else total + term
        out_ref[:, first : first + total.shape[1]] = total.astype(low)
        first += total.shape[1]


def outer(*groups, tile=256):
    model = groups[0][0][0].shape[1]
    wide = sum(group[0][1].shape[1] for group in groups)
    out = jax.ShapeDtypeStruct((model, wide), low)
    operands, specs, flops = [], [], 0
    for group in groups:
        for left, right in group:
            operands += [left, right]
            specs += [pl.BlockSpec((left.shape[0], tile), lambda i: (0, i)), whole(right)]
            flops += 2 * left.shape[0] * model * right.shape[1]
    return pl.pallas_call(
        functools.partial(outer_kernel, [len(group) for group in groups]),
        grid=(model // tile,),
        in_specs=specs,
        out_specs=pl.BlockSpec((tile, wide), lambda i: (i, 0)),
        out_shape=out,
        compiler_params=params,
        cost_estimate=cost(flops, *operands, out),
    )(*operands)


def swap(value, axis):
    return lax.ppermute(value, axis, [(0, 1), (1, 0)])


def gather_plane(own):
    half = own.shape[0] // 2
    from_x = swap(own, "tensor")
    from_y = swap(own, "y")
    chip = jnp.concatenate(
        [own, from_x, from_y, swap(from_x[:half], "y"), swap(from_y[half:], "tensor")], axis=0
    )
    return chip, swap(chip, "c")


def scatter_plane(mine, theirs):
    rows = mine.shape[0] // 4
    half = rows // 2
    other = swap(theirs, "c")

    def piece(dy, dx, bottom):
        first = (2 * dy + dx) * rows + bottom * half
        return mine[first : first + half].astype(f32) + other[first : first + half].astype(f32)

    top_x = swap(jnp.concatenate([piece(0, 1, 0), piece(1, 1, 0)], axis=0).astype(low), "tensor")
    bottom_y = swap(jnp.concatenate([piece(1, 0, 1), piece(1, 1, 1)], axis=0).astype(low), "y")
    top_y = swap((piece(1, 0, 0) + top_x[half:].astype(f32)).astype(low), "y")
    bottom_x = swap((piece(0, 1, 1) + bottom_y[half:].astype(f32)).astype(low), "tensor")
    top = piece(0, 0, 0) + top_x[:half].astype(f32) + top_y.astype(f32)
    bottom = piece(0, 0, 1) + bottom_y[:half].astype(f32) + bottom_x.astype(f32)
    return jnp.concatenate([top, bottom], axis=0)


def to_columns(parts):
    block = lax.all_to_all(parts, ("y", "c"), 0, 0, tiled=True)
    return block.reshape(-1, parts.shape[2])


def to_rows(block):
    parts = block.reshape(PLANE, block.shape[0] // PLANE, block.shape[1])
    return lax.all_to_all(parts, ("y", "c"), 0, 0, tiled=True)


def gather_line(block):
    return lax.all_gather(block, "z", axis=0, tiled=True)


def scatter_line(grads):
    return lax.psum_scatter(grads, "z", scatter_dimension=0, tiled=True)


def quarters(weight, width):
    return jnp.swapaxes(weight.reshape(weight.shape[0], PLANE, width), 0, 1)


def shard_of(parts):
    return jnp.swapaxes(parts, 0, 1).reshape(parts.shape[1], -1).astype(f32)


def shifted(value, step):
    count = lax.axis_size("z")
    return lax.ppermute(value, "z", [(i, (i + step) % count) for i in range(count)])


def plane_flip(value, dy, dc):
    if dy and dc:
        return lax.ppermute(value, ("y", "c"), [(i, i ^ 3) for i in range(4)])
    return swap(value, "y" if dy else "c")


def gather_gains(gains, place, level):
    plane = jnp.zeros((PLANE,) + gains.shape, gains.dtype)
    for flip in range(PLANE):
        piece = plane_flip(gains, flip // 2, flip % 2) if flip else gains
        plane = lax.dynamic_update_index_in_dim(plane, piece, place ^ flip, 0)
    count = lax.axis_size("z")
    every = jnp.zeros((count,) + plane.shape, gains.dtype)
    every = lax.dynamic_update_index_in_dim(every, plane, level, 0)
    for step in range(1, count):
        piece = shifted(plane, step)
        every = lax.dynamic_update_index_in_dim(
            every, piece, lax.rem(level - step + count, count), 0
        )
    return jnp.moveaxis(every, 2, 0).reshape(gains.shape[0], -1)


def scatter_gains(part, place, level):
    count = lax.axis_size("z")
    part = part + swap(part, "tensor")
    blocks = part.reshape(part.shape[0], count, PLANE, -1)
    mine = lax.dynamic_index_in_dim(blocks, place, 2, keepdims=False)
    for flip in range(1, PLANE):
        piece = lax.dynamic_index_in_dim(blocks, place ^ flip, 2, keepdims=False)
        mine = mine + plane_flip(piece, flip // 2, flip % 2)
    result = lax.dynamic_index_in_dim(mine, level, 1, keepdims=False)
    for step in range(1, count):
        piece = lax.dynamic_index_in_dim(mine, lax.rem(level + step, count), 1, keepdims=False)
        result = result + shifted(piece, step)
    return result


def normalize(rows):
    scale = lax.rsqrt(jnp.mean(rows * rows, axis=-1, keepdims=True) + epsilon)
    return rows * scale, scale


def norm_back(grad_normed, unit_rows, scale, gain):
    inner = grad_normed * gain
    mean_term = jnp.mean(inner * unit_rows, axis=-1, keepdims=True)
    return scale * (inner - unit_rows * mean_term), jnp.sum(grad_normed * unit_rows, axis=0)


def local(
    tokens,
    segments,
    gain_attn,
    gain_ffn,
    w_query,
    w_key,
    w_value,
    w_out,
    w_gate,
    w_up,
    w_down,
    cotangent,
):
    seq_len = segments.shape[1]
    side = lax.axis_index("tensor")
    level, place = lax.axis_index("z"), lax.axis_index("y") * 2 + lax.axis_index("c")
    width = w_query.shape[1] // PLANE
    units = w_gate.shape[1] // PLANE
    chunk = units // CHUNKS

    attn_block = to_columns(
        jnp.concatenate([quarters(w, width) for w in (w_query, w_key, w_value, w_out)], axis=2)
    )
    attn_weights = gather_line(attn_block)
    wide = [quarters(w, units) for w in (w_gate, w_up, w_down)]
    ffn_parts = jnp.concatenate(
        [w[:, :, k * chunk : (k + 1) * chunk] for k in range(CHUNKS) for w in wide], axis=2
    )
    ffn_block = to_columns(after(ffn_parts, attn_block))
    ffn_weights = [
        gather_line(ffn_block[:, 3 * k * chunk : 3 * (k + 1) * chunk]) for k in range(CHUNKS)
    ]

    gains = gather_gains(jnp.stack([gain_attn, gain_ffn]), place, level).astype(f32)
    gain_first, gain_second = gains[0], gains[1]
    inputs = tokens.astype(f32)
    unit_one, scale_one = normalize(inputs)
    rows_one = gather_plane((unit_one * gain_first).astype(low))
    grad_rows = gather_plane(after(cotangent, rows_one[0]))
    seg = jnp.concatenate(
        [segments] + [plane_flip(segments, dy, dc) for dc, dy in ((0, 1), (1, 0), (1, 1))], axis=0
    )
    places = lax.rem(jnp.arange(seq_len, dtype=jnp.int32) + side * (seq_len // 2), seq_len)
    seg = jnp.where(side == 0, seg, jnp.roll(seg, seq_len // 2, axis=1))
    same = seg[:, :, None] == seg[:, None, :]
    live = same & (places[None, None, :] <= places[None, :, None])
    positions = jnp.sum(live.astype(jnp.int32), axis=2) - 1
    freqs = theta ** (-(jnp.arange(HEAD_DIM // 2, dtype=f32) * 2.0 / HEAD_DIM))
    angles = (positions.astype(f32)[..., None] * freqs).reshape(2, -1, HEAD_DIM // 2)
    cosine, sine = jnp.cos(angles), jnp.sin(angles)
    cosine = jnp.concatenate([cosine, cosine], axis=2)
    sine = jnp.concatenate([-sine, sine], axis=2)
    live = live.astype(low).reshape(2, -1, seq_len)
    sides = range(2)

    qkv, mixed, parts = zip(
        *(attend(rows_one[i], attn_weights, cosine[i], sine[i], live[i]) for i in sides)
    )
    middle = inputs + scatter_plane(*parts)
    unit_two, scale_two = normalize(middle)
    rows_two = gather_plane((unit_two * gain_second).astype(low))

    both = [[None] * CHUNKS for _ in sides]
    hidden = [[None] * CHUNKS for _ in sides]
    ffn_sums = []
    grad_parts = None
    for k in range(CHUNKS):
        for i in sides:
            both[i][k], hidden[i][k] = gated(rows_two[i], grad_rows[i], ffn_weights[k])
        if k == CHUNKS - 1:
            grad_parts = [project(both[i], ffn_weights, 0) for i in sides]
        sums = outer(
            [(rows_two[i], both[i][k]) for i in sides],
            [(grad_rows[i], hidden[i][k]) for i in sides],
        )
        ffn_sums.append(to_rows(scatter_line(sums)))
    grad_normed_two = scatter_plane(*grad_parts)
    grad_unit_two, gain_two_part = norm_back(grad_normed_two, unit_two, scale_two, gain_second)
    grad_middle = cotangent.astype(f32) + grad_unit_two
    grad_branch = gather_plane(after(grad_middle.astype(low), sums))

    grads, parts = zip(
        *(
            attend_back(grad_branch[i], attn_weights, qkv[i], cosine[i], sine[i], live[i])
            for i in sides
        )
    )
    attn_sums = to_rows(
        scatter_line(
            outer(
                [(rows_one[i], grads[i]) for i in sides],
                [(grad_branch[i], mixed[i]) for i in sides],
            )
        )
    )
    grad_normed_one = scatter_plane(*parts)
    grad_unit_one, gain_one_part = norm_back(grad_normed_one, unit_one, scale_one, gain_first)
    grad_tokens = grad_middle + grad_unit_one
    out_parts = [project(after(hidden[i], grad_branch[1]), ffn_weights, 2 * chunk) for i in sides]
    output = (middle + scatter_plane(*out_parts)).astype(low)
    gain_sums = scatter_gains(jnp.stack([gain_one_part, gain_two_part]), place, level)

    attn_grads = [shard_of(attn_sums[:, :, k * width : (k + 1) * width]) for k in range(4)]
    ffn_grads = [
        shard_of(jnp.concatenate([s[:, :, k * chunk : (k + 1) * chunk] for s in ffn_sums], axis=2))
        for k in range(3)
    ]
    return (output, grad_tokens, gain_sums[0], gain_sums[1], *attn_grads, *ffn_grads)


def solution(mesh):
    lines = mesh.shape["dp"] // PLANE
    finer = Mesh(
        mesh.devices.reshape(lines, 2, 2, mesh.shape["tensor"]), ("z", "y", "c", "tensor")
    )
    dp = ("z", "y", "c")
    rows, grid = P(dp + ("tensor",), None), P(dp, "tensor")
    return jax.shard_map(
        local,
        mesh=finer,
        in_specs=(rows, P(dp, None), P(dp), P(dp)) + (grid,) * 7 + (rows,),
        out_specs=(rows, rows, P(dp), P(dp)) + (grid,) * 7,
        check_vma=False,
    )
```

time: 843 us -> 800 us (0.949)
  matrix products: 216 us -> 0 us
  Pallas kernels: 0 us -> 210 us
  waiting for transfers between devices: 265 us -> 376 us
  local copies, waits for them, and re-layouts: 158 us -> 48.7 us
  blocking collectives: 22.7 us -> 0 us
  starting transfers between devices: 90.6 us -> 78.1 us
    dot_general x25 -> x0, matrix products: 216 us -> none  [the longest x8 80.9 us: dot(): return jnp.dot(left, right, preferred_element_type=f32)]
    pallas_call x0 -> x15, Pallas kernels: none -> 210 us  [the longest x3 54.8 us: outer(): pl.pallas_call(functools.partial(outer_kernel, [len(group) for group in g...]
    ppermute x50 -> x47, waiting for transfers between devices: 222 us -> 342 us  [swap(): return lax.ppermute(value, axis, [(0, 1), (1, 0)])]
    unnamed x152 -> x67, local copies, waits for them, and re-layouts: 72.1 us -> 21.4 us
    all_to_all x1 -> x0, blocking collectives: 22.7 us -> none  [to_columns(): block = lax.all_to_all(parts, ('y', 'c'), 0, 0, tiled=True)]
    concatenate x7 -> x1, local copies, waits for them, and re-layouts: 21.8 us -> 0.89 us  [local(): jnp.concatenate([w[:, :, k * chunk:(k + 1) * chunk] for k in range(CHUNKS...]
    add x22 -> x11, other arithmetic: 36.3 us -> 16.7 us  [the longest x4 8.92 us: scatter_plane(): top = piece(0, 0, 0) + top_x[:half].astype(f32) + top_y.astype(f32)]
    slice x14 -> x4, local copies, waits for them, and re-layouts: 27.2 us -> 9.33 us  [the longest x2 4.12 us: local(): s[:, :, k * chunk:(k + 1) * chunk]]
  transfers between devices with their start and end apart: 80 -> 67, of which waited for: 35 -> 32; matrix products, arithmetic and copies ran while one was open for 44% -> 13% of each run, Pallas kernels for 0% -> 26%
where the time goes in v3:
time: 800 us; the launch traced here: 793 us
  waiting for transfers between devices  376 us (47%)
  Pallas kernels  210 us (26%)
  starting transfers between devices  78.1 us (10%)
  other arithmetic  65.7 us (8%)
  local copies, waits for them, and re-layouts  48.7 us (6%)
  between operations  15.2 us (2%)
    ppermute x47, waiting for transfers between devices, swap(): return lax.ppermute(value, axis, [(0, 1), (1, 0)])  342 us
    pallas_call x3, Pallas kernels, outer(): pl.pallas_call(functools.partial(outer_kernel, [len(group) for group in g...  54.8 us
    pallas_call x4, Pallas kernels, project(): pl.pallas_call(functools.partial(project_kernel, first, len(acts)), grid=...  53.2 us
    pallas_call x4, Pallas kernels, gated(): pl.pallas_call(functools.partial(gated_kernel, units), grid=(total // til...  49.2 us
    ppermute x47, starting transfers between devices, swap(): return lax.ppermute(value, axis, [(0, 1), (1, 0)])  45.7 us
    pallas_call x2, Pallas kernels, attend_back(): pl.pallas_call(functools.partial(attend_back_kernel, width), grid=(total...  28.2 us
    pallas_call x2, Pallas kernels, attend(): pl.pallas_call(functools.partial(attend_kernel, width), grid=(total // se...  24.6 us
    all_to_all x3, waiting for transfers between devices, to_rows(): return lax.all_to_all(parts, ('y', 'c'), 0, 0, tiled=True)  21.8 us
  transfers between devices with their start and end apart: 67, of which 32 were waited for; matrix products, arithmetic and copies ran while one was open for 13% of the time, Pallas kernels for 26%

profile of v3, /device:TPU:0, one launch (start us, length us, event | category | flops | bytes accessed | tf_op | source)
XLA Modules:
  0.0 793.2 jit_solution(530823298925482288)
XLA Ops:
  35.1 17.2 %collective-permute-done.6 = bf16[256,2048]{1,0:T(8,128)(2,1)S(1)} collective-permute-done((bf16[256,2048]{1,0:T(8,128)(2,1)}, bf16[256,2048]{1,0:T(8,128)(2,1)S(1)}, u32[]{:S(2)}, u32[]{:S(2)}) %collective-permute-start.6) | collective-permute-done | bytes 1048608 | tf_op jit(solution)/shard_map/ppermute | solution.py:224
  83.6 34.5 %collective-permute-done.10 = s32[1,512]{1,0:T(1,128)S(1)} collective-permute-done((s32[1,512]{1,0:T(1,128)S(1)}, s32[1,512]{1,0:T(1,128)S(1)}, u32[]{:S(2)}, u32[]{:S(2)}) %collective-permute-start.10) | collective-permute-done | bytes 2080 | tf_op jit(solution)/shard_map/ppermute | solution.py:224
  134.5 12.3 %shard_map.204 = (bf16[1024,768]{1,0:T(8,128)(2,1)}, bf16[1024,256]{1,0:T(8,128)(2,1)}, bf16[1024,2048]{1,0:T(8,128)(2,1)}) custom-call(bf16[1024,2048]{1,0:T(8,128)(2,1)} %collective-permute-done.13.rows_ref.refs_2_, bf16[2048,1024]{1,0:T(8,128)(2,1)} %all-gather.4.cloned.1.call-done.w_ref, f32[1024,128]{1,0:T(8,128)} %get-tuple-element.142.cos_ref, ...), custom_call_target="tpu_custom_call" | custom-call | flops 4831838208 | bytes 14680064 | tf_op jit(solution)/shard_map/pallas_call | solution.py:80
  146.9 12.3 %shard_map.203 = (bf16[1024,768]{1,0:T(8,128)(2,1)}, bf16[1024,256]{1,0:T(8,128)(2,1)}, bf16[1024,2048]{1,0:T(8,128)(2,1)}) custom-call(bf16[1024,2048]{1,0:T(8,128)(2,1)} %constant_dynamic-update-slice_fusion.rows_ref.refs_0_, bf16[2048,1024]{1,0:T(8,128)(2,1)} %all-gather.4.cloned.1.call-done.w_ref, f32[1024,128]{1,0:T(8,128)} %get-tuple-element.143.cos_ref, ...), custom_call_target="tpu_custom_call" | custom-call | flops 4831838208 | bytes 14680064 | tf_op jit(solution)/shard_map/pallas_call | solution.py:80
  163.6 23.8 %collective-permute-done.15 = bf16[256,2048]{1,0:T(8,128)(2,1)S(1)} collective-permute-done((bf16[256,2048]{1,0:T(8,128)(2,1)S(1)}, bf16[256,2048]{1,0:T(8,128)(2,1)S(1)}, u32[]{:S(2)}, u32[]{:S(2)}) %collective-permute-start.15) | collective-permute-done | bytes 1048608 | tf_op jit(solution)/shard_map/ppermute | solution.py:224
  190.2 34.0 %collective-permute-done.16 = bf16[128,2048]{1,0:T(8,128)(2,1)S(1)} collective-permute-done((bf16[128,2048]{1,0:T(8,128)(2,1)S(1)}, bf16[128,2048]{1,0:T(8,128)(2,1)S(1)}, u32[]{:S(2)}, u32[]{:S(2)}) %collective-permute-start.16) | collective-permute-done | bytes 524320 | tf_op jit(solution)/shard_map/ppermute | solution.py:224
  228.4 12.2 %collective-permute-done.18 = bf16[128,2048]{1,0:T(8,128)(2,1)S(1)} collective-permute-done((bf16[128,2048]{1,0:T(8,128)(2,1)S(1)}, bf16[128,2048]{1,0:T(8,128)(2,1)S(1)}, u32[]{:S(2)}, u32[]{:S(2)}) %collective-permute-start.18) | collective-permute-done | bytes 524320 | tf_op jit(solution)/shard_map/ppermute | solution.py:224
  246.8 16.5 %collective-permute-done.23 = bf16[256,2048]{1,0:T(8,128)(2,1)} collective-permute-done((bf16[256,2048]{1,0:T(8,128)(2,1)}, bf16[256,2048]{1,0:T(8,128)(2,1)}, u32[]{:S(2)}, u32[]{:S(2)}) %collective-permute-start.23) | collective-permute-done | bytes 1048608 | tf_op jit(solution)/shard_map/ppermute | solution.py:224
  286.0 8.7 %collective-permute-done.26 = bf16[128,2048]{1,0:T(8,128)(2,1)S(1)} collective-permute-done((bf16[128,2048]{1,0:T(8,128)(2,1)S(1)}, bf16[128,2048]{1,0:T(8,128)(2,1)S(1)}, u32[]{:S(2)}, u32[]{:S(2)}) %collective-permute-start.26) | collective-permute-done | bytes 524320 | tf_op jit(solution)/shard_map/ppermute | solution.py:224
  311.8 12.4 %shard_map.205 = (bf16[1024,1024]{1,0:T(8,128)(2,1)}, bf16[1024,512]{1,0:T(8,128)(2,1)}) custom-call(bf16[1024,2048]{1,0:T(8,128)(2,1)} %constant_dynamic-update-slice_fusion.5.rows_ref.refs_0_, bf16[1024,2048]{1,0:T(8,128)(2,1)} %constant_dynamic-update-slice_fusion.10.grad_ref.refs_4_, bf16[2048,1536]{1,0:T(8,128)(2,1)} %all-gather.6.cloned.1.call-done.w_ref.refs_2_), custom_call_target="tpu_custom_call" | custom-call | flops 6442450944 | bytes 17825792 | tf_op jit(solution)/shard_map/pallas_call | solution.py:153
  324.2 12.3 %shard_map.208 = (bf16[1024,1024]{1,0:T(8,128)(2,1)}, bf16[1024,512]{1,0:T(8,128)(2,1)}) custom-call(bf16[1024,2048]{1,0:T(8,128)(2,1)} %collective-permute-done.27.rows_ref.refs_2_, bf16[1024,2048]{1,0:T(8,128)(2,1)} %collective-permute-done.28.grad_ref.refs_6_, bf16[2048,1536]{1,0:T(8,128)(2,1)} %all-gather.6.cloned.1.call-done.w_ref.refs_2_), custom_call_target="tpu_custom_call" | custom-call | flops 6442450944 | bytes 17825792 | tf_op jit(solution)/shard_map/pallas_call | solution.py:153
  336.5 19.3 %shard_map.217 = bf16[2048,1536]{1,0:T(8,128)(2,1)} custom-call(bf16[1024,2048]{1,0:T(8,128)(2,1)} %constant_dynamic-update-slice_fusion.5.rows_ref.refs_0_, bf16[1024,1024]{1,0:T(8,128)(2,1)} %get-tuple-element.42.refs_0_.refs_1_, bf16[1024,2048]{1,0:T(8,128)(2,1)} %collective-permute-done.27.rows_ref.refs_2_, ...), custom_call_target="tpu_custom_call" | custom-call | flops 12884901888 | bytes 29360128 | tf_op jit(solution)/shard_map/pallas_call | solution.py:212
  362.7 12.3 %shard_map.209 = (bf16[1024,1024]{1,0:T(8,128)(2,1)}, bf16[1024,512]{1,0:T(8,128)(2,1)}) custom-call(bf16[1024,2048]{1,0:T(8,128)(2,1)} %collective-permute-done.27.rows_ref.refs_2_, bf16[1024,2048]{1,0:T(8,128)(2,1)} %collective-permute-done.28.grad_ref.refs_6_, bf16[2048,1536]{1,0:T(8,128)(2,1)} %all-gather.8.cloned.1.call-done.w_ref.refs_3_), custom_call_target="tpu_custom_call" | custom-call | flops 6442450944 | bytes 17825792 | tf_op jit(solution)/shard_map/pallas_call | solution.py:153
  374.9 15.5 %shard_map.210 = bf16[1024,2048]{1,0:T(8,128)(2,1)} custom-call(bf16[1024,1024]{1,0:T(8,128)(2,1)} %get-tuple-element.44.refs_0_.refs_3_, bf16[1024,1024]{1,0:T(8,128)(2,1)} %get-tuple-element.45.refs_1_.refs_3_, bf16[2048,1536]{1,0:T(8,128)(2,1)} %all-gather.6.cloned.1.call-done.w_ref.refs_2_, bf16[2048,1536]{1,0:T(8,128)(2,1)} %all-gather.8.cloned.1.call-done.w_ref.refs_3_), custom_call_target="tpu_custom_call" | custom-call | flops 8589934592 | bytes 20971520 | tf_op jit(solution)/shard_map/pallas_call | solution.py:176
  390.4 12.3 %shard_map.206 = (bf16[1024,1024]{1,0:T(8,128)(2,1)}, bf16[1024,512]{1,0:T(8,128)(2,1)}) custom-call(bf16[1024,2048]{1,0:T(8,128)(2,1)} %constant_dynamic-update-slice_fusion.5.rows_ref.refs_0_, bf16[1024,2048]{1,0:T(8,128)(2,1)} %constant_dynamic-update-slice_fusion.10.grad_ref.refs_4_, bf16[2048,1536]{1,0:T(8,128)(2,1)} %all-gather.8.cloned.1.call-done.w_ref.refs_3_), custom_call_target="tpu_custom_call" | custom-call | flops 6442450944 | bytes 17825792 | tf_op jit(solution)/shard_map/pallas_call | solution.py:153
  402.7 15.5 %shard_map.207 = bf16[1024,2048]{1,0:T(8,128)(2,1)} custom-call(bf16[1024,1024]{1,0:T(8,128)(2,1)} %get-tuple-element.42.refs_0_.refs_1_, bf16[1024,1024]{1,0:T(8,128)(2,1)} %get-tuple-element.43.refs_1_, bf16[2048,1536]{1,0:T(8,128)(2,1)} %all-gather.6.cloned.1.call-done.w_ref.refs_2_, bf16[2048,1536]{1,0:T(8,128)(2,1)} %all-gather.8.cloned.1.call-done.w_ref.refs_3_), custom_call_target="tpu_custom_call" | custom-call | flops 8589934592 | bytes 20971520 | tf_op jit(solution)/shard_map/pallas_call | solution.py:176
  422.4 24.1 %collective-permute-done.30 = bf16[256,2048]{1,0:T(8,128)(2,1)S(1)} collective-permute-done((bf16[256,2048]{1,0:T(8,128)(2,1)S(1)}, bf16[256,2048]{1,0:T(8,128)(2,1)S(1)}, u32[]{:S(2)}, u32[]{:S(2)}) %collective-permute-start.30) | collective-permute-done | bytes 1048608 | tf_op jit(solution)/shard_map/ppermute | solution.py:224
  449.3 34.0 %collective-permute-done.31 = bf16[128,2048]{1,0:T(8,128)(2,1)S(1)} collective-permute-done((bf16[128,2048]{1,0:T(8,128)(2,1)S(1)}, bf16[128,2048]{1,0:T(8,128)(2,1)S(1)}, u32[]{:S(2)}, u32[]{:S(2)}) %collective-permute-start.31) | collective-permute-done | bytes 524320 | tf_op jit(solution)/shard_map/ppermute | solution.py:224
  486.5 19.5 %shard_map.211 = bf16[2048,1536]{1,0:T(8,128)(2,1)} custom-call(bf16[1024,2048]{1,0:T(8,128)(2,1)} %constant_dynamic-update-slice_fusion.5.rows_ref.refs_0_, bf16[1024,1024]{1,0:T(8,128)(2,1)} %get-tuple-element.43.refs_1_, bf16[1024,2048]{1,0:T(8,128)(2,1)} %collective-permute-done.27.rows_ref.refs_2_, ...), custom_call_target="tpu_custom_call" | custom-call | flops 12884901888 | bytes 29360128 | tf_op jit(solution)/shard_map/pallas_call | solution.py:212
  514.0 21.7 %collective-permute-done.34 = bf16[256,2048]{1,0:T(8,128)(2,1)S(1)} collective-permute-done((bf16[256,2048]{1,0:T(8,128)(2,1)S(1)}, bf16[256,2048]{1,0:T(8,128)(2,1)S(1)}, u32[]{:S(2)}, u32[]{:S(2)}) %collective-permute-start.34) | collective-permute-done | bytes 1048608 | tf_op jit(solution)/shard_map/ppermute | solution.py:224
  538.4 8.8 %collective-permute-done.36 = bf16[128,2048]{1,0:T(8,128)(2,1)S(1)} collective-permute-done((bf16[128,2048]{1,0:T(8,128)(2,1)S(1)}, bf16[128,2048]{1,0:T(8,128)(2,1)S(1)}, u32[]{:S(2)}, u32[]{:S(2)}) %collective-permute-start.36) | collective-permute-done | bytes 524320 | tf_op jit(solution)/shard_map/ppermute | solution.py:224
  548.9 7.1 collective-permute-done.38.grad_ref.refs_6_
  558.0 14.2 %shard_map.215 = (bf16[1024,768]{1,0:T(8,128)(2,1)}, bf16[1024,2048]{1,0:T(8,128)(2,1)}) custom-call(bf16[1024,2048]{1,0:T(8,128)(2,1)} %copy-done.23, bf16[2048,1024]{1,0:T(8,128)(2,1)} %all-gather.4.cloned.1.call-done.w_ref, bf16[1024,768]{1,0:T(8,128)(2,1)} %get-tuple-element.55.qkv_ref, f32[1024,128]{1,0:T(8,128)} %get-tuple-element.142.cos_ref, ...), custom_call_target="tpu_custom_call" | custom-call | flops 5637144576 | bytes 15728640 | tf_op jit(solution)/shard_map/pallas_call | solution.py:115
  572.4 11.1 %shard_map.213 = bf16[1024,2048]{1,0:T(8,128)(2,1)} custom-call(bf16[1024,512]{1,0:T(8,128)(2,1)} %get-tuple-element.51.refs_0_.refs_7_, bf16[1024,512]{1,0:T(8,128)(2,1)} %get-tuple-element.52.refs_7_.refs_1_, bf16[2048,1536]{1,0:T(8,128)(2,1)} %all-gather.6.cloned.1.call-done.w_ref.refs_2_, bf16[2048,1536]{1,0:T(8,128)(2,1)} %all-gather.8.cloned.1.call-done.w_ref.refs_3_), custom_call_target="tpu_custom_call" | custom-call | flops 4294967296 | bytes 18874368 | tf_op jit(solution)/shard_map/pallas_call | solution.py:176
  583.8 14.0 %shard_map.214 = (bf16[1024,768]{1,0:T(8,128)(2,1)}, bf16[1024,2048]{1,0:T(8,128)(2,1)}) custom-call(bf16[1024,2048]{1,0:T(8,128)(2,1)} %copy-done.17, bf16[2048,1024]{1,0:T(8,128)(2,1)} %all-gather.4.cloned.1.call-done.w_ref, bf16[1024,768]{1,0:T(8,128)(2,1)} %get-tuple-element.53.qkv_ref, f32[1024,128]{1,0:T(8,128)} %get-tuple-element.143.cos_ref, ...), custom_call_target="tpu_custom_call" | custom-call | flops 5637144576 | bytes 15728640 | tf_op jit(solution)/shard_map/pallas_call | solution.py:115
  602.3 15.9 %shard_map.216 = bf16[2048,1024]{1,0:T(8,128)(2,1)} custom-call(bf16[1024,2048]{1,0:T(8,128)(2,1)} %constant_dynamic-update-slice_fusion.rows_ref.refs_0_, bf16[1024,768]{1,0:T(8,128)(2,1)} %get-tuple-element.57.refs_1_, bf16[1024,2048]{1,0:T(8,128)(2,1)} %collective-permute-done.13.rows_ref.refs_2_, bf16[1024,768]{1,0:T(8,128)(2,1)} %get-tuple-element.58.refs_3_, ...), custom_call_target="tpu_custom_call" | custom-call | flops 8589934592 | bytes 25165824 | tf_op jit(solution)/shard_map/pallas_call | solution.py:212
  618.2 11.1 %shard_map.212 = bf16[1024,2048]{1,0:T(8,128)(2,1)} custom-call(bf16[1024,512]{1,0:T(8,128)(2,1)} %get-tuple-element.48.refs_0_.refs_5_, bf16[1024,512]{1,0:T(8,128)(2,1)} %get-tuple-element.49.refs_5_.refs_1_, bf16[2048,1536]{1,0:T(8,128)(2,1)} %all-gather.6.cloned.1.call-done.w_ref.refs_2_, bf16[2048,1536]{1,0:T(8,128)(2,1)} %all-gather.8.cloned.1.call-done.w_ref.refs_3_), custom_call_target="tpu_custom_call" | custom-call | flops 4294967296 | bytes 18874368 | tf_op jit(solution)/shard_map/pallas_call | solution.py:176
  646.4 10.3 %all-to-all-done.4 = bf16[4,128,1536]{2,1,0:T(8,128)(2,1)} async-done(((bf16[4,128,1536]{2,1,0:T(8,128)(2,1)}), bf16[4,128,1536]{2,1,0:T(8,128)(2,1)}, u32[]{:S(2)}, u32[]{:S(2)}) %all-to-all-start.4) | async-done | bytes 1572896 | tf_op jit(solution)/shard_map/all_to_all | solution.py:262
  670.3 17.0 %collective-permute-done.40 = bf16[256,2048]{1,0:T(8,128)(2,1)} collective-permute-done((bf16[256,2048]{1,0:T(8,128)(2,1)}, bf16[256,2048]{1,0:T(8,128)(2,1)}, u32[]{:S(2)}, u32[]{:S(2)}) %collective-permute-start.40) | collective-permute-done | bytes 1048608 | tf_op jit(solution)/shard_map/ppermute | solution.py:224
  697.4 8.1 %collective-permute-done.46 = bf16[128,2048]{1,0:T(8,128)(2,1)S(1)} collective-permute-done((bf16[128,2048]{1,0:T(8,128)(2,1)S(1)}, bf16[128,2048]{1,0:T(8,128)(2,1)S(1)}, u32[]{:S(2)}, u32[]{:S(2)}) %collective-permute-start.46) | collective-permute-done | bytes 524320 | tf_op jit(solution)/shard_map/ppermute | solution.py:224
  708.3 29.1 %collective-permute-done.41 = bf16[128,2048]{1,0:T(8,128)(2,1)S(1)} collective-permute-done((bf16[128,2048]{1,0:T(8,128)(2,1)S(1)}, bf16[128,2048]{1,0:T(8,128)(2,1)S(1)}, u32[]{:S(2)}, u32[]{:S(2)}) %collective-permute-start.41) | collective-permute-done | bytes 524320 | tf_op jit(solution)/shard_map/ppermute | solution.py:224
  769.8 11.5 %all-to-all-done.2 = bf16[4,128,1024]{2,1,0:T(8,128)(2,1)} async-done(((bf16[4,128,1024]{2,1,0:T(8,128)(2,1)}), bf16[4,128,1024]{2,1,0:T(8,128)(2,1)}, u32[]{:S(2)}, u32[]{:S(2)}) %all-to-all-start.2) | async-done | bytes 1048608 | tf_op jit(solution)/shard_map/all_to_all | solution.py:262
  (293 shorter events, 249.3 us)
Async XLA Ops:
  17.8 116.7 %all-gather.4.cloned.1.call-start = ((), (), s32[]{:S(2)}) async-start(), calls=%async_computation.8 | async-start | bytes 5242880 | tf_op jit(solution)/shard_map/all_gather | solution.py:266
  33.3 26.3 %collective-permute-start.7 = (bf16[256,2048]{1,0:T(8,128)(2,1)}, bf16[256,2048]{1,0:T(8,128)(2,1)S(1)}, u32[]{:S(2)}, u32[]{:S(2)}) collective-permute-start(bf16[256,2048]{1,0:T(8,128)(2,1)} %get-tuple-element.72), channel_id=1, source_target_pairs={{0,4},{4,0},{1,5},{5,1},{2,6},{6,2},{3,7},{7,3},{8,12},{12,8},{9,1... | collective-permute-start | bytes 3145736 | tf_op jit(solution)/shard_map/ppermute | solution.py:224
  71.9 62.7 %collective-permute-start.13 = (bf16[1024,2048]{1,0:T(8,128)(2,1)}, bf16[1024,2048]{1,0:T(8,128)(2,1)}, u32[]{:S(2)}, u32[]{:S(2)}) collective-permute-start(bf16[1024,2048]{1,0:T(8,128)(2,1)} %constant_dynamic-update-slice_fusion.rows_ref.refs_0_), channel_id=1, source_target_pairs={{0,2},{2,0},{1,3},{3,1},{4,6},{6,4},{5,7},{7,5},{8,10},{10,8},{9,1... | collective-permute-start | bytes 12582920 | tf_op jit(solution)/shard_map/ppermute | solution.py:224
  76.3 50.8 %all-to-all-start.1 = ((bf16[4,128,3072]{2,1,0:T(8,128)(2,1)}), bf16[4,128,3072]{2,1,0:T(8,128)(2,1)}, u32[]{:S(2)}, u32[]{:S(2)}) async-start(bf16[4,128,3072]{2,1,0:T(8,128)(2,1)} %slice_dynamic-update-slice_fusion), calls=%async_computation.1 | async-start | bytes 6291456 | tf_op jit(solution)/shard_map/all_to_all | solution.py:256
  81.1 230.7 %all-gather.6.cloned.1.call-start = ((), (), s32[]{:S(2)}) async-start(), calls=%async_computation.9 | async-start | bytes 7864320 | tf_op jit(solution)/shard_map/all_gather | solution.py:266
  81.2 37.0 %collective-permute-start.10 = (s32[1,512]{1,0:T(1,128)S(1)}, s32[1,512]{1,0:T(1,128)S(1)}, u32[]{:S(2)}, u32[]{:S(2)}) collective-permute-start(s32[1,512]{1,0:T(1,128)S(1)} %copy-done.22), channel_id=1, source_target_pairs={{0,4},{4,0},{1,5},{5,1},{2,6},{6,2},{3,7},{7,3},{8,12},{12,8},{9,1... | collective-permute-start | bytes 6152 | tf_op jit(solution)/shard_map/ppermute | solution.py:224
  83.1 35.1 %collective-permute-start.11 = (s32[1,512]{1,0:T(1,128)S(1)}, s32[1,512]{1,0:T(1,128)S(1)}, u32[]{:S(2)}, u32[]{:S(2)}) collective-permute-start(s32[1,512]{1,0:T(1,128)S(1)} %copy-done.22), channel_id=1, source_target_pairs={{0,2},{2,0},{1,3},{3,1},{4,6},{6,4},{5,7},{7,5},{8,10},{10,8},{9,1... | collective-permute-start | bytes 6152 | tf_op jit(solution)/shard_map/ppermute | solution.py:224
  83.1 35.1 %collective-permute-start.12 = (s32[1,512]{1,0:T(1,128)S(1)}, s32[1,512]{1,0:T(1,128)S(1)}, u32[]{:S(2)}, u32[]{:S(2)}) collective-permute-start(s32[1,512]{1,0:T(1,128)S(1)} %copy-done.22), channel_id=1, source_target_pairs={{0,6},{2,4},{4,2},{6,0},{1,7},{3,5},{5,3},{7,1},{8,14},{10,12},{12... | collective-permute-start | bytes 6152 | tf_op jit(solution)/shard_map/ppermute | solution.py:288
  130.9 231.8 %all-gather.8.cloned.1.call-start = ((), (), s32[]{:S(2)}) async-start(), calls=%async_computation.10 | async-start | bytes 7864320 | tf_op jit(solution)/shard_map/all_gather | solution.py:266
  188.1 36.1 %collective-permute-start.17 = (bf16[256,2048]{1,0:T(8,128)(2,1)S(1)}, bf16[256,2048]{1,0:T(8,128)(2,1)S(1)}, u32[]{:S(2)}, u32[]{:S(2)}) collective-permute-start(bf16[256,2048]{1,0:T(8,128)(2,1)S(1)} %pad_maximum_fusion.4), channel_id=1, source_target_pairs={{0,4},{4,0},{1,5},{5,1},{2,6},{6,2},{3,7},{7,3},{8,12},{12,8},{9,1... | collective-permute-start | bytes 3145736 | tf_op jit(solution)/shard_map/ppermute | solution.py:224
  188.5 35.7 %collective-permute-start.16 = (bf16[128,2048]{1,0:T(8,128)(2,1)S(1)}, bf16[128,2048]{1,0:T(8,128)(2,1)S(1)}, u32[]{:S(2)}, u32[]{:S(2)}) collective-permute-start(bf16[128,2048]{1,0:T(8,128)(2,1)S(1)} %get-tuple-element.98), channel_id=1, source_target_pairs={{0,4},{4,0},{1,5},{5,1},{2,6},{6,2},{3,7},{7,3},{8,12},{12,8},{9,1... | collective-permute-start | bytes 1572872 | tf_op jit(solution)/shard_map/ppermute | solution.py:224
  227.5 35.7 %collective-permute-start.23 = (bf16[256,2048]{1,0:T(8,128)(2,1)}, bf16[256,2048]{1,0:T(8,128)(2,1)}, u32[]{:S(2)}, u32[]{:S(2)}) collective-permute-start(bf16[256,2048]{1,0:T(8,128)(2,1)} %param.23), channel_id=1, source_target_pairs={{0,1},{1,0},{2,3},{3,2},{4,5},{5,4},{6,7},{7,6},{8,9},{9,8},{10,11... | collective-permute-start | bytes 3145736 | tf_op jit(solution)/shard_map/ppermute | solution.py:224
  227.8 40.9 %collective-permute-start.24 = (bf16[256,2048]{1,0:T(8,128)(2,1)}, bf16[256,2048]{1,0:T(8,128)(2,1)}, u32[]{:S(2)}, u32[]{:S(2)}) collective-permute-start(bf16[256,2048]{1,0:T(8,128)(2,1)} %param.23), channel_id=1, source_target_pairs={{0,4},{4,0},{1,5},{5,1},{2,6},{6,2},{3,7},{7,3},{8,12},{12,8},{9,1... | collective-permute-start | bytes 3145736 | tf_op jit(solution)/shard_map/ppermute | solution.py:224
  228.2 369.7 %reduce-scatter.6.cloned.1.call-start = ((), (), s32[]{:S(2)}) async-start(), calls=%async_computation.12 | async-start | bytes 7864320 | tf_op jit(solution)/shard_map/reduce_scatter | solution.py:270
  245.0 40.5 %collective-permute-start.19 = (bf16[256,2048]{1,0:T(8,128)(2,1)S(1)}, bf16[256,2048]{1,0:T(8,128)(2,1)S(1)}, u32[]{:S(2)}, u32[]{:S(2)}) collective-permute-start(bf16[256,2048]{1,0:T(8,128)(2,1)S(1)} %get-tuple-element.68), channel_id=1, source_target_pairs={{0,1},{1,0},{2,3},{3,2},{4,5},{5,4},{6,7},{7,6},{8,9},{9,8},{10,11... | collective-permute-start | bytes 3145736 | tf_op jit(solution)/shard_map/ppermute | solution.py:224
  264.7 37.0 %collective-permute-start.20 = (bf16[256,2048]{1,0:T(8,128)(2,1)S(1)}, bf16[256,2048]{1,0:T(8,128)(2,1)S(1)}, u32[]{:S(2)}, u32[]{:S(2)}) collective-permute-start(bf16[256,2048]{1,0:T(8,128)(2,1)S(1)} %get-tuple-element.68), channel_id=1, source_target_pairs={{0,4},{4,0},{1,5},{5,1},{2,6},{6,2},{3,7},{7,3},{8,12},{12,8},{9,1... | collective-permute-start | bytes 3145736 | tf_op jit(solution)/shard_map/ppermute | solution.py:224
  295.6 28.6 %collective-permute-start.28 = (bf16[1024,2048]{1,0:T(8,128)(2,1)}, bf16[1024,2048]{1,0:T(8,128)(2,1)}, u32[]{:S(2)}, u32[]{:S(2)}) collective-permute-start(bf16[1024,2048]{1,0:T(8,128)(2,1)} %constant_dynamic-update-slice_fusion.10.grad_ref.refs_4_), channel_id=1, source_target_pairs={{0,2},{2,0},{1,3},{3,1},{4,6},{6,4},{5,7},{7,5},{8,10},{10,8},{9,1... | collective-permute-start | bytes 12582920 | tf_op jit(solution)/shard_map/ppermute | solution.py:224
  355.9 276.3 %reduce-scatter.8.cloned.1.call-start = ((), (), s32[]{:S(2)}) async-start(), calls=%async_computation.13 | async-start | bytes 7864320 | tf_op jit(solution)/shard_map/reduce_scatter | solution.py:270
  390.4 27.9 %collective-permute-start.29 = (bf16[1024,2048]{1,0:T(8,128)(2,1)}, bf16[1024,2048]{1,0:T(8,128)(2,1)S(1)}, u32[]{:S(2)}, u32[]{:S(2)}) collective-permute-start(bf16[1024,2048]{1,0:T(8,128)(2,1)} %shard_map.210), channel_id=1, source_target_pairs={{0,2},{2,0},{1,3},{3,1},{4,6},{6,4},{5,7},{7,5},{8,10},{10,8},{9,1... | collective-permute-start | bytes 12582920 | tf_op jit(solution)/shard_map/ppermute | solution.py:224
  447.2 36.1 %collective-permute-start.32 = (bf16[256,2048]{1,0:T(8,128)(2,1)S(1)}, bf16[256,2048]{1,0:T(8,128)(2,1)S(1)}, u32[]{:S(2)}, u32[]{:S(2)}) collective-permute-start(bf16[256,2048]{1,0:T(8,128)(2,1)S(1)} %pad_maximum_fusion.6), channel_id=1, source_target_pairs={{0,4},{4,0},{1,5},{5,1},{2,6},{6,2},{3,7},{7,3},{8,12},{12,8},{9,1... | collective-permute-start | bytes 3145736 | tf_op jit(solution)/shard_map/ppermute | solution.py:224
  448.7 34.6 %collective-permute-start.31 = (bf16[128,2048]{1,0:T(8,128)(2,1)S(1)}, bf16[128,2048]{1,0:T(8,128)(2,1)S(1)}, u32[]{:S(2)}, u32[]{:S(2)}) collective-permute-start(bf16[128,2048]{1,0:T(8,128)(2,1)S(1)} %get-tuple-element.91), channel_id=1, source_target_pairs={{0,4},{4,0},{1,5},{5,1},{2,6},{6,2},{3,7},{7,3},{8,12},{12,8},{9,1... | collective-permute-start | bytes 1572872 | tf_op jit(solution)/shard_map/ppermute | solution.py:224
  572.2 57.2 %collective-permute-start.44 = (bf16[1024,2048]{1,0:T(8,128)(2,1)}, bf16[1024,2048]{1,0:T(8,128)(2,1)}, u32[]{:S(2)}, u32[]{:S(2)}) collective-permute-start(bf16[1024,2048]{1,0:T(8,128)(2,1)} %get-tuple-element.56), channel_id=1, source_target_pairs={{0,2},{2,0},{1,3},{3,1},{4,6},{6,4},{5,7},{7,5},{8,10},{10,8},{9,1... | collective-permute-start | bytes 12582920 | tf_op jit(solution)/shard_map/ppermute | solution.py:224
  583.4 58.5 %collective-permute-start.39 = (bf16[1024,2048]{1,0:T(8,128)(2,1)}, bf16[1024,2048]{1,0:T(8,128)(2,1)}, u32[]{:S(2)}, u32[]{:S(2)}) collective-permute-start(bf16[1024,2048]{1,0:T(8,128)(2,1)} %shard_map.213), channel_id=1, source_target_pairs={{0,2},{2,0},{1,3},{3,1},{4,6},{6,4},{5,7},{7,5},{8,10},{10,8},{9,1... | collective-permute-start | bytes 12582920 | tf_op jit(solution)/shard_map/ppermute | solution.py:224
  597.9 34.4 %all-to-all-start.3 = ((bf16[4,128,1536]{2,1,0:T(8,128)(2,1)}), bf16[4,128,1536]{2,1,0:T(8,128)(2,1)}, u32[]{:S(2)}, u32[]{:S(2)}) async-start(bf16[4,128,1536]{2,1,0:T(8,128)(2,1)} %bitcast.135), calls=%async_computation.5 | async-start | bytes 3145728 | tf_op jit(solution)/shard_map/all_to_all | solution.py:262
  602.2 160.3 %reduce-scatter.4.cloned.1.call-start = ((), (), s32[]{:S(2)}) async-start(), calls=%async_computation.11 | async-start | bytes 5242880 | tf_op jit(solution)/shard_map/reduce_scatter | solution.py:270
  638.9 26.3 %collective-permute-start.45 = (bf16[256,2048]{1,0:T(8,128)(2,1)}, bf16[256,2048]{1,0:T(8,128)(2,1)}, u32[]{:S(2)}, u32[]{:S(2)}) collective-permute-start(bf16[256,2048]{1,0:T(8,128)(2,1)} %pad_maximum_fusion.9), channel_id=1, source_target_pairs={{0,1},{1,0},{2,3},{3,2},{4,5},{5,4},{6,7},{7,6},{8,9},{9,8},{10,11... | collective-permute-start | bytes 3145736 | tf_op jit(solution)/shard_map/ppermute | solution.py:224
  645.0 42.3 %collective-permute-start.40 = (bf16[256,2048]{1,0:T(8,128)(2,1)}, bf16[256,2048]{1,0:T(8,128)(2,1)}, u32[]{:S(2)}, u32[]{:S(2)}) collective-permute-start(bf16[256,2048]{1,0:T(8,128)(2,1)} %pad_maximum_fusion.7), channel_id=1, source_target_pairs={{0,1},{1,0},{2,3},{3,2},{4,5},{5,4},{6,7},{7,6},{8,9},{9,8},{10,11... | collective-permute-start | bytes 3145736 | tf_op jit(solution)/shard_map/ppermute | solution.py:224
  668.1 37.4 %collective-permute-start.47 = (bf16[256,2048]{1,0:T(8,128)(2,1)S(1)}, bf16[256,2048]{1,0:T(8,128)(2,1)S(1)}, u32[]{:S(2)}, u32[]{:S(2)}) collective-permute-start(bf16[256,2048]{1,0:T(8,128)(2,1)S(1)} %pad_maximum_fusion.10), channel_id=1, source_target_pairs={{0,4},{4,0},{1,5},{5,1},{2,6},{6,2},{3,7},{7,3},{8,12},{12,8},{9,1... | collective-permute-start | bytes 3145736 | tf_op jit(solution)/shard_map/ppermute | solution.py:224
  670.2 35.3 %collective-permute-start.46 = (bf16[128,2048]{1,0:T(8,128)(2,1)S(1)}, bf16[128,2048]{1,0:T(8,128)(2,1)S(1)}, u32[]{:S(2)}, u32[]{:S(2)}) collective-permute-start(bf16[128,2048]{1,0:T(8,128)(2,1)S(1)} %get-tuple-element.77), channel_id=1, source_target_pairs={{0,4},{4,0},{1,5},{5,1},{2,6},{6,2},{3,7},{7,3},{8,12},{12,8},{9,1... | collective-permute-start | bytes 1572872 | tf_op jit(solution)/shard_map/ppermute | solution.py:224
  689.6 47.9 %collective-permute-start.42 = (bf16[256,2048]{1,0:T(8,128)(2,1)S(1)}, bf16[256,2048]{1,0:T(8,128)(2,1)S(1)}, u32[]{:S(2)}, u32[]{:S(2)}) collective-permute-start(bf16[256,2048]{1,0:T(8,128)(2,1)S(1)} %pad_maximum_fusion.8), channel_id=1, source_target_pairs={{0,4},{4,0},{1,5},{5,1},{2,6},{6,2},{3,7},{7,3},{8,12},{12,8},{9,1... | collective-permute-start | bytes 3145736 | tf_op jit(solution)/shard_map/ppermute | solution.py:224
  696.5 40.9 %collective-permute-start.41 = (bf16[128,2048]{1,0:T(8,128)(2,1)S(1)}, bf16[128,2048]{1,0:T(8,128)(2,1)S(1)}, u32[]{:S(2)}, u32[]{:S(2)}) collective-permute-start(bf16[128,2048]{1,0:T(8,128)(2,1)S(1)} %get-tuple-element.84), channel_id=1, source_target_pairs={{0,4},{4,0},{1,5},{5,1},{2,6},{6,2},{3,7},{7,3},{8,12},{12,8},{9,1... | collective-permute-start | bytes 1572872 | tf_op jit(solution)/shard_map/ppermute | solution.py:224
  707.7 33.7 %collective-permute-start.48 = (bf16[128,2048]{1,0:T(8,128)(2,1)S(1)}, bf16[128,2048]{1,0:T(8,128)(2,1)S(1)}, u32[]{:S(2)}, u32[]{:S(2)}) collective-permute-start(bf16[128,2048]{1,0:T(8,128)(2,1)S(1)} %get-tuple-element.76), channel_id=1, source_target_pairs={{0,1},{1,0},{2,3},{3,2},{4,5},{5,4},{6,7},{7,6},{8,9},{9,8},{10,11... | collective-permute-start | bytes 1572872 | tf_op jit(solution)/shard_map/ppermute | solution.py:224
  (59 other events, 803.8 us)
Sparse Core Ops, SparseCore 0:
  33.4 81.2 all-gather.3
  131.0 115.8 all-gather.5
  249.1 113.5 all-gather.7
  364.8 108.9 reduce-scatter.5
  506.2 108.0 reduce-scatter.7
  618.3 75.4 reduce-scatter.3

commit v4 on v3

--- a/solution.py
+++ b/solution.py
@@ -35,6 +35,10 @@
 
 def after(value, *earlier):
     return lax.optimization_barrier((value,) + earlier)[0]
+
+
+def together(*values):
+    return lax.optimization_barrier(values)
 
 
 def whole(array):
@@ -224,17 +228,20 @@
     return lax.ppermute(value, axis, [(0, 1), (1, 0)])
 
 
-def gather_plane(own):
+def gather_first(own):
     half = own.shape[0] // 2
-    from_x = swap(own, "tensor")
-    from_y = swap(own, "y")
-    chip = jnp.concatenate(
-        [own, from_x, from_y, swap(from_x[:half], "y"), swap(from_y[half:], "tensor")], axis=0
-    )
+    from_x, from_y = together(swap(own, "tensor"), swap(own, "y"))
+    return own, from_x, from_y, (from_x[:half], from_y[half:])
+
+
+def gather_last(state):
+    own, from_x, from_y, (top, bottom) = state
+    top, bottom = together(swap(top, "y"), swap(bottom, "tensor"))
+    chip = jnp.concatenate([own, from_x, from_y, top, bottom], axis=0)
     return chip, swap(chip, "c")
 
 
-def scatter_plane(mine, theirs):
+def scatter_first(mine, theirs):
     rows = mine.shape[0] // 4
     half = rows // 2
     other = swap(theirs, "c")
@@ -243,13 +250,30 @@
         first = (2 * dy + dx) * rows + bottom * half
         return mine[first : first + half].astype(f32) + other[first : first + half].astype(f32)
 
-    top_x = swap(jnp.concatenate([piece(0, 1, 0), piece(1, 1, 0)], axis=0).astype(low), "tensor")
-    bottom_y = swap(jnp.concatenate([piece(1, 0, 1), piece(1, 1, 1)], axis=0).astype(low), "y")
-    top_y = swap((piece(1, 0, 0) + top_x[half:].astype(f32)).astype(low), "y")
-    bottom_x = swap((piece(0, 1, 1) + bottom_y[half:].astype(f32)).astype(low), "tensor")
-    top = piece(0, 0, 0) + top_x[:half].astype(f32) + top_y.astype(f32)
-    bottom = piece(0, 0, 1) + bottom_y[:half].astype(f32) + bottom_x.astype(f32)
+    top_x = jnp.concatenate([piece(0, 1, 0), piece(1, 1, 0)], axis=0).astype(low)
+    bottom_y = jnp.concatenate([piece(1, 0, 1), piece(1, 1, 1)], axis=0).astype(low)
+    return piece, half, together(top_x, bottom_y)
+
+
+def scatter_second(state):
+    piece, half, (top_x, bottom_y) = state
+    top_x, bottom_y = together(swap(top_x, "tensor"), swap(bottom_y, "y"))
+    top_y = (piece(1, 0, 0) + top_x[half:].astype(f32)).astype(low)
+    bottom_x = (piece(0, 1, 1) + bottom_y[half:].astype(f32)).astype(low)
+    return piece, half, (top_x[:half], bottom_y[:half], top_y, bottom_x)
+
+
+def scatter_last(state):
+    piece, half, (top_x, bottom_y, top_y, bottom_x) = state
+    top_y, bottom_x = together(swap(top_y, "y"), swap(bottom_x, "tensor"))
+    top = piece(0, 0, 0) + top_x.astype(f32) + top_y.astype(f32)
+    bottom = piece(0, 0, 1) + bottom_y.astype(f32) + bottom_x.astype(f32)
     return jnp.concatenate([top, bottom], axis=0)
+
+
+def beside(state, *others):
+    sends, *others = together(state[-1], *others)
+    return (*state[:-1], sends), *others
 
 
 def to_columns(parts):
@@ -360,20 +384,16 @@
     ffn_parts = jnp.concatenate(
         [w[:, :, k * chunk : (k + 1) * chunk] for k in range(CHUNKS) for w in wide], axis=2
     )
-    ffn_block = to_columns(after(ffn_parts, attn_block))
-    ffn_weights = [
-        gather_line(ffn_block[:, 3 * k * chunk : 3 * (k + 1) * chunk]) for k in range(CHUNKS)
-    ]
-
-    gains = gather_gains(jnp.stack([gain_attn, gain_ffn]), place, level).astype(f32)
-    gain_first, gain_second = gains[0], gains[1]
+    ffn_block = to_columns(ffn_parts)
+
+    gains = gather_gains(jnp.stack([gain_attn, gain_ffn]), place, level)
+    seg = jnp.concatenate(
+        [segments] + [plane_flip(segments, dy, dc) for dc, dy in ((0, 1), (1, 0), (1, 1))], axis=0
+    )
+    gains, seg = together(gains, seg)
+    gain_first, gain_second = gains[0].astype(f32), gains[1].astype(f32)
     inputs = tokens.astype(f32)
     unit_one, scale_one = normalize(inputs)
-    rows_one = gather_plane((unit_one * gain_first).astype(low))
-    grad_rows = gather_plane(after(cotangent, rows_one[0]))
-    seg = jnp.concatenate(
-        [segments] + [plane_flip(segments, dy, dc) for dc, dy in ((0, 1), (1, 0), (1, 1))], axis=0
-    )
     places = lax.rem(jnp.arange(seq_len, dtype=jnp.int32) + side * (seq_len // 2), seq_len)
     seg = jnp.where(side == 0, seg, jnp.roll(seg, seq_len // 2, axis=1))
     same = seg[:, :, None] == seg[:, None, :]
@@ -386,13 +406,25 @@
     sine = jnp.concatenate([-sine, sine], axis=2)
     live = live.astype(low).reshape(2, -1, seq_len)
     sides = range(2)
+    state, live, cosine, sine, ffn_block = beside(
+        gather_first((unit_one * gain_first).astype(low)), live, cosine, sine, ffn_block
+    )
+    rows_one = gather_last(state)
+    ffn_weights = [
+        gather_line(ffn_block[:, 3 * k * chunk : 3 * (k + 1) * chunk]) for k in range(CHUNKS)
+    ]
+    grad_own, attn_weights = together(cotangent, attn_weights)
 
     qkv, mixed, parts = zip(
         *(attend(rows_one[i], attn_weights, cosine[i], sine[i], live[i]) for i in sides)
     )
-    middle = inputs + scatter_plane(*parts)
+    grad_state, parts = beside(gather_first(grad_own), parts)
+    middle = inputs + scatter_last(scatter_second(scatter_first(*parts)))
     unit_two, scale_two = normalize(middle)
-    rows_two = gather_plane((unit_two * gain_second).astype(low))
+    rows_two = gather_last(gather_first((unit_two * gain_second).astype(low)))
+    grad_state, rows_own = beside(grad_state, rows_two[0])
+    rows_two = (rows_own, rows_two[1])
+    grad_rows = gather_last(grad_state)
 
     both = [[None] * CHUNKS for _ in sides]
     hidden = [[None] * CHUNKS for _ in sides]
@@ -407,11 +439,18 @@
             [(rows_two[i], both[i][k]) for i in sides],
             [(grad_rows[i], hidden[i][k]) for i in sides],
         )
-        ffn_sums.append(to_rows(scatter_line(sums)))
-    grad_normed_two = scatter_plane(*grad_parts)
+        if k == CHUNKS - 1:
+            grad_state, sums = beside(scatter_second(scatter_first(*grad_parts)), sums)
+        ffn_sums.append(scatter_line(sums))
+    grad_normed_two = scatter_last(grad_state)
     grad_unit_two, gain_two_part = norm_back(grad_normed_two, unit_two, scale_two, gain_second)
     grad_middle = cotangent.astype(f32) + grad_unit_two
-    grad_branch = gather_plane(after(grad_middle.astype(low), sums))
+    grad_branch = gather_first(grad_middle.astype(low))
+    out_parts = [project(hidden[i], ffn_weights, 2 * chunk) for i in sides]
+    grad_branch, out_parts = beside(grad_branch, out_parts)
+    grad_branch = gather_last(grad_branch)
+    out_state, grad_own = beside(scatter_first(*out_parts), grad_branch[0])
+    grad_branch = (grad_own, grad_branch[1])
 
     grads, parts = zip(
         *(
@@ -419,24 +458,24 @@
             for i in sides
         )
     )
-    attn_sums = to_rows(
-        scatter_line(
-            outer(
-                [(rows_one[i], grads[i]) for i in sides],
-                [(grad_branch[i], mixed[i]) for i in sides],
-            )
-        )
-    )
-    grad_normed_one = scatter_plane(*parts)
+    ffn_rows = [to_rows(ffn_sums[0])]
+    out_state, grads, ffn_rows = beside(scatter_second(out_state), grads, ffn_rows)
+    sums = outer(
+        [(rows_one[i], grads[i]) for i in sides],
+        [(grad_branch[i], mixed[i]) for i in sides],
+    )
+    sums, out_sums = together(sums, scatter_last(out_state))
+    attn_sums = to_rows(scatter_line(sums))
+    output = (middle + out_sums).astype(low)
+    grad_normed_one = scatter_last(scatter_second(scatter_first(*parts)))
+    ffn_rows += [to_rows(s) for s in ffn_sums[1:]]
     grad_unit_one, gain_one_part = norm_back(grad_normed_one, unit_one, scale_one, gain_first)
     grad_tokens = grad_middle + grad_unit_one
-    out_parts = [project(after(hidden[i], grad_branch[1]), ffn_weights, 2 * chunk) for i in sides]
-    output = (middle + scatter_plane(*out_parts)).astype(low)
     gain_sums = scatter_gains(jnp.stack([gain_one_part, gain_two_part]), place, level)
 
     attn_grads = [shard_of(attn_sums[:, :, k * width : (k + 1) * width]) for k in range(4)]
     ffn_grads = [
-        shard_of(jnp.concatenate([s[:, :, k * chunk : (k + 1) * chunk] for s in ffn_sums], axis=2))
+        shard_of(jnp.concatenate([s[:, :, k * chunk : (k + 1) * chunk] for s in ffn_rows], axis=2))
         for k in range(3)
     ]
     return (output, grad_tokens, gain_sums[0], gain_sums[1], *attn_grads, *ffn_grads)

time: 800 us -> 700 us (0.88)
  waiting for transfers between devices: 376 us -> 263 us
  local copies, waits for them, and re-layouts: 48.7 us -> 66.9 us
  other arithmetic: 65.7 us -> 57.5 us
    ppermute x47, waiting for transfers between devices: 342 us -> 189 us  [swap(): return lax.ppermute(value, axis, [(0, 1), (1, 0)])]
    all_gather x3, waiting for transfers between devices: 6.34 us -> 51 us  [gather_line(): return lax.all_gather(block, 'z', axis=0, tiled=True)]
    slice x10 -> x12, local copies, waits for them, and re-layouts: 3.88 us -> 13.3 us  [the longest x4 7.56 us: scatter_second(): return (piece, half, (top_x[:half], bottom_y[:half], top_y, bottom_x))]
    add x8 -> x4, other arithmetic: 16.7 us -> 9.92 us  [scatter_last(): top = piece(0, 0, 0) + top_x.astype(f32) + top_y.astype(f32)]
    unnamed x67 -> x82, local copies, waits for them, and re-layouts: 21.4 us -> 24 us
  transfers between devices with their start and end apart: 67 -> 67, of which waited for: 32 -> 32; matrix products, arithmetic and copies ran while one was open for 13% -> 17% of each run, Pallas kernels for 26% -> 31%
where the time goes in v4:
time: 700 us; the launch traced here: 691 us
  waiting for transfers between devices  263 us (38%)
  Pallas kernels  213 us (30%)
  starting transfers between devices  75.8 us (11%)
  local copies, waits for them, and re-layouts  66.9 us (10%)
  other arithmetic  57.5 us (8%)
  between operations  15.5 us (2%)
    ppermute x47, waiting for transfers between devices, swap(): return lax.ppermute(value, axis, [(0, 1), (1, 0)])  189 us
    pallas_call x3, Pallas kernels, outer(): pl.pallas_call(functools.partial(outer_kernel, [len(group) for group in g...  55 us
    pallas_call x4, Pallas kernels, project(): pl.pallas_call(functools.partial(project_kernel, first, len(acts)), grid=...  54.4 us
    all_gather x3, waiting for transfers between devices, gather_line(): return lax.all_gather(block, 'z', axis=0, tiled=True)  51 us
    pallas_call x4, Pallas kernels, gated(): pl.pallas_call(functools.partial(gated_kernel, units), grid=(total // til...  49.2 us
    ppermute x47, starting transfers between devices, swap(): return lax.ppermute(value, axis, [(0, 1), (1, 0)])  42.6 us
    pallas_call x2, Pallas kernels, attend_back(): pl.pallas_call(functools.partial(attend_back_kernel, width), grid=(total...  28.6 us
    pallas_call x2, Pallas kernels, attend(): pl.pallas_call(functools.partial(attend_kernel, width), grid=(total // se...  25.4 us
  transfers between devices with their start and end apart: 67, of which 32 were waited for; matrix products, arithmetic and copies ran while one was open for 17% of the time, Pallas kernels for 31%

profile of v4, /device:TPU:0, one launch (start us, length us, event | category | flops | bytes accessed | tf_op | source)
XLA Modules:
  0.0 691.1 jit_solution(14361012714029105957)
XLA Ops:
  35.2 4.6 all-to-all-start.1
  54.8 13.4 %collective-permute-done.11 = bf16[256,2048]{1,0:T(8,128)(2,1)} collective-permute-done((bf16[256,2048]{1,0:T(8,128)(2,1)}, bf16[256,2048]{1,0:T(8,128)(2,1)}, u32[]{:S(2)}, u32[]{:S(2)}) %collective-permute-start.11) | collective-permute-done | bytes 1048608 | tf_op jit(solution)/shard_map/ppermute | solution.py:228
  68.3 31.0 %collective-permute-done.12 = bf16[256,2048]{1,0:T(8,128)(2,1)} collective-permute-done((bf16[256,2048]{1,0:T(8,128)(2,1)}, bf16[256,2048]{1,0:T(8,128)(2,1)}, u32[]{:S(2)}, u32[]{:S(2)}) %collective-permute-start.12) | collective-permute-done | bytes 1048608 | tf_op jit(solution)/shard_map/ppermute | solution.py:228
  109.9 6.8 collective-permute-done.13
  132.0 13.1 %shard_map.203 = (bf16[1024,768]{1,0:T(8,128)(2,1)}, bf16[1024,256]{1,0:T(8,128)(2,1)}, bf16[1024,2048]{1,0:T(8,128)(2,1)}) custom-call(bf16[1024,2048]{1,0:T(8,128)(2,1)} %constant_dynamic-update-slice_fusion.rows_ref.refs_0_, bf16[2048,1024]{1,0:T(8,128)(2,1)} %all-gather.4.cloned.1.call-done.w_ref, f32[1024,128]{1,0:T(8,128)} %get-tuple-element.267.cos_ref, ...), custom_call_target="tpu_custom_call" | custom-call | flops 4831838208 | bytes 14680064 | tf_op jit(solution)/shard_map/pallas_call | solution.py:84
  145.1 12.4 %shard_map.204 = (bf16[1024,768]{1,0:T(8,128)(2,1)}, bf16[1024,256]{1,0:T(8,128)(2,1)}, bf16[1024,2048]{1,0:T(8,128)(2,1)}) custom-call(bf16[1024,2048]{1,0:T(8,128)(2,1)} %collective-permute-done.15.rows_ref.refs_2_, bf16[2048,1024]{1,0:T(8,128)(2,1)} %all-gather.4.cloned.1.call-done.w_ref, f32[1024,128]{1,0:T(8,128)} %get-tuple-element.266.cos_ref, ...), custom_call_target="tpu_custom_call" | custom-call | flops 4831838208 | bytes 14680064 | tf_op jit(solution)/shard_map/pallas_call | solution.py:84
  159.3 7.4 %collective-permute-done.16 = bf16[1024,2048]{1,0:T(8,128)(2,1)S(1)} collective-permute-done((bf16[1024,2048]{1,0:T(8,128)(2,1)}, bf16[1024,2048]{1,0:T(8,128)(2,1)S(1)}, u32[]{:S(2)}, u32[]{:S(2)}) %collective-permute-start.16) | collective-permute-done | bytes 4194336 | tf_op jit(solution)/shard_map/ppermute | solution.py:228
  168.0 24.9 %collective-permute-done.17 = bf16[256,2048]{1,0:T(8,128)(2,1)S(1)} collective-permute-done((bf16[256,2048]{1,0:T(8,128)(2,1)S(1)}, bf16[256,2048]{1,0:T(8,128)(2,1)S(1)}, u32[]{:S(2)}, u32[]{:S(2)}) %collective-permute-start.17) | collective-permute-done | bytes 1048608 | tf_op jit(solution)/shard_map/ppermute | solution.py:228
  197.0 11.1 %collective-permute-done.19 = bf16[128,2048]{1,0:T(8,128)(2,1)} collective-permute-done((bf16[128,2048]{1,0:T(8,128)(2,1)}, bf16[128,2048]{1,0:T(8,128)(2,1)}, u32[]{:S(2)}, u32[]{:S(2)}) %collective-permute-start.19) | collective-permute-done | bytes 524320 | tf_op jit(solution)/shard_map/ppermute | solution.py:228
  215.5 20.5 %collective-permute-done.21 = bf16[256,2048]{1,0:T(8,128)(2,1)S(1)} collective-permute-done((bf16[256,2048]{1,0:T(8,128)(2,1)S(1)}, bf16[256,2048]{1,0:T(8,128)(2,1)S(1)}, u32[]{:S(2)}, u32[]{:S(2)}) %collective-permute-start.21) | collective-permute-done | bytes 1048608 | tf_op jit(solution)/shard_map/ppermute | solution.py:228
  241.6 6.3 collective-permute-done.23
  262.3 12.3 %shard_map.205 = (bf16[1024,1024]{1,0:T(8,128)(2,1)}, bf16[1024,512]{1,0:T(8,128)(2,1)}) custom-call(bf16[1024,2048]{1,0:T(8,128)(2,1)} %constant_dynamic-update-slice_fusion.5.rows_ref.refs_0_, bf16[1024,2048]{1,0:T(8,128)(2,1)} %constant_dynamic-update-slice_fusion.10.grad_ref.refs_4_, bf16[2048,1536]{1,0:T(8,128)(2,1)} %all-gather.6.cloned.1.call-done.w_ref.refs_2_), custom_call_target="tpu_custom_call" | custom-call | flops 6442450944 | bytes 17825792 | tf_op jit(solution)/shard_map/pallas_call | solution.py:157
  274.6 12.4 %shard_map.208 = (bf16[1024,1024]{1,0:T(8,128)(2,1)}, bf16[1024,512]{1,0:T(8,128)(2,1)}) custom-call(bf16[1024,2048]{1,0:T(8,128)(2,1)} %collective-permute-done.27.rows_ref.refs_2_, bf16[1024,2048]{1,0:T(8,128)(2,1)} %collective-permute-done.28.grad_ref.refs_6_, bf16[2048,1536]{1,0:T(8,128)(2,1)} %all-gather.6.cloned.1.call-done.w_ref.refs_2_), custom_call_target="tpu_custom_call" | custom-call | flops 6442450944 | bytes 17825792 | tf_op jit(solution)/shard_map/pallas_call | solution.py:157
  286.9 19.3 %shard_map.216 = bf16[2048,1536]{1,0:T(8,128)(2,1)} custom-call(bf16[1024,2048]{1,0:T(8,128)(2,1)} %constant_dynamic-update-slice_fusion.5.rows_ref.refs_0_, bf16[1024,1024]{1,0:T(8,128)(2,1)} %get-tuple-element.144.refs_0_.refs_1_, bf16[1024,2048]{1,0:T(8,128)(2,1)} %collective-permute-done.27.rows_ref.refs_2_, ...), custom_call_target="tpu_custom_call" | custom-call | flops 12884901888 | bytes 29360128 | tf_op jit(solution)/shard_map/pallas_call | solution.py:216
  306.5 51.0 %all-gather.8.cloned.1.call-done.w_ref.refs_3_ = bf16[2048,1536]{1,0:T(8,128)(2,1)} async-done(((bf16[512,1536]{1,0:T(8,128)(2,1)}), bf16[2048,1536]{1,0:T(8,128)(2,1)}) %all-gather.8.cloned.1.call-update) | async-done | bytes 6291472 | tf_op jit(solution)/shard_map/all_gather | solution.py:290
  357.5 12.3 %shard_map.209 = (bf16[1024,1024]{1,0:T(8,128)(2,1)}, bf16[1024,512]{1,0:T(8,128)(2,1)}) custom-call(bf16[1024,2048]{1,0:T(8,128)(2,1)} %collective-permute-done.27.rows_ref.refs_2_, bf16[1024,2048]{1,0:T(8,128)(2,1)} %collective-permute-done.28.grad_ref.refs_6_, bf16[2048,1536]{1,0:T(8,128)(2,1)} %all-gather.8.cloned.1.call-done.w_ref.refs_3_), custom_call_target="tpu_custom_call" | custom-call | flops 6442450944 | bytes 17825792 | tf_op jit(solution)/shard_map/pallas_call | solution.py:157
  369.8 15.5 %shard_map.210 = bf16[1024,2048]{1,0:T(8,128)(2,1)} custom-call(bf16[1024,1024]{1,0:T(8,128)(2,1)} %get-tuple-element.146.refs_0_.refs_3_, bf16[1024,1024]{1,0:T(8,128)(2,1)} %get-tuple-element.147.refs_1_.refs_3_, bf16[2048,1536]{1,0:T(8,128)(2,1)} %all-gather.6.cloned.1.call-done.w_ref.refs_2_, bf16[2048,1536]{1,0:T(8,128)(2,1)} %all-gather.8.cloned.1.call-done.w_ref.refs_3_), custom_call_target="tpu_custom_call" | custom-call | flops 8589934592 | bytes 20971520 | tf_op jit(solution)/shard_map/pallas_call | solution.py:180
  385.3 12.3 %shard_map.206 = (bf16[1024,1024]{1,0:T(8,128)(2,1)}, bf16[1024,512]{1,0:T(8,128)(2,1)}) custom-call(bf16[1024,2048]{1,0:T(8,128)(2,1)} %constant_dynamic-update-slice_fusion.5.rows_ref.refs_0_, bf16[1024,2048]{1,0:T(8,128)(2,1)} %constant_dynamic-update-slice_fusion.10.grad_ref.refs_4_, bf16[2048,1536]{1,0:T(8,128)(2,1)} %all-gather.8.cloned.1.call-done.w_ref.refs_3_), custom_call_target="tpu_custom_call" | custom-call | flops 6442450944 | bytes 17825792 | tf_op jit(solution)/shard_map/pallas_call | solution.py:157
  397.5 15.5 %shard_map.207 = bf16[1024,2048]{1,0:T(8,128)(2,1)} custom-call(bf16[1024,1024]{1,0:T(8,128)(2,1)} %get-tuple-element.144.refs_0_.refs_1_, bf16[1024,1024]{1,0:T(8,128)(2,1)} %get-tuple-element.145.refs_1_, bf16[2048,1536]{1,0:T(8,128)(2,1)} %all-gather.6.cloned.1.call-done.w_ref.refs_2_, bf16[2048,1536]{1,0:T(8,128)(2,1)} %all-gather.8.cloned.1.call-done.w_ref.refs_3_), custom_call_target="tpu_custom_call" | custom-call | flops 8589934592 | bytes 20971520 | tf_op jit(solution)/shard_map/pallas_call | solution.py:180
  422.0 19.7 %shard_map.211 = bf16[2048,1536]{1,0:T(8,128)(2,1)} custom-call(bf16[1024,2048]{1,0:T(8,128)(2,1)} %constant_dynamic-update-slice_fusion.5.rows_ref.refs_0_, bf16[1024,1024]{1,0:T(8,128)(2,1)} %get-tuple-element.145.refs_1_, bf16[1024,2048]{1,0:T(8,128)(2,1)} %collective-permute-done.27.rows_ref.refs_2_, ...), custom_call_target="tpu_custom_call" | custom-call | flops 12884901888 | bytes 29360128 | tf_op jit(solution)/shard_map/pallas_call | solution.py:216
  455.3 11.4 %collective-permute-done.32 = bf16[128,2048]{1,0:T(8,128)(2,1)S(1)} collective-permute-done((bf16[128,2048]{1,0:T(8,128)(2,1)}, bf16[128,2048]{1,0:T(8,128)(2,1)S(1)}, u32[]{:S(2)}, u32[]{:S(2)}) %collective-permute-start.32) | collective-permute-done | bytes 524320 | tf_op jit(solution)/shard_map/ppermute | solution.py:228
  475.1 12.2 %shard_map.212 = bf16[1024,2048]{1,0:T(8,128)(2,1)} custom-call(bf16[1024,512]{1,0:T(8,128)(2,1)} %get-tuple-element.162.refs_0_.refs_5_, bf16[1024,512]{1,0:T(8,128)(2,1)} %get-tuple-element.152.refs_5_.refs_1_, bf16[2048,1536]{1,0:T(8,128)(2,1)} %all-gather.6.cloned.1.call-done.w_ref.refs_2_, bf16[2048,1536]{1,0:T(8,128)(2,1)} %all-gather.8.cloned.1.call-done.w_ref.refs_3_), custom_call_target="tpu_custom_call" | custom-call | flops 4294967296 | bytes 18874368 | tf_op jit(solution)/shard_map/pallas_call | solution.py:180
  487.4 11.3 %shard_map.213 = bf16[1024,2048]{1,0:T(8,128)(2,1)} custom-call(bf16[1024,512]{1,0:T(8,128)(2,1)} %get-tuple-element.163.refs_0_.refs_7_, bf16[1024,512]{1,0:T(8,128)(2,1)} %get-tuple-element.153.refs_7_.refs_1_, bf16[2048,1536]{1,0:T(8,128)(2,1)} %all-gather.6.cloned.1.call-done.w_ref.refs_2_, bf16[2048,1536]{1,0:T(8,128)(2,1)} %all-gather.8.cloned.1.call-done.w_ref.refs_3_), custom_call_target="tpu_custom_call" | custom-call | flops 4294967296 | bytes 18874368 | tf_op jit(solution)/shard_map/pallas_call | solution.py:180
  504.0 9.2 %collective-permute-done.37 = bf16[128,2048]{1,0:T(8,128)(2,1)S(1)} collective-permute-done((bf16[128,2048]{1,0:T(8,128)(2,1)S(1)}, bf16[128,2048]{1,0:T(8,128)(2,1)S(1)}, u32[]{:S(2)}, u32[]{:S(2)}) %collective-permute-start.37) | collective-permute-done | bytes 524320 | tf_op jit(solution)/shard_map/ppermute | solution.py:228
  522.4 4.4 all-to-all-start.2
  526.8 14.5 %shard_map.215 = (bf16[1024,768]{1,0:T(8,128)(2,1)}, bf16[1024,2048]{1,0:T(8,128)(2,1)}) custom-call(bf16[1024,2048]{1,0:T(8,128)(2,1)} %collective-permute-done.41.grad_ref.refs_6_, bf16[2048,1024]{1,0:T(8,128)(2,1)} %all-gather.4.cloned.1.call-done.w_ref, bf16[1024,768]{1,0:T(8,128)(2,1)} %get-tuple-element.179.qkv_ref, ...), custom_call_target="tpu_custom_call" | custom-call | flops 5637144576 | bytes 15728640 | tf_op jit(solution)/shard_map/pallas_call | solution.py:119
  541.7 14.1 %shard_map.214 = (bf16[1024,768]{1,0:T(8,128)(2,1)}, bf16[1024,2048]{1,0:T(8,128)(2,1)}) custom-call(bf16[1024,2048]{1,0:T(8,128)(2,1)} %constant_dynamic-update-slice_fusion.15.grad_ref.refs_4_, bf16[2048,1024]{1,0:T(8,128)(2,1)} %all-gather.4.cloned.1.call-done.w_ref, bf16[1024,768]{1,0:T(8,128)(2,1)} %get-tuple-element.177.qkv_ref, ...), custom_call_target="tpu_custom_call" | custom-call | flops 5637144576 | bytes 15728640 | tf_op jit(solution)/shard_map/pallas_call | solution.py:119
  565.4 16.0 %shard_map.217 = bf16[2048,1024]{1,0:T(8,128)(2,1)} custom-call(bf16[1024,2048]{1,0:T(8,128)(2,1)} %constant_dynamic-update-slice_fusion.rows_ref.refs_0_, bf16[1024,768]{1,0:T(8,128)(2,1)} %get-tuple-element.181.refs_1_, bf16[1024,2048]{1,0:T(8,128)(2,1)} %collective-permute-done.15.rows_ref.refs_2_, bf16[1024,768]{1,0:T(8,128)(2,1)} %get-tuple-element.182.refs_3_, ...), custom_call_target="tpu_custom_call" | custom-call | flops 8589934592 | bytes 25165824 | tf_op jit(solution)/shard_map/pallas_call | solution.py:216
  592.0 21.7 %collective-permute-done.45 = bf16[256,2048]{1,0:T(8,128)(2,1)S(1)} collective-permute-done((bf16[256,2048]{1,0:T(8,128)(2,1)S(1)}, bf16[256,2048]{1,0:T(8,128)(2,1)S(1)}, u32[]{:S(2)}, u32[]{:S(2)}) %collective-permute-start.45) | collective-permute-done | bytes 1048608 | tf_op jit(solution)/shard_map/ppermute | solution.py:228
  620.7 8.3 %collective-permute-done.47 = bf16[128,2048]{1,0:T(8,128)(2,1)S(1)} collective-permute-done((bf16[128,2048]{1,0:T(8,128)(2,1)S(1)}, bf16[128,2048]{1,0:T(8,128)(2,1)S(1)}, u32[]{:S(2)}, u32[]{:S(2)}) %collective-permute-start.47) | collective-permute-done | bytes 524320 | tf_op jit(solution)/shard_map/ppermute | solution.py:228
  649.4 12.7 %all-to-all-done.4 = bf16[4,128,1536]{2,1,0:T(8,128)(2,1)} async-done(((bf16[4,128,1536]{2,1,0:T(8,128)(2,1)}), bf16[4,128,1536]{2,1,0:T(8,128)(2,1)}, u32[]{:S(2)}, u32[]{:S(2)}) %all-to-all-start.4) | async-done | bytes 1572896 | tf_op jit(solution)/shard_map/all_to_all | solution.py:286
  672.9 7.2 %all-to-all-done.3 = bf16[4,128,1024]{2,1,0:T(8,128)(2,1)S(1)} async-done(((bf16[4,128,1024]{2,1,0:T(8,128)(2,1)}), bf16[4,128,1024]{2,1,0:T(8,128)(2,1)S(1)}, u32[]{:S(2)}, u32[]{:S(2)}) %all-to-all-start.3) | async-done | bytes 1048608 | tf_op jit(solution)/shard_map/all_to_all | solution.py:286
  (313 shorter events, 211.1 us)
Async XLA Ops:
  7.9 18.5 %collective-permute-start.2 = (bf16[2,128]{1,0:T(2,128)(2,1)S(1)}, bf16[2,128]{1,0:T(2,128)(2,1)S(1)}, u32[]{:S(2)}, u32[]{:S(2)}) collective-permute-start(bf16[2,128]{1,0:T(2,128)(2,1)S(1)} %get-tuple-element.217), channel_id=1, source_target_pairs={{0,2},{2,0},{1,3},{3,1},{4,6},{6,4},{5,7},{7,5},{8,10},{10,8},{9,1... | collective-permute-start | bytes 1544 | tf_op jit(solution)/shard_map/ppermute | solution.py:228
  11.1 20.5 %collective-permute-start.10 = (s32[1,512]{1,0:T(1,128)}, s32[1,512]{1,0:T(1,128)S(1)}, u32[]{:S(2)}, u32[]{:S(2)}) collective-permute-start(s32[1,512]{1,0:T(1,128)} %param.13), channel_id=1, source_target_pairs={{0,6},{2,4},{4,2},{6,0},{1,7},{3,5},{5,3},{7,1},{8,14},{10,12},{12... | collective-permute-start | bytes 6152 | tf_op jit(solution)/shard_map/ppermute | solution.py:312
  12.7 20.2 %collective-permute-start.8 = (s32[1,512]{1,0:T(1,128)}, s32[1,512]{1,0:T(1,128)S(1)}, u32[]{:S(2)}, u32[]{:S(2)}) collective-permute-start(s32[1,512]{1,0:T(1,128)} %param.13), channel_id=1, source_target_pairs={{0,4},{4,0},{1,5},{5,1},{2,6},{6,2},{3,7},{7,3},{8,12},{12,8},{9,1... | collective-permute-start | bytes 6152 | tf_op jit(solution)/shard_map/ppermute | solution.py:228
  35.2 67.9 %all-to-all-start.1 = ((bf16[4,128,3072]{2,1,0:T(8,128)(2,1)}), bf16[4,128,3072]{2,1,0:T(8,128)(2,1)}, u32[]{:S(2)}, u32[]{:S(2)}) async-start(bf16[4,128,3072]{2,1,0:T(8,128)(2,1)} %slice_dynamic-update-slice_fusion), calls=%async_computation.1 | async-start | bytes 6291456 | tf_op jit(solution)/shard_map/all_to_all | solution.py:280
  39.8 86.8 %all-gather.4.cloned.1.call-start = ((), (), s32[]{:S(2)}) async-start(), calls=%async_computation.8 | async-start | bytes 5242880 | tf_op jit(solution)/shard_map/all_gather | solution.py:290
  40.5 221.7 %all-gather.6.cloned.1.call-start = ((), (), s32[]{:S(2)}) async-start(), calls=%async_computation.9 | async-start | bytes 7864320 | tf_op jit(solution)/shard_map/all_gather | solution.py:290
  42.3 26.0 %collective-permute-start.11 = (bf16[256,2048]{1,0:T(8,128)(2,1)}, bf16[256,2048]{1,0:T(8,128)(2,1)}, u32[]{:S(2)}, u32[]{:S(2)}) collective-permute-start(bf16[256,2048]{1,0:T(8,128)(2,1)} %get-tuple-element.215), channel_id=1, source_target_pairs={{0,1},{1,0},{2,3},{3,2},{4,5},{5,4},{6,7},{7,6},{8,9},{9,8},{10,11... | collective-permute-start | bytes 3145736 | tf_op jit(solution)/shard_map/ppermute | solution.py:228
  44.2 55.1 %collective-permute-start.12 = (bf16[256,2048]{1,0:T(8,128)(2,1)}, bf16[256,2048]{1,0:T(8,128)(2,1)}, u32[]{:S(2)}, u32[]{:S(2)}) collective-permute-start(bf16[256,2048]{1,0:T(8,128)(2,1)} %get-tuple-element.215), channel_id=1, source_target_pairs={{0,4},{4,0},{1,5},{5,1},{2,6},{6,2},{3,7},{7,3},{8,12},{12,8},{9,1... | collective-permute-start | bytes 3145736 | tf_op jit(solution)/shard_map/ppermute | solution.py:228
  118.8 26.2 %collective-permute-start.15 = (bf16[1024,2048]{1,0:T(8,128)(2,1)}, bf16[1024,2048]{1,0:T(8,128)(2,1)}, u32[]{:S(2)}, u32[]{:S(2)}) collective-permute-start(bf16[1024,2048]{1,0:T(8,128)(2,1)} %constant_dynamic-update-slice_fusion.rows_ref.refs_0_), channel_id=1, source_target_pairs={{0,2},{2,0},{1,3},{3,1},{4,6},{6,4},{5,7},{7,5},{8,10},{10,8},{9,1... | collective-permute-start | bytes 12582920 | tf_op jit(solution)/shard_map/ppermute | solution.py:228
  122.6 234.9 %all-gather.8.cloned.1.call-start = ((), (), s32[]{:S(2)}) async-start(), calls=%async_computation.10 | async-start | bytes 7864320 | tf_op jit(solution)/shard_map/all_gather | solution.py:290
  126.6 30.8 %collective-permute-start = (bf16[256,2048]{1,0:T(8,128)(2,1)}, bf16[256,2048]{1,0:T(8,128)(2,1)S(1)}, u32[]{:S(2)}, u32[]{:S(2)}) collective-permute-start(bf16[256,2048]{1,0:T(8,128)(2,1)} %param.23), channel_id=1, source_target_pairs={{0,1},{1,0},{2,3},{3,2},{4,5},{5,4},{6,7},{7,6},{8,9},{9,8},{10,11... | collective-permute-start | bytes 3145736 | tf_op jit(solution)/shard_map/ppermute | solution.py:228
  128.3 29.1 %collective-permute-start.1 = (bf16[256,2048]{1,0:T(8,128)(2,1)}, bf16[256,2048]{1,0:T(8,128)(2,1)S(1)}, u32[]{:S(2)}, u32[]{:S(2)}) collective-permute-start(bf16[256,2048]{1,0:T(8,128)(2,1)} %param.23), channel_id=1, source_target_pairs={{0,4},{4,0},{1,5},{5,1},{2,6},{6,2},{3,7},{7,3},{8,12},{12,8},{9,1... | collective-permute-start | bytes 3145736 | tf_op jit(solution)/shard_map/ppermute | solution.py:228
  167.7 25.3 %collective-permute-start.17 = (bf16[256,2048]{1,0:T(8,128)(2,1)S(1)}, bf16[256,2048]{1,0:T(8,128)(2,1)S(1)}, u32[]{:S(2)}, u32[]{:S(2)}) collective-permute-start(bf16[256,2048]{1,0:T(8,128)(2,1)S(1)} %pad_maximum_fusion.6), channel_id=1, source_target_pairs={{0,1},{1,0},{2,3},{3,2},{4,5},{5,4},{6,7},{7,6},{8,9},{9,8},{10,11... | collective-permute-start | bytes 3145736 | tf_op jit(solution)/shard_map/ppermute | solution.py:228
  167.7 25.3 %collective-permute-start.18 = (bf16[256,2048]{1,0:T(8,128)(2,1)S(1)}, bf16[256,2048]{1,0:T(8,128)(2,1)S(1)}, u32[]{:S(2)}, u32[]{:S(2)}) collective-permute-start(bf16[256,2048]{1,0:T(8,128)(2,1)S(1)} %pad_maximum_fusion.7), channel_id=1, source_target_pairs={{0,4},{4,0},{1,5},{5,1},{2,6},{6,2},{3,7},{7,3},{8,12},{12,8},{9,1... | collective-permute-start | bytes 3145736 | tf_op jit(solution)/shard_map/ppermute | solution.py:228
  196.5 325.9 %reduce-scatter.4.cloned.1.call-start = ((), (), s32[]{:S(2)}) async-start(), calls=%async_computation.11 | async-start | bytes 7864320 | tf_op jit(solution)/shard_map/reduce_scatter | solution.py:294
  212.5 23.5 %collective-permute-start.21 = (bf16[256,2048]{1,0:T(8,128)(2,1)S(1)}, bf16[256,2048]{1,0:T(8,128)(2,1)S(1)}, u32[]{:S(2)}, u32[]{:S(2)}) collective-permute-start(bf16[256,2048]{1,0:T(8,128)(2,1)S(1)} %get-tuple-element.211), channel_id=1, source_target_pairs={{0,1},{1,0},{2,3},{3,2},{4,5},{5,4},{6,7},{7,6},{8,9},{9,8},{10,11... | collective-permute-start | bytes 3145736 | tf_op jit(solution)/shard_map/ppermute | solution.py:228
  213.8 23.1 %collective-permute-start.22 = (bf16[256,2048]{1,0:T(8,128)(2,1)S(1)}, bf16[256,2048]{1,0:T(8,128)(2,1)S(1)}, u32[]{:S(2)}, u32[]{:S(2)}) collective-permute-start(bf16[256,2048]{1,0:T(8,128)(2,1)S(1)} %get-tuple-element.211), channel_id=1, source_target_pairs={{0,4},{4,0},{1,5},{5,1},{2,6},{6,2},{3,7},{7,3},{8,12},{12,8},{9,1... | collective-permute-start | bytes 3145736 | tf_op jit(solution)/shard_map/ppermute | solution.py:228
  255.6 18.9 %collective-permute-start.27 = (bf16[1024,2048]{1,0:T(8,128)(2,1)}, bf16[1024,2048]{1,0:T(8,128)(2,1)}, u32[]{:S(2)}, u32[]{:S(2)}) collective-permute-start(bf16[1024,2048]{1,0:T(8,128)(2,1)} %constant_dynamic-update-slice_fusion.5.rows_ref.refs_0_), channel_id=1, source_target_pairs={{0,2},{2,0},{1,3},{3,1},{4,6},{6,4},{5,7},{7,5},{8,10},{10,8},{9,1... | collective-permute-start | bytes 12582920 | tf_op jit(solution)/shard_map/ppermute | solution.py:228
  306.3 331.3 %reduce-scatter.8.cloned.1.call-start = ((), (), s32[]{:S(2)}) async-start(), calls=%async_computation.13 | async-start | bytes 7864320 | tf_op jit(solution)/shard_map/reduce_scatter | solution.py:294
  385.2 27.8 %collective-permute-start.29 = (bf16[1024,2048]{1,0:T(8,128)(2,1)}, bf16[1024,2048]{1,0:T(8,128)(2,1)S(1)}, u32[]{:S(2)}, u32[]{:S(2)}) collective-permute-start(bf16[1024,2048]{1,0:T(8,128)(2,1)} %shard_map.210), channel_id=1, source_target_pairs={{0,2},{2,0},{1,3},{3,1},{4,6},{6,4},{5,7},{7,5},{8,10},{10,8},{9,1... | collective-permute-start | bytes 12582920 | tf_op jit(solution)/shard_map/ppermute | solution.py:228
  419.0 25.8 %collective-permute-start.30 = (bf16[256,2048]{1,0:T(8,128)(2,1)}, bf16[256,2048]{1,0:T(8,128)(2,1)}, u32[]{:S(2)}, u32[]{:S(2)}) collective-permute-start(bf16[256,2048]{1,0:T(8,128)(2,1)} %pad_maximum_fusion.8), channel_id=1, source_target_pairs={{0,1},{1,0},{2,3},{3,2},{4,5},{5,4},{6,7},{7,6},{8,9},{9,8},{10,11... | collective-permute-start | bytes 3145736 | tf_op jit(solution)/shard_map/ppermute | solution.py:228
  420.5 25.6 %collective-permute-start.31 = (bf16[256,2048]{1,0:T(8,128)(2,1)}, bf16[256,2048]{1,0:T(8,128)(2,1)}, u32[]{:S(2)}, u32[]{:S(2)}) collective-permute-start(bf16[256,2048]{1,0:T(8,128)(2,1)} %pad_maximum_fusion.9), channel_id=1, source_target_pairs={{0,4},{4,0},{1,5},{5,1},{2,6},{6,2},{3,7},{7,3},{8,12},{12,8},{9,1... | collective-permute-start | bytes 3145736 | tf_op jit(solution)/shard_map/ppermute | solution.py:228
  474.1 24.6 %collective-permute-start.34 = (bf16[256,2048]{1,0:T(8,128)(2,1)S(1)}, bf16[256,2048]{1,0:T(8,128)(2,1)S(1)}, u32[]{:S(2)}, u32[]{:S(2)}) collective-permute-start(bf16[256,2048]{1,0:T(8,128)(2,1)S(1)} %get-tuple-element.208), channel_id=1, source_target_pairs={{0,1},{1,0},{2,3},{3,2},{4,5},{5,4},{6,7},{7,6},{8,9},{9,8},{10,11... | collective-permute-start | bytes 3145736 | tf_op jit(solution)/shard_map/ppermute | solution.py:228
  474.7 24.0 %collective-permute-start.35 = (bf16[256,2048]{1,0:T(8,128)(2,1)S(1)}, bf16[256,2048]{1,0:T(8,128)(2,1)S(1)}, u32[]{:S(2)}, u32[]{:S(2)}) collective-permute-start(bf16[256,2048]{1,0:T(8,128)(2,1)S(1)} %get-tuple-element.208), channel_id=1, source_target_pairs={{0,4},{4,0},{1,5},{5,1},{2,6},{6,2},{3,7},{7,3},{8,12},{12,8},{9,1... | collective-permute-start | bytes 3145736 | tf_op jit(solution)/shard_map/ppermute | solution.py:228
  520.4 35.3 %collective-permute-start.39 = (bf16[256,2048]{1,0:T(8,128)(2,1)}, bf16[256,2048]{1,0:T(8,128)(2,1)}, u32[]{:S(2)}, u32[]{:S(2)}) collective-permute-start(bf16[256,2048]{1,0:T(8,128)(2,1)} %pad_maximum_fusion.10), channel_id=1, source_target_pairs={{0,1},{1,0},{2,3},{3,2},{4,5},{5,4},{6,7},{7,6},{8,9},{9,8},{10,11... | collective-permute-start | bytes 3145736 | tf_op jit(solution)/shard_map/ppermute | solution.py:228
  521.8 33.9 %collective-permute-start.40 = (bf16[256,2048]{1,0:T(8,128)(2,1)}, bf16[256,2048]{1,0:T(8,128)(2,1)}, u32[]{:S(2)}, u32[]{:S(2)}) collective-permute-start(bf16[256,2048]{1,0:T(8,128)(2,1)} %pad_maximum_fusion.11), channel_id=1, source_target_pairs={{0,4},{4,0},{1,5},{5,1},{2,6},{6,2},{3,7},{7,3},{8,12},{12,8},{9,1... | collective-permute-start | bytes 3145736 | tf_op jit(solution)/shard_map/ppermute | solution.py:228
  522.4 41.9 %all-to-all-start.2 = ((bf16[4,128,1536]{2,1,0:T(8,128)(2,1)}), bf16[4,128,1536]{2,1,0:T(8,128)(2,1)}, u32[]{:S(2)}, u32[]{:S(2)}) async-start(bf16[4,128,1536]{2,1,0:T(8,128)(2,1)} %bitcast.151), calls=%async_computation.3 | async-start | bytes 3145728 | tf_op jit(solution)/shard_map/all_to_all | solution.py:286
  526.8 135.4 %reduce-scatter.6.cloned.1.call-start = ((), (), s32[]{:S(2)}) async-start(), calls=%async_computation.12 | async-start | bytes 5242880 | tf_op jit(solution)/shard_map/reduce_scatter | solution.py:294
  541.3 44.5 %collective-permute-start.44 = (bf16[1024,2048]{1,0:T(8,128)(2,1)}, bf16[1024,2048]{1,0:T(8,128)(2,1)}, u32[]{:S(2)}, u32[]{:S(2)}) collective-permute-start(bf16[1024,2048]{1,0:T(8,128)(2,1)} %get-tuple-element.193), channel_id=1, source_target_pairs={{0,2},{2,0},{1,3},{3,1},{4,6},{6,4},{5,7},{7,5},{8,10},{10,8},{9,1... | collective-permute-start | bytes 12582920 | tf_op jit(solution)/shard_map/ppermute | solution.py:228
  588.9 24.7 %collective-permute-start.45 = (bf16[256,2048]{1,0:T(8,128)(2,1)S(1)}, bf16[256,2048]{1,0:T(8,128)(2,1)S(1)}, u32[]{:S(2)}, u32[]{:S(2)}) collective-permute-start(bf16[256,2048]{1,0:T(8,128)(2,1)S(1)} %pad_maximum_fusion.12), channel_id=1, source_target_pairs={{0,1},{1,0},{2,3},{3,2},{4,5},{5,4},{6,7},{7,6},{8,9},{9,8},{10,11... | collective-permute-start | bytes 3145736 | tf_op jit(solution)/shard_map/ppermute | solution.py:228
  590.5 24.4 %collective-permute-start.46 = (bf16[256,2048]{1,0:T(8,128)(2,1)S(1)}, bf16[256,2048]{1,0:T(8,128)(2,1)S(1)}, u32[]{:S(2)}, u32[]{:S(2)}) collective-permute-start(bf16[256,2048]{1,0:T(8,128)(2,1)S(1)} %pad_maximum_fusion.13), channel_id=1, source_target_pairs={{0,4},{4,0},{1,5},{5,1},{2,6},{6,2},{3,7},{7,3},{8,12},{12,8},{9,1... | collective-permute-start | bytes 3145736 | tf_op jit(solution)/shard_map/ppermute | solution.py:228
  637.6 24.5 %all-to-all-start.4 = ((bf16[4,128,1536]{2,1,0:T(8,128)(2,1)}), bf16[4,128,1536]{2,1,0:T(8,128)(2,1)}, u32[]{:S(2)}, u32[]{:S(2)}) async-start(bf16[4,128,1536]{2,1,0:T(8,128)(2,1)} %bitcast.150), calls=%async_computation.7 | async-start | bytes 3145728 | tf_op jit(solution)/shard_map/all_to_all | solution.py:286
  (67 other events, 656.0 us)
Sparse Core Ops, SparseCore 0:
  42.8 82.8 all-gather.3
  127.8 113.8 all-gather.5
  243.9 113.5 all-gather.7
  359.7 108.9 reduce-scatter.3
  470.8 111.2 reduce-scatter.7
  585.9 75.7 reduce-scatter.5

commit v5 on v4

--- a/solution.py
+++ b/solution.py
@@ -379,12 +379,14 @@
     attn_block = to_columns(
         jnp.concatenate([quarters(w, width) for w in (w_query, w_key, w_value, w_out)], axis=2)
     )
+    wide = [quarters(w, units) for w in (w_gate, w_up, w_down)]
+    ffn_parts = [
+        jnp.concatenate([w[:, :, k * chunk : (k + 1) * chunk] for w in wide], axis=2)
+        for k in range(CHUNKS)
+    ]
+    ffn_parts[0], attn_block = together(ffn_parts[0], attn_block)
+    ffn_first = to_columns(ffn_parts[0])
     attn_weights = gather_line(attn_block)
-    wide = [quarters(w, units) for w in (w_gate, w_up, w_down)]
-    ffn_parts = jnp.concatenate(
-        [w[:, :, k * chunk : (k + 1) * chunk] for k in range(CHUNKS) for w in wide], axis=2
-    )
-    ffn_block = to_columns(ffn_parts)
 
     gains = gather_gains(jnp.stack([gain_attn, gain_ffn]), place, level)
     seg = jnp.concatenate(
@@ -406,14 +408,16 @@
     sine = jnp.concatenate([-sine, sine], axis=2)
     live = live.astype(low).reshape(2, -1, seq_len)
     sides = range(2)
-    state, live, cosine, sine, ffn_block = beside(
-        gather_first((unit_one * gain_first).astype(low)), live, cosine, sine, ffn_block
+    state, live, cosine, sine, ffn_first = beside(
+        gather_first((unit_one * gain_first).astype(low)), live, cosine, sine, ffn_first
     )
     rows_one = gather_last(state)
-    ffn_weights = [
-        gather_line(ffn_block[:, 3 * k * chunk : 3 * (k + 1) * chunk]) for k in range(CHUNKS)
-    ]
-    grad_own, attn_weights = together(cotangent, attn_weights)
+    ffn_weights = [gather_line(ffn_first)]
+    ffn_parts[1], rows_own = together(ffn_parts[1], rows_one[0])
+    rows_one = (rows_own, rows_one[1])
+    ffn_second = to_columns(ffn_parts[1])
+    grad_own, attn_weights, ffn_second = together(cotangent, attn_weights, ffn_second)
+    ffn_weights.append(gather_line(ffn_second))
 
     qkv, mixed, parts = zip(
         *(attend(rows_one[i], attn_weights, cosine[i], sine[i], live[i]) for i in sides)

time: 700 us -> 690 us (0.986)
  waiting for transfers between devices: 263 us -> 255 us
    ppermute x47, waiting for transfers between devices: 189 us -> 155 us  [swap(): return lax.ppermute(value, axis, [(0, 1), (1, 0)])]
    all_to_all x2 -> x3, waiting for transfers between devices: 0.79 us -> 28.1 us  [to_columns(): block = lax.all_to_all(parts, ('y', 'c'), 0, 0, tiled=True)]
    unnamed x82 -> x83, local copies, waits for them, and re-layouts: 24 us -> 20.5 us
  transfers between devices with their start and end apart: 67 -> 68, of which waited for: 32 -> 33; matrix products, arithmetic and copies ran while one was open for 17% -> 16% of each run, Pallas kernels for 31% -> 31%
where the time goes in v5:
time: 690 us; the launch traced here: 681 us
  waiting for transfers between devices  255 us (37%)
  Pallas kernels  212 us (31%)
  starting transfers between devices  77.6 us (11%)
  local copies, waits for them, and re-layouts  60.8 us (9%)
  other arithmetic  59.8 us (9%)
  between operations  15.6 us (2%)
    ppermute x47, waiting for transfers between devices, swap(): return lax.ppermute(value, axis, [(0, 1), (1, 0)])  155 us
    pallas_call x3, Pallas kernels, outer(): pl.pallas_call(functools.partial(outer_kernel, [len(group) for group in g...  55 us
    pallas_call x4, Pallas kernels, project(): pl.pallas_call(functools.partial(project_kernel, first, len(acts)), grid=...  54.4 us
    pallas_call x4, Pallas kernels, gated(): pl.pallas_call(functools.partial(gated_kernel, units), grid=(total // til...  49.2 us
    all_gather x3, waiting for transfers between devices, gather_line(): return lax.all_gather(block, 'z', axis=0, tiled=True)  47.7 us
    ppermute x47, starting transfers between devices, swap(): return lax.ppermute(value, axis, [(0, 1), (1, 0)])  40.6 us
    pallas_call x2, Pallas kernels, attend_back(): pl.pallas_call(functools.partial(attend_back_kernel, width), grid=(total...  28.5 us
    all_to_all x3, waiting for transfers between devices, to_columns(): block = lax.all_to_all(parts, ('y', 'c'), 0, 0, tiled=True)  28.1 us
  transfers between devices with their start and end apart: 68, of which 33 were waited for; matrix products, arithmetic and copies ran while one was open for 16% of the time, Pallas kernels for 31%

profile of v5, /device:TPU:0, one launch (start us, length us, event | category | flops | bytes accessed | tf_op | source)
XLA Modules:
  0.0 680.6 jit_solution(15158682464328923523)
XLA Ops:
  38.8 4.4 all-to-all-start.1
  51.8 11.4 %collective-permute-done.10 = bf16[256,2048]{1,0:T(8,128)(2,1)} collective-permute-done((bf16[256,2048]{1,0:T(8,128)(2,1)}, bf16[256,2048]{1,0:T(8,128)(2,1)}, u32[]{:S(2)}, u32[]{:S(2)}) %collective-permute-start.10) | collective-permute-done | bytes 1048608 | tf_op jit(solution)/shard_map/ppermute | solution.py:228
  67.0 12.4 %all-to-all-done.1 = bf16[4,128,1536]{2,1,0:T(8,128)(2,1)} async-done(((bf16[4,128,1536]{2,1,0:T(8,128)(2,1)}), bf16[4,128,1536]{2,1,0:T(8,128)(2,1)}, u32[]{:S(2)}, u32[]{:S(2)}) %all-to-all-start.1) | async-done | bytes 1572896 | tf_op jit(solution)/shard_map/all_to_all | solution.py:280
  86.0 6.8 collective-permute-done.11
  104.9 15.4 %all-to-all-done.2 = bf16[4,128,1536]{2,1,0:T(8,128)(2,1)} async-done(((bf16[4,128,1536]{2,1,0:T(8,128)(2,1)}), bf16[4,128,1536]{2,1,0:T(8,128)(2,1)}, u32[]{:S(2)}, u32[]{:S(2)}) %all-to-all-start.2) | async-done | bytes 1572896 | tf_op jit(solution)/shard_map/all_to_all | solution.py:280
  124.5 12.9 %shard_map.203 = (bf16[1024,768]{1,0:T(8,128)(2,1)}, bf16[1024,256]{1,0:T(8,128)(2,1)}, bf16[1024,2048]{1,0:T(8,128)(2,1)}) custom-call(bf16[1024,2048]{1,0:T(8,128)(2,1)} %constant_dynamic-update-slice_fusion.rows_ref.refs_0_, bf16[2048,1024]{1,0:T(8,128)(2,1)} %all-gather.4.cloned.1.call-done.w_ref, f32[1024,128]{1,0:T(8,128)} %get-tuple-element.275.cos_ref, ...), custom_call_target="tpu_custom_call" | custom-call | flops 4831838208 | bytes 14680064 | tf_op jit(solution)/shard_map/pallas_call | solution.py:84
  137.4 12.4 %shard_map.204 = (bf16[1024,768]{1,0:T(8,128)(2,1)}, bf16[1024,256]{1,0:T(8,128)(2,1)}, bf16[1024,2048]{1,0:T(8,128)(2,1)}) custom-call(bf16[1024,2048]{1,0:T(8,128)(2,1)} %collective-permute-done.15.rows_ref.refs_2_, bf16[2048,1024]{1,0:T(8,128)(2,1)} %all-gather.4.cloned.1.call-done.w_ref, f32[1024,128]{1,0:T(8,128)} %get-tuple-element.274.cos_ref, ...), custom_call_target="tpu_custom_call" | custom-call | flops 4831838208 | bytes 14680064 | tf_op jit(solution)/shard_map/pallas_call | solution.py:84
  151.6 7.4 %collective-permute-done.16 = bf16[1024,2048]{1,0:T(8,128)(2,1)S(1)} collective-permute-done((bf16[1024,2048]{1,0:T(8,128)(2,1)}, bf16[1024,2048]{1,0:T(8,128)(2,1)S(1)}, u32[]{:S(2)}, u32[]{:S(2)}) %collective-permute-start.16) | collective-permute-done | bytes 4194336 | tf_op jit(solution)/shard_map/ppermute | solution.py:228
  162.1 23.1 %collective-permute-done.17 = bf16[256,2048]{1,0:T(8,128)(2,1)S(1)} collective-permute-done((bf16[256,2048]{1,0:T(8,128)(2,1)S(1)}, bf16[256,2048]{1,0:T(8,128)(2,1)S(1)}, u32[]{:S(2)}, u32[]{:S(2)}) %collective-permute-start.17) | collective-permute-done | bytes 1048608 | tf_op jit(solution)/shard_map/ppermute | solution.py:228
  190.6 9.7 %collective-permute-done.19 = bf16[128,2048]{1,0:T(8,128)(2,1)} collective-permute-done((bf16[128,2048]{1,0:T(8,128)(2,1)}, bf16[128,2048]{1,0:T(8,128)(2,1)}, u32[]{:S(2)}, u32[]{:S(2)}) %collective-permute-start.19) | collective-permute-done | bytes 524320 | tf_op jit(solution)/shard_map/ppermute | solution.py:228
  207.6 21.4 %collective-permute-done.21 = bf16[256,2048]{1,0:T(8,128)(2,1)S(1)} collective-permute-done((bf16[256,2048]{1,0:T(8,128)(2,1)S(1)}, bf16[256,2048]{1,0:T(8,128)(2,1)S(1)}, u32[]{:S(2)}, u32[]{:S(2)}) %collective-permute-start.21) | collective-permute-done | bytes 1048608 | tf_op jit(solution)/shard_map/ppermute | solution.py:228
  233.6 7.5 %collective-permute-done.23 = bf16[128,2048]{1,0:T(8,128)(2,1)S(1)} collective-permute-done((bf16[128,2048]{1,0:T(8,128)(2,1)S(1)}, bf16[128,2048]{1,0:T(8,128)(2,1)S(1)}, u32[]{:S(2)}, u32[]{:S(2)}) %collective-permute-start.23) | collective-permute-done | bytes 524320 | tf_op jit(solution)/shard_map/ppermute | solution.py:228
  255.1 12.4 %shard_map.205 = (bf16[1024,1024]{1,0:T(8,128)(2,1)}, bf16[1024,512]{1,0:T(8,128)(2,1)}) custom-call(bf16[1024,2048]{1,0:T(8,128)(2,1)} %constant_dynamic-update-slice_fusion.5.rows_ref.refs_0_, bf16[1024,2048]{1,0:T(8,128)(2,1)} %constant_dynamic-update-slice_fusion.10.grad_ref.refs_4_, bf16[2048,1536]{1,0:T(8,128)(2,1)} %all-gather.6.cloned.1.call-done.w_ref.refs_2_), custom_call_target="tpu_custom_call" | custom-call | flops 6442450944 | bytes 17825792 | tf_op jit(solution)/shard_map/pallas_call | solution.py:157
  267.5 12.3 %shard_map.208 = (bf16[1024,1024]{1,0:T(8,128)(2,1)}, bf16[1024,512]{1,0:T(8,128)(2,1)}) custom-call(bf16[1024,2048]{1,0:T(8,128)(2,1)} %collective-permute-done.27.rows_ref.refs_2_, bf16[1024,2048]{1,0:T(8,128)(2,1)} %collective-permute-done.28.grad_ref.refs_6_, bf16[2048,1536]{1,0:T(8,128)(2,1)} %all-gather.6.cloned.1.call-done.w_ref.refs_2_), custom_call_target="tpu_custom_call" | custom-call | flops 6442450944 | bytes 17825792 | tf_op jit(solution)/shard_map/pallas_call | solution.py:157
  279.8 19.4 %shard_map.216 = bf16[2048,1536]{1,0:T(8,128)(2,1)} custom-call(bf16[1024,2048]{1,0:T(8,128)(2,1)} %constant_dynamic-update-slice_fusion.5.rows_ref.refs_0_, bf16[1024,1024]{1,0:T(8,128)(2,1)} %get-tuple-element.153.refs_0_.refs_1_, bf16[1024,2048]{1,0:T(8,128)(2,1)} %collective-permute-done.27.rows_ref.refs_2_, ...), custom_call_target="tpu_custom_call" | custom-call | flops 12884901888 | bytes 29360128 | tf_op jit(solution)/shard_map/pallas_call | solution.py:216
  299.4 47.7 %all-gather.8.cloned.1.call-done.w_ref.refs_3_ = bf16[2048,1536]{1,0:T(8,128)(2,1)} async-done(((bf16[512,1536]{1,0:T(8,128)(2,1)}), bf16[2048,1536]{1,0:T(8,128)(2,1)}) %all-gather.8.cloned.1.call-update) | async-done | bytes 6291472 | tf_op jit(solution)/shard_map/all_gather | solution.py:290
  347.1 12.3 %shard_map.209 = (bf16[1024,1024]{1,0:T(8,128)(2,1)}, bf16[1024,512]{1,0:T(8,128)(2,1)}) custom-call(bf16[1024,2048]{1,0:T(8,128)(2,1)} %collective-permute-done.27.rows_ref.refs_2_, bf16[1024,2048]{1,0:T(8,128)(2,1)} %collective-permute-done.28.grad_ref.refs_6_, bf16[2048,1536]{1,0:T(8,128)(2,1)} %all-gather.8.cloned.1.call-done.w_ref.refs_3_), custom_call_target="tpu_custom_call" | custom-call | flops 6442450944 | bytes 17825792 | tf_op jit(solution)/shard_map/pallas_call | solution.py:157
  359.4 15.5 %shard_map.210 = bf16[1024,2048]{1,0:T(8,128)(2,1)} custom-call(bf16[1024,1024]{1,0:T(8,128)(2,1)} %get-tuple-element.156.refs_0_.refs_3_, bf16[1024,1024]{1,0:T(8,128)(2,1)} %get-tuple-element.157.refs_1_.refs_3_, bf16[2048,1536]{1,0:T(8,128)(2,1)} %all-gather.6.cloned.1.call-done.w_ref.refs_2_, bf16[2048,1536]{1,0:T(8,128)(2,1)} %all-gather.8.cloned.1.call-done.w_ref.refs_3_), custom_call_target="tpu_custom_call" | custom-call | flops 8589934592 | bytes 20971520 | tf_op jit(solution)/shard_map/pallas_call | solution.py:180
  374.9 12.3 %shard_map.206 = (bf16[1024,1024]{1,0:T(8,128)(2,1)}, bf16[1024,512]{1,0:T(8,128)(2,1)}) custom-call(bf16[1024,2048]{1,0:T(8,128)(2,1)} %constant_dynamic-update-slice_fusion.5.rows_ref.refs_0_, bf16[1024,2048]{1,0:T(8,128)(2,1)} %constant_dynamic-update-slice_fusion.10.grad_ref.refs_4_, bf16[2048,1536]{1,0:T(8,128)(2,1)} %all-gather.8.cloned.1.call-done.w_ref.refs_3_), custom_call_target="tpu_custom_call" | custom-call | flops 6442450944 | bytes 17825792 | tf_op jit(solution)/shard_map/pallas_call | solution.py:157
  387.2 15.5 %shard_map.207 = bf16[1024,2048]{1,0:T(8,128)(2,1)} custom-call(bf16[1024,1024]{1,0:T(8,128)(2,1)} %get-tuple-element.153.refs_0_.refs_1_, bf16[1024,1024]{1,0:T(8,128)(2,1)} %get-tuple-element.155.refs_1_, bf16[2048,1536]{1,0:T(8,128)(2,1)} %all-gather.6.cloned.1.call-done.w_ref.refs_2_, bf16[2048,1536]{1,0:T(8,128)(2,1)} %all-gather.8.cloned.1.call-done.w_ref.refs_3_), custom_call_target="tpu_custom_call" | custom-call | flops 8589934592 | bytes 20971520 | tf_op jit(solution)/shard_map/pallas_call | solution.py:180
  411.6 19.7 %shard_map.211 = bf16[2048,1536]{1,0:T(8,128)(2,1)} custom-call(bf16[1024,2048]{1,0:T(8,128)(2,1)} %constant_dynamic-update-slice_fusion.5.rows_ref.refs_0_, bf16[1024,1024]{1,0:T(8,128)(2,1)} %get-tuple-element.155.refs_1_, bf16[1024,2048]{1,0:T(8,128)(2,1)} %collective-permute-done.27.rows_ref.refs_2_, ...), custom_call_target="tpu_custom_call" | custom-call | flops 12884901888 | bytes 29360128 | tf_op jit(solution)/shard_map/pallas_call | solution.py:216
  445.0 11.4 %collective-permute-done.32 = bf16[128,2048]{1,0:T(8,128)(2,1)S(1)} collective-permute-done((bf16[128,2048]{1,0:T(8,128)(2,1)}, bf16[128,2048]{1,0:T(8,128)(2,1)S(1)}, u32[]{:S(2)}, u32[]{:S(2)}) %collective-permute-start.32) | collective-permute-done | bytes 524320 | tf_op jit(solution)/shard_map/ppermute | solution.py:228
  464.7 12.2 %shard_map.212 = bf16[1024,2048]{1,0:T(8,128)(2,1)} custom-call(bf16[1024,512]{1,0:T(8,128)(2,1)} %get-tuple-element.172.refs_0_.refs_5_, bf16[1024,512]{1,0:T(8,128)(2,1)} %get-tuple-element.162.refs_5_.refs_1_, bf16[2048,1536]{1,0:T(8,128)(2,1)} %all-gather.6.cloned.1.call-done.w_ref.refs_2_, bf16[2048,1536]{1,0:T(8,128)(2,1)} %all-gather.8.cloned.1.call-done.w_ref.refs_3_), custom_call_target="tpu_custom_call" | custom-call | flops 4294967296 | bytes 18874368 | tf_op jit(solution)/shard_map/pallas_call | solution.py:180
  476.9 11.3 %shard_map.213 = bf16[1024,2048]{1,0:T(8,128)(2,1)} custom-call(bf16[1024,512]{1,0:T(8,128)(2,1)} %get-tuple-element.173.refs_0_.refs_7_, bf16[1024,512]{1,0:T(8,128)(2,1)} %get-tuple-element.163.refs_7_.refs_1_, bf16[2048,1536]{1,0:T(8,128)(2,1)} %all-gather.6.cloned.1.call-done.w_ref.refs_2_, bf16[2048,1536]{1,0:T(8,128)(2,1)} %all-gather.8.cloned.1.call-done.w_ref.refs_3_), custom_call_target="tpu_custom_call" | custom-call | flops 4294967296 | bytes 18874368 | tf_op jit(solution)/shard_map/pallas_call | solution.py:180
  493.6 9.1 %collective-permute-done.37 = bf16[128,2048]{1,0:T(8,128)(2,1)S(1)} collective-permute-done((bf16[128,2048]{1,0:T(8,128)(2,1)S(1)}, bf16[128,2048]{1,0:T(8,128)(2,1)S(1)}, u32[]{:S(2)}, u32[]{:S(2)}) %collective-permute-start.37) | collective-permute-done | bytes 524320 | tf_op jit(solution)/shard_map/ppermute | solution.py:228
  516.4 14.5 %shard_map.215 = (bf16[1024,768]{1,0:T(8,128)(2,1)}, bf16[1024,2048]{1,0:T(8,128)(2,1)}) custom-call(bf16[1024,2048]{1,0:T(8,128)(2,1)} %collective-permute-done.41.grad_ref.refs_6_, bf16[2048,1024]{1,0:T(8,128)(2,1)} %all-gather.4.cloned.1.call-done.w_ref, bf16[1024,768]{1,0:T(8,128)(2,1)} %get-tuple-element.189.qkv_ref, ...), custom_call_target="tpu_custom_call" | custom-call | flops 5637144576 | bytes 15728640 | tf_op jit(solution)/shard_map/pallas_call | solution.py:119
  531.3 14.1 %shard_map.214 = (bf16[1024,768]{1,0:T(8,128)(2,1)}, bf16[1024,2048]{1,0:T(8,128)(2,1)}) custom-call(bf16[1024,2048]{1,0:T(8,128)(2,1)} %constant_dynamic-update-slice_fusion.15.grad_ref.refs_4_, bf16[2048,1024]{1,0:T(8,128)(2,1)} %all-gather.4.cloned.1.call-done.w_ref, bf16[1024,768]{1,0:T(8,128)(2,1)} %get-tuple-element.187.qkv_ref, ...), custom_call_target="tpu_custom_call" | custom-call | flops 5637144576 | bytes 15728640 | tf_op jit(solution)/shard_map/pallas_call | solution.py:119
  555.0 16.0 %shard_map.217 = bf16[2048,1024]{1,0:T(8,128)(2,1)} custom-call(bf16[1024,2048]{1,0:T(8,128)(2,1)} %constant_dynamic-update-slice_fusion.rows_ref.refs_0_, bf16[1024,768]{1,0:T(8,128)(2,1)} %get-tuple-element.191.refs_1_, bf16[1024,2048]{1,0:T(8,128)(2,1)} %collective-permute-done.15.rows_ref.refs_2_, bf16[1024,768]{1,0:T(8,128)(2,1)} %get-tuple-element.192.refs_3_, ...), custom_call_target="tpu_custom_call" | custom-call | flops 8589934592 | bytes 25165824 | tf_op jit(solution)/shard_map/pallas_call | solution.py:216
  581.6 21.7 %collective-permute-done.45 = bf16[256,2048]{1,0:T(8,128)(2,1)S(1)} collective-permute-done((bf16[256,2048]{1,0:T(8,128)(2,1)S(1)}, bf16[256,2048]{1,0:T(8,128)(2,1)S(1)}, u32[]{:S(2)}, u32[]{:S(2)}) %collective-permute-start.45) | collective-permute-done | bytes 1048608 | tf_op jit(solution)/shard_map/ppermute | solution.py:228
  610.3 8.3 %collective-permute-done.47 = bf16[128,2048]{1,0:T(8,128)(2,1)S(1)} collective-permute-done((bf16[128,2048]{1,0:T(8,128)(2,1)S(1)}, bf16[128,2048]{1,0:T(8,128)(2,1)S(1)}, u32[]{:S(2)}, u32[]{:S(2)}) %collective-permute-start.47) | collective-permute-done | bytes 524320 | tf_op jit(solution)/shard_map/ppermute | solution.py:228
  639.0 12.7 %all-to-all-done.5 = bf16[4,128,1536]{2,1,0:T(8,128)(2,1)} async-done(((bf16[4,128,1536]{2,1,0:T(8,128)(2,1)}), bf16[4,128,1536]{2,1,0:T(8,128)(2,1)}, u32[]{:S(2)}, u32[]{:S(2)}) %all-to-all-start.5) | async-done | bytes 1572896 | tf_op jit(solution)/shard_map/all_to_all | solution.py:286
  662.4 7.2 %all-to-all-done.4 = bf16[4,128,1024]{2,1,0:T(8,128)(2,1)S(1)} async-done(((bf16[4,128,1024]{2,1,0:T(8,128)(2,1)}), bf16[4,128,1024]{2,1,0:T(8,128)(2,1)S(1)}, u32[]{:S(2)}, u32[]{:S(2)}) %all-to-all-start.4) | async-done | bytes 1048608 | tf_op jit(solution)/shard_map/all_to_all | solution.py:286
  (318 shorter events, 215.3 us)
Async XLA Ops:
  11.1 20.0 %collective-permute-start.6 = (s32[1,512]{1,0:T(1,128)}, s32[1,512]{1,0:T(1,128)S(1)}, u32[]{:S(2)}, u32[]{:S(2)}) collective-permute-start(s32[1,512]{1,0:T(1,128)} %param.13), channel_id=1, source_target_pairs={{0,4},{4,0},{1,5},{5,1},{2,6},{6,2},{3,7},{7,3},{8,12},{12,8},{9,1... | collective-permute-start | bytes 6152 | tf_op jit(solution)/shard_map/ppermute | solution.py:228
  12.8 19.6 %collective-permute-start.7 = (s32[1,512]{1,0:T(1,128)}, s32[1,512]{1,0:T(1,128)S(1)}, u32[]{:S(2)}, u32[]{:S(2)}) collective-permute-start(s32[1,512]{1,0:T(1,128)} %param.13), channel_id=1, source_target_pairs={{0,2},{2,0},{1,3},{3,1},{4,6},{6,4},{5,7},{7,5},{8,10},{10,8},{9,1... | collective-permute-start | bytes 6152 | tf_op jit(solution)/shard_map/ppermute | solution.py:228
  19.8 100.5 %all-gather.4.cloned.1.call-start = ((), (), s32[]{:S(2)}) async-start(), calls=%async_computation.9 | async-start | bytes 5242880 | tf_op jit(solution)/shard_map/all_gather | solution.py:290
  36.9 26.3 %collective-permute-start.10 = (bf16[256,2048]{1,0:T(8,128)(2,1)}, bf16[256,2048]{1,0:T(8,128)(2,1)}, u32[]{:S(2)}, u32[]{:S(2)}) collective-permute-start(bf16[256,2048]{1,0:T(8,128)(2,1)} %get-tuple-element.225), channel_id=1, source_target_pairs={{0,4},{4,0},{1,5},{5,1},{2,6},{6,2},{3,7},{7,3},{8,12},{12,8},{9,1... | collective-permute-start | bytes 3145736 | tf_op jit(solution)/shard_map/ppermute | solution.py:228
  37.3 26.0 %collective-permute-start.9 = (bf16[256,2048]{1,0:T(8,128)(2,1)}, bf16[256,2048]{1,0:T(8,128)(2,1)}, u32[]{:S(2)}, u32[]{:S(2)}) collective-permute-start(bf16[256,2048]{1,0:T(8,128)(2,1)} %get-tuple-element.225), channel_id=1, source_target_pairs={{0,1},{1,0},{2,3},{3,2},{4,5},{5,4},{6,7},{7,6},{8,9},{9,8},{10,11... | collective-permute-start | bytes 3145736 | tf_op jit(solution)/shard_map/ppermute | solution.py:228
  38.8 40.6 %all-to-all-start.1 = ((bf16[4,128,1536]{2,1,0:T(8,128)(2,1)}), bf16[4,128,1536]{2,1,0:T(8,128)(2,1)}, u32[]{:S(2)}, u32[]{:S(2)}) async-start(bf16[4,128,1536]{2,1,0:T(8,128)(2,1)} %pad_maximum_fusion.3), calls=%async_computation.1 | async-start | bytes 3145728 | tf_op jit(solution)/shard_map/all_to_all | solution.py:280
  94.5 42.9 %collective-permute-start.15 = (bf16[1024,2048]{1,0:T(8,128)(2,1)}, bf16[1024,2048]{1,0:T(8,128)(2,1)}, u32[]{:S(2)}, u32[]{:S(2)}) collective-permute-start(bf16[1024,2048]{1,0:T(8,128)(2,1)} %constant_dynamic-update-slice_fusion.rows_ref.refs_0_), channel_id=1, source_target_pairs={{0,2},{2,0},{1,3},{3,1},{4,6},{6,4},{5,7},{7,5},{8,10},{10,8},{9,1... | collective-permute-start | bytes 12582920 | tf_op jit(solution)/shard_map/ppermute | solution.py:228
  95.8 24.5 %all-to-all-start.2 = ((bf16[4,128,1536]{2,1,0:T(8,128)(2,1)}), bf16[4,128,1536]{2,1,0:T(8,128)(2,1)}, u32[]{:S(2)}, u32[]{:S(2)}) async-start(bf16[4,128,1536]{2,1,0:T(8,128)(2,1)} %pad_maximum_fusion.4), calls=%async_computation.2 | async-start | bytes 3145728 | tf_op jit(solution)/shard_map/all_to_all | solution.py:280
  100.1 155.0 %all-gather.6.cloned.1.call-start = ((), (), s32[]{:S(2)}) async-start(), calls=%async_computation.10 | async-start | bytes 7864320 | tf_op jit(solution)/shard_map/all_gather | solution.py:290
  100.9 246.2 %all-gather.8.cloned.1.call-start = ((), (), s32[]{:S(2)}) async-start(), calls=%async_computation.11 | async-start | bytes 7864320 | tf_op jit(solution)/shard_map/all_gather | solution.py:290
  120.3 29.5 %collective-permute-start.13 = (bf16[256,2048]{1,0:T(8,128)(2,1)}, bf16[256,2048]{1,0:T(8,128)(2,1)S(1)}, u32[]{:S(2)}, u32[]{:S(2)}) collective-permute-start(bf16[256,2048]{1,0:T(8,128)(2,1)} %param.23), channel_id=1, source_target_pairs={{0,1},{1,0},{2,3},{3,2},{4,5},{5,4},{6,7},{7,6},{8,9},{9,8},{10,11... | collective-permute-start | bytes 3145736 | tf_op jit(solution)/shard_map/ppermute | solution.py:228
  121.8 28.0 %collective-permute-start.14 = (bf16[256,2048]{1,0:T(8,128)(2,1)}, bf16[256,2048]{1,0:T(8,128)(2,1)S(1)}, u32[]{:S(2)}, u32[]{:S(2)}) collective-permute-start(bf16[256,2048]{1,0:T(8,128)(2,1)} %param.23), channel_id=1, source_target_pairs={{0,4},{4,0},{1,5},{5,1},{2,6},{6,2},{3,7},{7,3},{8,12},{12,8},{9,1... | collective-permute-start | bytes 3145736 | tf_op jit(solution)/shard_map/ppermute | solution.py:228
  159.9 25.3 %collective-permute-start.17 = (bf16[256,2048]{1,0:T(8,128)(2,1)S(1)}, bf16[256,2048]{1,0:T(8,128)(2,1)S(1)}, u32[]{:S(2)}, u32[]{:S(2)}) collective-permute-start(bf16[256,2048]{1,0:T(8,128)(2,1)S(1)} %pad_maximum_fusion.8), channel_id=1, source_target_pairs={{0,1},{1,0},{2,3},{3,2},{4,5},{5,4},{6,7},{7,6},{8,9},{9,8},{10,11... | collective-permute-start | bytes 3145736 | tf_op jit(solution)/shard_map/ppermute | solution.py:228
  160.5 24.9 %collective-permute-start.18 = (bf16[256,2048]{1,0:T(8,128)(2,1)S(1)}, bf16[256,2048]{1,0:T(8,128)(2,1)S(1)}, u32[]{:S(2)}, u32[]{:S(2)}) collective-permute-start(bf16[256,2048]{1,0:T(8,128)(2,1)S(1)} %pad_maximum_fusion.9), channel_id=1, source_target_pairs={{0,4},{4,0},{1,5},{5,1},{2,6},{6,2},{3,7},{7,3},{8,12},{12,8},{9,1... | collective-permute-start | bytes 3145736 | tf_op jit(solution)/shard_map/ppermute | solution.py:228
  190.1 321.9 %reduce-scatter.4.cloned.1.call-start = ((), (), s32[]{:S(2)}) async-start(), calls=%async_computation.12 | async-start | bytes 7864320 | tf_op jit(solution)/shard_map/reduce_scatter | solution.py:294
  205.8 23.1 %collective-permute-start.21 = (bf16[256,2048]{1,0:T(8,128)(2,1)S(1)}, bf16[256,2048]{1,0:T(8,128)(2,1)S(1)}, u32[]{:S(2)}, u32[]{:S(2)}) collective-permute-start(bf16[256,2048]{1,0:T(8,128)(2,1)S(1)} %get-tuple-element.221), channel_id=1, source_target_pairs={{0,1},{1,0},{2,3},{3,2},{4,5},{5,4},{6,7},{7,6},{8,9},{9,8},{10,11... | collective-permute-start | bytes 3145736 | tf_op jit(solution)/shard_map/ppermute | solution.py:228
  207.2 23.1 %collective-permute-start.22 = (bf16[256,2048]{1,0:T(8,128)(2,1)S(1)}, bf16[256,2048]{1,0:T(8,128)(2,1)S(1)}, u32[]{:S(2)}, u32[]{:S(2)}) collective-permute-start(bf16[256,2048]{1,0:T(8,128)(2,1)S(1)} %get-tuple-element.221), channel_id=1, source_target_pairs={{0,4},{4,0},{1,5},{5,1},{2,6},{6,2},{3,7},{7,3},{8,12},{12,8},{9,1... | collective-permute-start | bytes 3145736 | tf_op jit(solution)/shard_map/ppermute | solution.py:228
  248.3 19.2 %collective-permute-start.27 = (bf16[1024,2048]{1,0:T(8,128)(2,1)}, bf16[1024,2048]{1,0:T(8,128)(2,1)}, u32[]{:S(2)}, u32[]{:S(2)}) collective-permute-start(bf16[1024,2048]{1,0:T(8,128)(2,1)} %constant_dynamic-update-slice_fusion.5.rows_ref.refs_0_), channel_id=1, source_target_pairs={{0,2},{2,0},{1,3},{3,1},{4,6},{6,4},{5,7},{7,5},{8,10},{10,8},{9,1... | collective-permute-start | bytes 12582920 | tf_op jit(solution)/shard_map/ppermute | solution.py:228
  299.2 328.0 %reduce-scatter.8.cloned.1.call-start = ((), (), s32[]{:S(2)}) async-start(), calls=%async_computation.14 | async-start | bytes 7864320 | tf_op jit(solution)/shard_map/reduce_scatter | solution.py:294
  374.9 27.8 %collective-permute-start.29 = (bf16[1024,2048]{1,0:T(8,128)(2,1)}, bf16[1024,2048]{1,0:T(8,128)(2,1)S(1)}, u32[]{:S(2)}, u32[]{:S(2)}) collective-permute-start(bf16[1024,2048]{1,0:T(8,128)(2,1)} %shard_map.210), channel_id=1, source_target_pairs={{0,2},{2,0},{1,3},{3,1},{4,6},{6,4},{5,7},{7,5},{8,10},{10,8},{9,1... | collective-permute-start | bytes 12582920 | tf_op jit(solution)/shard_map/ppermute | solution.py:228
  408.6 25.8 %collective-permute-start.30 = (bf16[256,2048]{1,0:T(8,128)(2,1)}, bf16[256,2048]{1,0:T(8,128)(2,1)}, u32[]{:S(2)}, u32[]{:S(2)}) collective-permute-start(bf16[256,2048]{1,0:T(8,128)(2,1)} %pad_maximum_fusion.10), channel_id=1, source_target_pairs={{0,1},{1,0},{2,3},{3,2},{4,5},{5,4},{6,7},{7,6},{8,9},{9,8},{10,11... | collective-permute-start | bytes 3145736 | tf_op jit(solution)/shard_map/ppermute | solution.py:228
  410.1 25.6 %collective-permute-start.31 = (bf16[256,2048]{1,0:T(8,128)(2,1)}, bf16[256,2048]{1,0:T(8,128)(2,1)}, u32[]{:S(2)}, u32[]{:S(2)}) collective-permute-start(bf16[256,2048]{1,0:T(8,128)(2,1)} %pad_maximum_fusion.11), channel_id=1, source_target_pairs={{0,4},{4,0},{1,5},{5,1},{2,6},{6,2},{3,7},{7,3},{8,12},{12,8},{9,1... | collective-permute-start | bytes 3145736 | tf_op jit(solution)/shard_map/ppermute | solution.py:228
  463.7 24.5 %collective-permute-start.34 = (bf16[256,2048]{1,0:T(8,128)(2,1)S(1)}, bf16[256,2048]{1,0:T(8,128)(2,1)S(1)}, u32[]{:S(2)}, u32[]{:S(2)}) collective-permute-start(bf16[256,2048]{1,0:T(8,128)(2,1)S(1)} %get-tuple-element.218), channel_id=1, source_target_pairs={{0,1},{1,0},{2,3},{3,2},{4,5},{5,4},{6,7},{7,6},{8,9},{9,8},{10,11... | collective-permute-start | bytes 3145736 | tf_op jit(solution)/shard_map/ppermute | solution.py:228
  464.3 23.9 %collective-permute-start.35 = (bf16[256,2048]{1,0:T(8,128)(2,1)S(1)}, bf16[256,2048]{1,0:T(8,128)(2,1)S(1)}, u32[]{:S(2)}, u32[]{:S(2)}) collective-permute-start(bf16[256,2048]{1,0:T(8,128)(2,1)S(1)} %get-tuple-element.218), channel_id=1, source_target_pairs={{0,4},{4,0},{1,5},{5,1},{2,6},{6,2},{3,7},{7,3},{8,12},{12,8},{9,1... | collective-permute-start | bytes 3145736 | tf_op jit(solution)/shard_map/ppermute | solution.py:228
  510.1 35.3 %collective-permute-start.39 = (bf16[256,2048]{1,0:T(8,128)(2,1)}, bf16[256,2048]{1,0:T(8,128)(2,1)}, u32[]{:S(2)}, u32[]{:S(2)}) collective-permute-start(bf16[256,2048]{1,0:T(8,128)(2,1)} %pad_maximum_fusion.12), channel_id=1, source_target_pairs={{0,1},{1,0},{2,3},{3,2},{4,5},{5,4},{6,7},{7,6},{8,9},{9,8},{10,11... | collective-permute-start | bytes 3145736 | tf_op jit(solution)/shard_map/ppermute | solution.py:228
  511.5 33.9 %collective-permute-start.40 = (bf16[256,2048]{1,0:T(8,128)(2,1)}, bf16[256,2048]{1,0:T(8,128)(2,1)}, u32[]{:S(2)}, u32[]{:S(2)}) collective-permute-start(bf16[256,2048]{1,0:T(8,128)(2,1)} %pad_maximum_fusion.13), channel_id=1, source_target_pairs={{0,4},{4,0},{1,5},{5,1},{2,6},{6,2},{3,7},{7,3},{8,12},{12,8},{9,1... | collective-permute-start | bytes 3145736 | tf_op jit(solution)/shard_map/ppermute | solution.py:228
  512.0 41.9 %all-to-all-start.3 = ((bf16[4,128,1536]{2,1,0:T(8,128)(2,1)}), bf16[4,128,1536]{2,1,0:T(8,128)(2,1)}, u32[]{:S(2)}, u32[]{:S(2)}) async-start(bf16[4,128,1536]{2,1,0:T(8,128)(2,1)} %bitcast.149), calls=%async_computation.4 | async-start | bytes 3145728 | tf_op jit(solution)/shard_map/all_to_all | solution.py:286
  516.4 135.3 %reduce-scatter.6.cloned.1.call-start = ((), (), s32[]{:S(2)}) async-start(), calls=%async_computation.13 | async-start | bytes 5242880 | tf_op jit(solution)/shard_map/reduce_scatter | solution.py:294
  530.9 44.5 %collective-permute-start.44 = (bf16[1024,2048]{1,0:T(8,128)(2,1)}, bf16[1024,2048]{1,0:T(8,128)(2,1)}, u32[]{:S(2)}, u32[]{:S(2)}) collective-permute-start(bf16[1024,2048]{1,0:T(8,128)(2,1)} %get-tuple-element.203), channel_id=1, source_target_pairs={{0,2},{2,0},{1,3},{3,1},{4,6},{6,4},{5,7},{7,5},{8,10},{10,8},{9,1... | collective-permute-start | bytes 12582920 | tf_op jit(solution)/shard_map/ppermute | solution.py:228
  578.5 24.7 %collective-permute-start.45 = (bf16[256,2048]{1,0:T(8,128)(2,1)S(1)}, bf16[256,2048]{1,0:T(8,128)(2,1)S(1)}, u32[]{:S(2)}, u32[]{:S(2)}) collective-permute-start(bf16[256,2048]{1,0:T(8,128)(2,1)S(1)} %pad_maximum_fusion.14), channel_id=1, source_target_pairs={{0,1},{1,0},{2,3},{3,2},{4,5},{5,4},{6,7},{7,6},{8,9},{9,8},{10,11... | collective-permute-start | bytes 3145736 | tf_op jit(solution)/shard_map/ppermute | solution.py:228
  580.1 24.4 %collective-permute-start.46 = (bf16[256,2048]{1,0:T(8,128)(2,1)S(1)}, bf16[256,2048]{1,0:T(8,128)(2,1)S(1)}, u32[]{:S(2)}, u32[]{:S(2)}) collective-permute-start(bf16[256,2048]{1,0:T(8,128)(2,1)S(1)} %pad_maximum_fusion.15), channel_id=1, source_target_pairs={{0,4},{4,0},{1,5},{5,1},{2,6},{6,2},{3,7},{7,3},{8,12},{12,8},{9,1... | collective-permute-start | bytes 3145736 | tf_op jit(solution)/shard_map/ppermute | solution.py:228
  627.2 24.5 %all-to-all-start.5 = ((bf16[4,128,1536]{2,1,0:T(8,128)(2,1)}), bf16[4,128,1536]{2,1,0:T(8,128)(2,1)}, u32[]{:S(2)}, u32[]{:S(2)}) async-start(bf16[4,128,1536]{2,1,0:T(8,128)(2,1)} %bitcast.148), calls=%async_computation.8 | async-start | bytes 3145728 | tf_op jit(solution)/shard_map/all_to_all | solution.py:286
  (71 other events, 697.1 us)
Sparse Core Ops, SparseCore 0:
  35.3 81.0 all-gather.3
  118.0 113.8 all-gather.5
  233.5 113.5 all-gather.7
  349.3 108.9 reduce-scatter.3
  460.4 111.2 reduce-scatter.7
  575.5 75.7 reduce-scatter.5

commit v6 on v5

--- a/solution.py
+++ b/solution.py
@@ -170,23 +170,29 @@
     for act_ref, w_ref in zip(refs[:count], refs[count : 2 * count]):
         term = dot_rt(act_ref[...], w_ref[:, first : first + act_ref.shape[1]])
         total = term if total is None else total + term
-    refs[-1][...] = total.astype(low)
-
-
-def project(acts, weights, first, tile=256):
+    for ref in refs[2 * count : -1]:
+        total = total + ref[...]
+    refs[-1][...] = total.astype(refs[-1].dtype)
+
+
+def project(acts, weights, first, *earlier, dtype=low, tile=256):
     total, wide = acts[0].shape
     model = weights[0].shape[0]
-    out = jax.ShapeDtypeStruct((total, model), low)
+    out = jax.ShapeDtypeStruct((total, model), dtype)
+    tiled = lambda columns: pl.BlockSpec((tile, columns), lambda i: (i, 0))
     return pl.pallas_call(
         functools.partial(project_kernel, first, len(acts)),
         grid=(total // tile,),
-        in_specs=[pl.BlockSpec((tile, wide), lambda i: (i, 0))] * len(acts)
-        + [whole(w) for w in weights],
-        out_specs=pl.BlockSpec((tile, model), lambda i: (i, 0)),
+        in_specs=[tiled(wide)] * len(acts)
+        + [whole(w) for w in weights]
+        + [tiled(model)] * len(earlier),
+        out_specs=tiled(model),
         out_shape=out,
         compiler_params=params,
-        cost_estimate=cost(2 * total * model * wide * len(acts), *acts, *weights, out),
-    )(*acts, *weights)
+        cost_estimate=cost(
+            2 * total * model * wide * len(acts), *acts, *weights, *earlier, out
+        ),
+    )(*acts, *weights, *earlier)
 
 
 def outer_kernel(groups, *refs):
@@ -224,6 +230,44 @@
     )(*operands)
 
 
+def pack_kernel(width, *refs):
+    out_ref = refs[-1]
+    for k, ref in enumerate(refs[:-1]):
+        for q in range(PLANE):
+            out_ref[q, :, k * width : (k + 1) * width] = ref[:, q * width : (q + 1) * width]
+
+
+def pack(*weights):
+    rows, columns = weights[0].shape
+    width = columns // PLANE
+    out = jax.ShapeDtypeStruct((PLANE, rows, width * len(weights)), low)
+    return pl.pallas_call(
+        functools.partial(pack_kernel, width),
+        out_shape=out,
+        compiler_params=params,
+        cost_estimate=cost(0, *weights, out),
+    )(*weights)
+
+
+def unpack_kernel(width, parts_ref, *out_refs):
+    for k, ref in enumerate(out_refs):
+        for q in range(PLANE):
+            ref[:, q * width : (q + 1) * width] = parts_ref[
+                q, :, k * width : (k + 1) * width
+            ].astype(f32)
+
+
+def unpack(parts, count):
+    rows, width = parts.shape[1], parts.shape[2] // count
+    outs = [jax.ShapeDtypeStruct((rows, PLANE * width), f32)] * count
+    return pl.pallas_call(
+        functools.partial(unpack_kernel, width),
+        out_shape=outs,
+        compiler_params=params,
+        cost_estimate=cost(0, parts, *outs),
+    )(parts)
+
+
 def swap(value, axis):
     return lax.ppermute(value, axis, [(0, 1), (1, 0)])
 
@@ -234,11 +278,13 @@
     return own, from_x, from_y, (from_x[:half], from_y[half:])
 
 
-def gather_last(state):
+def gather_last(state, *before_core):
     own, from_x, from_y, (top, bottom) = state
     top, bottom = together(swap(top, "y"), swap(bottom, "tensor"))
     chip = jnp.concatenate([own, from_x, from_y, top, bottom], axis=0)
-    return chip, swap(chip, "c")
+    if before_core:
+        chip, *before_core = together(chip, *before_core)
+    return chip, swap(chip, "c"), *before_core
 
 
 def scatter_first(mine, theirs):
@@ -376,9 +422,11 @@
     units = w_gate.shape[1] // PLANE
     chunk = units // CHUNKS
 
-    attn_block = to_columns(
-        jnp.concatenate([quarters(w, width) for w in (w_query, w_key, w_value, w_out)], axis=2)
-    )
+    attn_parts = pack(w_query, w_key, w_value, w_out)
+    attn_parts, gain_attn, gain_ffn, segments = together(
+        attn_parts, gain_attn, gain_ffn, segments
+    )
+    attn_block = to_columns(attn_parts)
     wide = [quarters(w, units) for w in (w_gate, w_up, w_down)]
     ffn_parts = [
         jnp.concatenate([w[:, :, k * chunk : (k + 1) * chunk] for w in wide], axis=2)
@@ -411,19 +459,19 @@
     state, live, cosine, sine, ffn_first = beside(
         gather_first((unit_one * gain_first).astype(low)), live, cosine, sine, ffn_first
     )
-    rows_one = gather_last(state)
+    *rows_one, attn_weights = gather_last(state, attn_weights)
     ffn_weights = [gather_line(ffn_first)]
-    ffn_parts[1], rows_own = together(ffn_parts[1], rows_one[0])
-    rows_one = (rows_own, rows_one[1])
+    grad_own, attn_weights = together(cotangent, attn_weights)
+
+    qkv, mixed, parts = [None, None], [None, None], [None, None]
+    for i in sides:
+        qkv[i], mixed[i], parts[i] = attend(rows_one[i], attn_weights, cosine[i], sine[i], live[i])
+    parts[0], ffn_parts[1] = together(parts[0], ffn_parts[1])
     ffn_second = to_columns(ffn_parts[1])
-    grad_own, attn_weights, ffn_second = together(cotangent, attn_weights, ffn_second)
+    grad_state, parts = beside(gather_first(grad_own), parts)
+    state, ffn_second = beside(scatter_second(scatter_first(*parts)), ffn_second)
     ffn_weights.append(gather_line(ffn_second))
-
-    qkv, mixed, parts = zip(
-        *(attend(rows_one[i], attn_weights, cosine[i], sine[i], live[i]) for i in sides)
-    )
-    grad_state, parts = beside(gather_first(grad_own), parts)
-    middle = inputs + scatter_last(scatter_second(scatter_first(*parts)))
+    middle = inputs + scatter_last(state)
     unit_two, scale_two = normalize(middle)
     rows_two = gather_last(gather_first((unit_two * gain_second).astype(low)))
     grad_state, rows_own = beside(grad_state, rows_two[0])
@@ -438,11 +486,18 @@
         for i in sides:
             both[i][k], hidden[i][k] = gated(rows_two[i], grad_rows[i], ffn_weights[k])
         if k == CHUNKS - 1:
-            grad_parts = [project(both[i], ffn_weights, 0) for i in sides]
+            grad_parts = [
+                project(both[i][k:], ffn_weights[k:], 0, grad_parts[i]) for i in sides
+            ]
         sums = outer(
             [(rows_two[i], both[i][k]) for i in sides],
             [(grad_rows[i], hidden[i][k]) for i in sides],
         )
+        if k < CHUNKS - 1:
+            grad_parts = [
+                project([both[i][k]], [ffn_weights[k]], 0, dtype=f32) for i in sides
+            ]
+            grad_parts, ffn_weights[k + 1] = together(grad_parts, ffn_weights[k + 1])
         if k == CHUNKS - 1:
             grad_state, sums = beside(scatter_second(scatter_first(*grad_parts)), sums)
         ffn_sums.append(scatter_line(sums))

time: 690 us -> 680 us (0.986)
  waiting for transfers between devices: 255 us -> 235 us
  Pallas kernels: 212 us -> 225 us
    all_gather x3, waiting for transfers between devices: 47.7 us -> 10.6 us  [gather_line(): return lax.all_gather(block, 'z', axis=0, tiled=True)]
    ppermute x47, waiting for transfers between devices: 155 us -> 165 us  [swap(): return lax.ppermute(value, axis, [(0, 1), (1, 0)])]
    pallas_call x4 -> x6, Pallas kernels: 54.4 us -> 64.2 us  [project(): pl.pallas_call(functools.partial(project_kernel, first, len(acts)), grid=...]
    unnamed x83 -> x81, local copies, waits for them, and re-layouts: 20.5 us -> 21 us
  transfers between devices with their start and end apart: 68 -> 68, of which waited for: 33 -> 36; matrix products, arithmetic and copies ran while one was open for 16% -> 17% of each run, Pallas kernels for 31% -> 33%
where the time goes in v6:
time: 680 us; the launch traced here: 675 us
  waiting for transfers between devices  235 us (35%)
  Pallas kernels  225 us (33%)
  starting transfers between devices  76 us (11%)
  other arithmetic  63 us (9%)
  local copies, waits for them, and re-layouts  60.8 us (9%)
  between operations  15.4 us (2%)
    ppermute x47, waiting for transfers between devices, swap(): return lax.ppermute(value, axis, [(0, 1), (1, 0)])  165 us
    pallas_call x6, Pallas kernels, project(): pl.pallas_call(functools.partial(project_kernel, first, len(acts)), grid=...  64.2 us
    pallas_call x3, Pallas kernels, outer(): pl.pallas_call(functools.partial(outer_kernel, [len(group) for group in g...  55.1 us
    pallas_call x4, Pallas kernels, gated(): pl.pallas_call(functools.partial(gated_kernel, units), grid=(total // til...  49.2 us
    ppermute x47, starting transfers between devices, swap(): return lax.ppermute(value, axis, [(0, 1), (1, 0)])  41.2 us
    pallas_call x2, Pallas kernels, attend_back(): pl.pallas_call(functools.partial(attend_back_kernel, width), grid=(total...  28.4 us
    all_to_all x3, waiting for transfers between devices, to_columns(): block = lax.all_to_all(parts, ('y', 'c'), 0, 0, tiled=True)  27.6 us
    pallas_call x2, Pallas kernels, attend(): pl.pallas_call(functools.partial(attend_kernel, width), grid=(total // se...  25.6 us
  transfers between devices with their start and end apart: 68, of which 36 were waited for; matrix products, arithmetic and copies ran while one was open for 17% of the time, Pallas kernels for 33%

profile of v6, /device:TPU:0, one launch (start us, length us, event | category | flops | bytes accessed | tf_op | source)
XLA Modules:
  0.0 674.9 jit_solution(14784699575680231926)
XLA Ops:
  20.2 8.1 %all-to-all-done = bf16[4,128,1024]{2,1,0:T(8,128)(2,1)S(1)} async-done(((bf16[4,128,1024]{2,1,0:T(8,128)(2,1)}), bf16[4,128,1024]{2,1,0:T(8,128)(2,1)S(1)}, u32[]{:S(2)}, u32[]{:S(2)}) %all-to-all-start) | async-done | bytes 1048608 | tf_op jit(solution)/shard_map/all_to_all | solution.py:326
  61.3 11.2 %collective-permute-done.10 = bf16[256,2048]{1,0:T(8,128)(2,1)} collective-permute-done((bf16[256,2048]{1,0:T(8,128)(2,1)}, bf16[256,2048]{1,0:T(8,128)(2,1)}, u32[]{:S(2)}, u32[]{:S(2)}) %collective-permute-start.10) | collective-permute-done | bytes 1048608 | tf_op jit(solution)/shard_map/ppermute | solution.py:272
  76.3 10.2 %all-to-all-done.1 = bf16[4,128,1536]{2,1,0:T(8,128)(2,1)} async-done(((bf16[4,128,1536]{2,1,0:T(8,128)(2,1)}), bf16[4,128,1536]{2,1,0:T(8,128)(2,1)}, u32[]{:S(2)}, u32[]{:S(2)}) %all-to-all-start.1) | async-done | bytes 1572896 | tf_op jit(solution)/shard_map/all_to_all | solution.py:326
  100.6 10.6 %all-gather.4.cloned.1.call-done.w_ref = bf16[2048,1024]{1,0:T(8,128)(2,1)} async-done(((bf16[512,1024]{1,0:T(8,128)(2,1)}), bf16[2048,1024]{1,0:T(8,128)(2,1)}) %all-gather.4.cloned.1.call-update) | async-done | bytes 4194320 | tf_op jit(solution)/shard_map/all_gather | solution.py:336
  120.5 12.7 %shard_map.204 = (bf16[1024,768]{1,0:T(8,128)(2,1)}, bf16[1024,256]{1,0:T(8,128)(2,1)}, bf16[1024,2048]{1,0:T(8,128)(2,1)}) custom-call(bf16[1024,2048]{1,0:T(8,128)(2,1)} %constant_dynamic-update-slice_fusion.rows_ref.refs_0_, bf16[2048,1024]{1,0:T(8,128)(2,1)} %all-gather.4.cloned.1.call-done.w_ref, f32[1024,128]{1,0:T(8,128)} %get-tuple-element.301.cos_ref, ...), custom_call_target="tpu_custom_call" | custom-call | flops 4831838208 | bytes 14680064 | tf_op jit(solution)/shard_map/pallas_call | solution.py:84
  143.7 12.9 %shard_map.205 = (bf16[1024,768]{1,0:T(8,128)(2,1)}, bf16[1024,256]{1,0:T(8,128)(2,1)}, bf16[1024,2048]{1,0:T(8,128)(2,1)}) custom-call(bf16[1024,2048]{1,0:T(8,128)(2,1)} %collective-permute-done.15.rows_ref.refs_2_, bf16[2048,1024]{1,0:T(8,128)(2,1)} %all-gather.4.cloned.1.call-done.w_ref, f32[1024,128]{1,0:T(8,128)} %get-tuple-element.300.cos_ref, ...), custom_call_target="tpu_custom_call" | custom-call | flops 4831838208 | bytes 14680064 | tf_op jit(solution)/shard_map/pallas_call | solution.py:84
  156.6 7.4 %collective-permute-done.16 = bf16[1024,2048]{1,0:T(8,128)(2,1)S(1)} collective-permute-done((bf16[1024,2048]{1,0:T(8,128)(2,1)}, bf16[1024,2048]{1,0:T(8,128)(2,1)S(1)}, u32[]{:S(2)}, u32[]{:S(2)}) %collective-permute-start.16) | collective-permute-done | bytes 4194336 | tf_op jit(solution)/shard_map/ppermute | solution.py:272
  173.7 19.9 %collective-permute-done.17 = bf16[256,2048]{1,0:T(8,128)(2,1)} collective-permute-done((bf16[256,2048]{1,0:T(8,128)(2,1)}, bf16[256,2048]{1,0:T(8,128)(2,1)}, u32[]{:S(2)}, u32[]{:S(2)}) %collective-permute-start.17) | collective-permute-done | bytes 1048608 | tf_op jit(solution)/shard_map/ppermute | solution.py:272
  202.2 9.3 %all-to-all-done.2 = bf16[4,128,1536]{2,1,0:T(8,128)(2,1)S(1)} async-done(((bf16[4,128,1536]{2,1,0:T(8,128)(2,1)}), bf16[4,128,1536]{2,1,0:T(8,128)(2,1)S(1)}, u32[]{:S(2)}, u32[]{:S(2)}) %all-to-all-start.2) | async-done | bytes 1572896 | tf_op jit(solution)/shard_map/all_to_all | solution.py:326
  212.7 12.0 %collective-permute-done.19 = bf16[128,2048]{1,0:T(8,128)(2,1)} collective-permute-done((bf16[128,2048]{1,0:T(8,128)(2,1)}, bf16[128,2048]{1,0:T(8,128)(2,1)}, u32[]{:S(2)}, u32[]{:S(2)}) %collective-permute-start.19) | collective-permute-done | bytes 524320 | tf_op jit(solution)/shard_map/ppermute | solution.py:272
  231.3 20.9 %collective-permute-done.22 = bf16[256,2048]{1,0:T(8,128)(2,1)S(1)} collective-permute-done((bf16[256,2048]{1,0:T(8,128)(2,1)S(1)}, bf16[256,2048]{1,0:T(8,128)(2,1)S(1)}, u32[]{:S(2)}, u32[]{:S(2)}) %collective-permute-start.22) | collective-permute-done | bytes 1048608 | tf_op jit(solution)/shard_map/ppermute | solution.py:272
  257.3 7.4 %collective-permute-done.24 = bf16[128,2048]{1,0:T(8,128)(2,1)S(1)} collective-permute-done((bf16[128,2048]{1,0:T(8,128)(2,1)S(1)}, bf16[128,2048]{1,0:T(8,128)(2,1)S(1)}, u32[]{:S(2)}, u32[]{:S(2)}) %collective-permute-start.24) | collective-permute-done | bytes 524320 | tf_op jit(solution)/shard_map/ppermute | solution.py:272
  278.2 12.3 %shard_map.206 = (bf16[1024,1024]{1,0:T(8,128)(2,1)}, bf16[1024,512]{1,0:T(8,128)(2,1)}) custom-call(bf16[1024,2048]{1,0:T(8,128)(2,1)} %constant_dynamic-update-slice_fusion.5.rows_ref.refs_0_, bf16[1024,2048]{1,0:T(8,128)(2,1)} %constant_dynamic-update-slice_fusion.10.grad_ref.refs_4_, bf16[2048,1536]{1,0:T(8,128)(2,1)} %all-gather.6.cloned.1.call-done.w_ref.refs_1_.refs_2_), custom_call_target="tpu_custom_call" | custom-call | flops 6442450944 | bytes 17825792 | tf_op jit(solution)/shard_map/pallas_call | solution.py:157
  290.5 12.4 %shard_map.208 = (bf16[1024,1024]{1,0:T(8,128)(2,1)}, bf16[1024,512]{1,0:T(8,128)(2,1)}) custom-call(bf16[1024,2048]{1,0:T(8,128)(2,1)} %collective-permute-done.27.rows_ref.refs_2_, bf16[1024,2048]{1,0:T(8,128)(2,1)} %collective-permute-done.28.grad_ref.refs_6_, bf16[2048,1536]{1,0:T(8,128)(2,1)} %all-gather.6.cloned.1.call-done.w_ref.refs_1_.refs_2_), custom_call_target="tpu_custom_call" | custom-call | flops 6442450944 | bytes 17825792 | tf_op jit(solution)/shard_map/pallas_call | solution.py:157
  302.9 19.4 %shard_map.219 = bf16[2048,1536]{1,0:T(8,128)(2,1)} custom-call(bf16[1024,2048]{1,0:T(8,128)(2,1)} %constant_dynamic-update-slice_fusion.5.rows_ref.refs_0_, bf16[1024,1024]{1,0:T(8,128)(2,1)} %get-tuple-element.176.refs_0_.refs_1_, bf16[1024,2048]{1,0:T(8,128)(2,1)} %collective-permute-done.27.rows_ref.refs_2_, ...), custom_call_target="tpu_custom_call" | custom-call | flops 12884901888 | bytes 29360128 | tf_op jit(solution)/shard_map/pallas_call | solution.py:222
  322.4 9.8 %shard_map.207.refs_2_ = f32[1024,2048]{1,0:T(8,128)} custom-call(bf16[1024,1024]{1,0:T(8,128)(2,1)} %get-tuple-element.176.refs_0_.refs_1_, bf16[2048,1536]{1,0:T(8,128)(2,1)} %all-gather.6.cloned.1.call-done.w_ref.refs_1_.refs_2_), custom_call_target="tpu_custom_call" | custom-call | flops 4294967296 | bytes 16777216 | tf_op jit(solution)/shard_map/pallas_call | solution.py:183
  332.2 9.6 %shard_map.209.refs_2_ = f32[1024,2048]{1,0:T(8,128)} custom-call(bf16[1024,1024]{1,0:T(8,128)(2,1)} %get-tuple-element.177.refs_0_.refs_3_, bf16[2048,1536]{1,0:T(8,128)(2,1)} %all-gather.6.cloned.1.call-done.w_ref.refs_1_.refs_2_), custom_call_target="tpu_custom_call" | custom-call | flops 4294967296 | bytes 16777216 | tf_op jit(solution)/shard_map/pallas_call | solution.py:183
  341.8 12.3 %shard_map.212 = (bf16[1024,1024]{1,0:T(8,128)(2,1)}, bf16[1024,512]{1,0:T(8,128)(2,1)}) custom-call(bf16[1024,2048]{1,0:T(8,128)(2,1)} %collective-permute-done.27.rows_ref.refs_2_, bf16[1024,2048]{1,0:T(8,128)(2,1)} %collective-permute-done.28.grad_ref.refs_6_, bf16[2048,1536]{1,0:T(8,128)(2,1)} %all-gather.8.cloned.1.call-done.w_ref.refs_1_.refs_3_), custom_call_target="tpu_custom_call" | custom-call | flops 6442450944 | bytes 17825792 | tf_op jit(solution)/shard_map/pallas_call | solution.py:157
  354.1 10.8 %shard_map.213 = bf16[1024,2048]{1,0:T(8,128)(2,1)} custom-call(bf16[1024,1024]{1,0:T(8,128)(2,1)} %get-tuple-element.182.refs_0_.refs_3_, bf16[2048,1536]{1,0:T(8,128)(2,1)} %all-gather.8.cloned.1.call-done.w_ref.refs_1_.refs_3_, f32[1024,2048]{1,0:T(8,128)} %shard_map.209.refs_2_), custom_call_target="tpu_custom_call" | custom-call | flops 4294967296 | bytes 20971520 | tf_op jit(solution)/shard_map/pallas_call | solution.py:183
  365.4 12.3 %shard_map.210 = (bf16[1024,1024]{1,0:T(8,128)(2,1)}, bf16[1024,512]{1,0:T(8,128)(2,1)}) custom-call(bf16[1024,2048]{1,0:T(8,128)(2,1)} %constant_dynamic-update-slice_fusion.5.rows_ref.refs_0_, bf16[1024,2048]{1,0:T(8,128)(2,1)} %constant_dynamic-update-slice_fusion.10.grad_ref.refs_4_, bf16[2048,1536]{1,0:T(8,128)(2,1)} %all-gather.8.cloned.1.call-done.w_ref.refs_1_.refs_3_), custom_call_target="tpu_custom_call" | custom-call | flops 6442450944 | bytes 17825792 | tf_op jit(solution)/shard_map/pallas_call | solution.py:157
  377.7 10.8 %shard_map.211 = bf16[1024,2048]{1,0:T(8,128)(2,1)} custom-call(bf16[1024,1024]{1,0:T(8,128)(2,1)} %get-tuple-element.180.refs_0_.refs_1_, bf16[2048,1536]{1,0:T(8,128)(2,1)} %all-gather.8.cloned.1.call-done.w_ref.refs_1_.refs_3_, f32[1024,2048]{1,0:T(8,128)} %shard_map.207.refs_2_), custom_call_target="tpu_custom_call" | custom-call | flops 4294967296 | bytes 20971520 | tf_op jit(solution)/shard_map/pallas_call | solution.py:183
  397.1 19.7 %shard_map.214 = bf16[2048,1536]{1,0:T(8,128)(2,1)} custom-call(bf16[1024,2048]{1,0:T(8,128)(2,1)} %constant_dynamic-update-slice_fusion.5.rows_ref.refs_0_, bf16[1024,1024]{1,0:T(8,128)(2,1)} %get-tuple-element.180.refs_0_.refs_1_, bf16[1024,2048]{1,0:T(8,128)(2,1)} %collective-permute-done.27.rows_ref.refs_2_, ...), custom_call_target="tpu_custom_call" | custom-call | flops 12884901888 | bytes 29360128 | tf_op jit(solution)/shard_map/pallas_call | solution.py:222
  430.3 11.2 %collective-permute-done.32 = bf16[128,2048]{1,0:T(8,128)(2,1)S(1)} collective-permute-done((bf16[128,2048]{1,0:T(8,128)(2,1)}, bf16[128,2048]{1,0:T(8,128)(2,1)S(1)}, u32[]{:S(2)}, u32[]{:S(2)}) %collective-permute-start.32) | collective-permute-done | bytes 524320 | tf_op jit(solution)/shard_map/ppermute | solution.py:272
  449.9 11.2 %shard_map.216 = bf16[1024,2048]{1,0:T(8,128)(2,1)} custom-call(bf16[1024,512]{1,0:T(8,128)(2,1)} %get-tuple-element.199.refs_0_.refs_7_, bf16[1024,512]{1,0:T(8,128)(2,1)} %get-tuple-element.189.refs_7_.refs_1_, bf16[2048,1536]{1,0:T(8,128)(2,1)} %all-gather.6.cloned.1.call-done.w_ref.refs_1_.refs_2_, ...), custom_call_target="tpu_custom_call" | custom-call | flops 4294967296 | bytes 18874368 | tf_op jit(solution)/shard_map/pallas_call | solution.py:183
  461.1 12.0 %shard_map.215 = bf16[1024,2048]{1,0:T(8,128)(2,1)} custom-call(bf16[1024,512]{1,0:T(8,128)(2,1)} %get-tuple-element.198.refs_0_.refs_5_, bf16[1024,512]{1,0:T(8,128)(2,1)} %get-tuple-element.188.refs_5_.refs_1_, bf16[2048,1536]{1,0:T(8,128)(2,1)} %all-gather.6.cloned.1.call-done.w_ref.refs_1_.refs_2_, ...), custom_call_target="tpu_custom_call" | custom-call | flops 4294967296 | bytes 18874368 | tf_op jit(solution)/shard_map/pallas_call | solution.py:183
  478.6 9.0 %collective-permute-done.37 = bf16[128,2048]{1,0:T(8,128)(2,1)S(1)} collective-permute-done((bf16[128,2048]{1,0:T(8,128)(2,1)S(1)}, bf16[128,2048]{1,0:T(8,128)(2,1)S(1)}, u32[]{:S(2)}, u32[]{:S(2)}) %collective-permute-start.37) | collective-permute-done | bytes 524320 | tf_op jit(solution)/shard_map/ppermute | solution.py:272
  501.7 14.4 %shard_map.218 = (bf16[1024,768]{1,0:T(8,128)(2,1)}, bf16[1024,2048]{1,0:T(8,128)(2,1)}) custom-call(bf16[1024,2048]{1,0:T(8,128)(2,1)} %collective-permute-done.41.grad_ref.refs_6_, bf16[2048,1024]{1,0:T(8,128)(2,1)} %all-gather.4.cloned.1.call-done.w_ref, bf16[1024,768]{1,0:T(8,128)(2,1)} %get-tuple-element.215.qkv_ref, ...), custom_call_target="tpu_custom_call" | custom-call | flops 5637144576 | bytes 15728640 | tf_op jit(solution)/shard_map/pallas_call | solution.py:119
  516.1 14.1 %shard_map.217 = (bf16[1024,768]{1,0:T(8,128)(2,1)}, bf16[1024,2048]{1,0:T(8,128)(2,1)}) custom-call(bf16[1024,2048]{1,0:T(8,128)(2,1)} %constant_dynamic-update-slice_fusion.15.grad_ref.refs_4_, bf16[2048,1024]{1,0:T(8,128)(2,1)} %all-gather.4.cloned.1.call-done.w_ref, bf16[1024,768]{1,0:T(8,128)(2,1)} %get-tuple-element.213.qkv_ref, ...), custom_call_target="tpu_custom_call" | custom-call | flops 5637144576 | bytes 15728640 | tf_op jit(solution)/shard_map/pallas_call | solution.py:119
  530.2 7.5 %collective-permute-done.40 = bf16[256,2048]{1,0:T(8,128)(2,1)S(1)} collective-permute-done((bf16[256,2048]{1,0:T(8,128)(2,1)S(1)}, bf16[256,2048]{1,0:T(8,128)(2,1)S(1)}, u32[]{:S(2)}, u32[]{:S(2)}) %collective-permute-start.40) | collective-permute-done | bytes 1048608 | tf_op jit(solution)/shard_map/ppermute | solution.py:272
  544.2 16.0 %shard_map.220 = bf16[2048,1024]{1,0:T(8,128)(2,1)} custom-call(bf16[1024,2048]{1,0:T(8,128)(2,1)} %constant_dynamic-update-slice_fusion.rows_ref.refs_0_, bf16[1024,768]{1,0:T(8,128)(2,1)} %get-tuple-element.217.refs_1_, bf16[1024,2048]{1,0:T(8,128)(2,1)} %collective-permute-done.15.rows_ref.refs_2_, bf16[1024,768]{1,0:T(8,128)(2,1)} %get-tuple-element.218.refs_3_, ...), custom_call_target="tpu_custom_call" | custom-call | flops 8589934592 | bytes 25165824 | tf_op jit(solution)/shard_map/pallas_call | solution.py:222
  570.0 22.2 %collective-permute-done.45 = bf16[256,2048]{1,0:T(8,128)(2,1)S(1)} collective-permute-done((bf16[256,2048]{1,0:T(8,128)(2,1)S(1)}, bf16[256,2048]{1,0:T(8,128)(2,1)S(1)}, u32[]{:S(2)}, u32[]{:S(2)}) %collective-permute-start.45) | collective-permute-done | bytes 1048608 | tf_op jit(solution)/shard_map/ppermute | solution.py:272
  627.4 13.4 %all-to-all-done.5 = bf16[4,128,1536]{2,1,0:T(8,128)(2,1)} async-done(((bf16[4,128,1536]{2,1,0:T(8,128)(2,1)}), bf16[4,128,1536]{2,1,0:T(8,128)(2,1)}, u32[]{:S(2)}, u32[]{:S(2)}) %all-to-all-start.5) | async-done | bytes 1572896 | tf_op jit(solution)/shard_map/all_to_all | solution.py:332
  (318 shorter events, 256.5 us)
Async XLA Ops:
  9.6 18.7 %all-to-all-start = ((bf16[4,128,1024]{2,1,0:T(8,128)(2,1)}), bf16[4,128,1024]{2,1,0:T(8,128)(2,1)S(1)}, u32[]{:S(2)}, u32[]{:S(2)}) async-start(bf16[4,128,1024]{2,1,0:T(8,128)(2,1)} %shard_map.203), calls=%async_computation | async-start | bytes 2097152 | tf_op jit(solution)/shard_map/all_to_all | solution.py:326
  13.8 97.4 %all-gather.4.cloned.1.call-start = ((), (), s32[]{:S(2)}) async-start(), calls=%async_computation.9 | async-start | bytes 5242880 | tf_op jit(solution)/shard_map/all_gather | solution.py:336
  46.1 26.4 %collective-permute-start.10 = (bf16[256,2048]{1,0:T(8,128)(2,1)}, bf16[256,2048]{1,0:T(8,128)(2,1)}, u32[]{:S(2)}, u32[]{:S(2)}) collective-permute-start(bf16[256,2048]{1,0:T(8,128)(2,1)} %get-tuple-element.251), channel_id=1, source_target_pairs={{0,4},{4,0},{1,5},{5,1},{2,6},{6,2},{3,7},{7,3},{8,12},{12,8},{9,1... | collective-permute-start | bytes 3145736 | tf_op jit(solution)/shard_map/ppermute | solution.py:272
  46.5 26.1 %collective-permute-start.9 = (bf16[256,2048]{1,0:T(8,128)(2,1)}, bf16[256,2048]{1,0:T(8,128)(2,1)}, u32[]{:S(2)}, u32[]{:S(2)}) collective-permute-start(bf16[256,2048]{1,0:T(8,128)(2,1)} %get-tuple-element.251), channel_id=1, source_target_pairs={{0,1},{1,0},{2,3},{3,2},{4,5},{5,4},{6,7},{7,6},{8,9},{9,8},{10,11... | collective-permute-start | bytes 3145736 | tf_op jit(solution)/shard_map/ppermute | solution.py:272
  48.0 38.5 %all-to-all-start.1 = ((bf16[4,128,1536]{2,1,0:T(8,128)(2,1)}), bf16[4,128,1536]{2,1,0:T(8,128)(2,1)}, u32[]{:S(2)}, u32[]{:S(2)}) async-start(bf16[4,128,1536]{2,1,0:T(8,128)(2,1)} %pad_maximum_fusion.3), calls=%async_computation.1 | async-start | bytes 3145728 | tf_op jit(solution)/shard_map/all_to_all | solution.py:326
  52.4 225.8 %all-gather.6.cloned.1.call-start = ((), (), s32[]{:S(2)}) async-start(), calls=%async_computation.10 | async-start | bytes 7864320 | tf_op jit(solution)/shard_map/all_gather | solution.py:336
  111.2 32.5 %collective-permute-start.15 = (bf16[1024,2048]{1,0:T(8,128)(2,1)}, bf16[1024,2048]{1,0:T(8,128)(2,1)}, u32[]{:S(2)}, u32[]{:S(2)}) collective-permute-start(bf16[1024,2048]{1,0:T(8,128)(2,1)} %constant_dynamic-update-slice_fusion.rows_ref.refs_0_), channel_id=1, source_target_pairs={{0,2},{2,0},{1,3},{3,1},{4,6},{6,4},{5,7},{7,5},{8,10},{10,8},{9,1... | collective-permute-start | bytes 12582920 | tf_op jit(solution)/shard_map/ppermute | solution.py:272
  114.1 25.6 %collective-permute-start.14 = (bf16[256,2048]{1,0:T(8,128)(2,1)S(1)}, bf16[256,2048]{1,0:T(8,128)(2,1)S(1)}, u32[]{:S(2)}, u32[]{:S(2)}) collective-permute-start(bf16[256,2048]{1,0:T(8,128)(2,1)S(1)} %copy-done.7), channel_id=1, source_target_pairs={{0,4},{4,0},{1,5},{5,1},{2,6},{6,2},{3,7},{7,3},{8,12},{12,8},{9,1... | collective-permute-start | bytes 3145736 | tf_op jit(solution)/shard_map/ppermute | solution.py:272
  115.5 25.4 %collective-permute-start.13 = (bf16[256,2048]{1,0:T(8,128)(2,1)S(1)}, bf16[256,2048]{1,0:T(8,128)(2,1)}, u32[]{:S(2)}, u32[]{:S(2)}) collective-permute-start(bf16[256,2048]{1,0:T(8,128)(2,1)S(1)} %copy-done.7), channel_id=1, source_target_pairs={{0,1},{1,0},{2,3},{3,2},{4,5},{5,4},{6,7},{7,6},{8,9},{9,8},{10,11... | collective-permute-start | bytes 3145736 | tf_op jit(solution)/shard_map/ppermute | solution.py:272
  168.0 25.5 %collective-permute-start.17 = (bf16[256,2048]{1,0:T(8,128)(2,1)}, bf16[256,2048]{1,0:T(8,128)(2,1)}, u32[]{:S(2)}, u32[]{:S(2)}) collective-permute-start(bf16[256,2048]{1,0:T(8,128)(2,1)} %pad_maximum_fusion.7), channel_id=1, source_target_pairs={{0,1},{1,0},{2,3},{3,2},{4,5},{5,4},{6,7},{7,6},{8,9},{9,8},{10,11... | collective-permute-start | bytes 3145736 | tf_op jit(solution)/shard_map/ppermute | solution.py:272
  169.5 26.4 %collective-permute-start.18 = (bf16[256,2048]{1,0:T(8,128)(2,1)}, bf16[256,2048]{1,0:T(8,128)(2,1)}, u32[]{:S(2)}, u32[]{:S(2)}) collective-permute-start(bf16[256,2048]{1,0:T(8,128)(2,1)} %pad_maximum_fusion.8), channel_id=1, source_target_pairs={{0,4},{4,0},{1,5},{5,1},{2,6},{6,2},{3,7},{7,3},{8,12},{12,8},{9,1... | collective-permute-start | bytes 3145736 | tf_op jit(solution)/shard_map/ppermute | solution.py:272
  170.1 41.4 %all-to-all-start.2 = ((bf16[4,128,1536]{2,1,0:T(8,128)(2,1)}), bf16[4,128,1536]{2,1,0:T(8,128)(2,1)S(1)}, u32[]{:S(2)}, u32[]{:S(2)}) async-start(bf16[4,128,1536]{2,1,0:T(8,128)(2,1)} %pad_maximum_fusion.4), calls=%async_computation.2 | async-start | bytes 3145728 | tf_op jit(solution)/shard_map/all_to_all | solution.py:326
  173.6 168.2 %all-gather.8.cloned.1.call-start = ((), (), s32[]{:S(2)}) async-start(), calls=%async_computation.11 | async-start | bytes 7864320 | tf_op jit(solution)/shard_map/all_gather | solution.py:336
  212.7 278.1 %reduce-scatter.4.cloned.1.call-start = ((), (), s32[]{:S(2)}) async-start(), calls=%async_computation.12 | async-start | bytes 7864320 | tf_op jit(solution)/shard_map/reduce_scatter | solution.py:340
  229.3 23.0 %collective-permute-start.22 = (bf16[256,2048]{1,0:T(8,128)(2,1)S(1)}, bf16[256,2048]{1,0:T(8,128)(2,1)S(1)}, u32[]{:S(2)}, u32[]{:S(2)}) collective-permute-start(bf16[256,2048]{1,0:T(8,128)(2,1)S(1)} %get-tuple-element.247), channel_id=1, source_target_pairs={{0,4},{4,0},{1,5},{5,1},{2,6},{6,2},{3,7},{7,3},{8,12},{12,8},{9,1... | collective-permute-start | bytes 3145736 | tf_op jit(solution)/shard_map/ppermute | solution.py:272
  230.8 23.1 %collective-permute-start.21 = (bf16[256,2048]{1,0:T(8,128)(2,1)S(1)}, bf16[256,2048]{1,0:T(8,128)(2,1)S(1)}, u32[]{:S(2)}, u32[]{:S(2)}) collective-permute-start(bf16[256,2048]{1,0:T(8,128)(2,1)S(1)} %get-tuple-element.247), channel_id=1, source_target_pairs={{0,1},{1,0},{2,3},{3,2},{4,5},{5,4},{6,7},{7,6},{8,9},{9,8},{10,11... | collective-permute-start | bytes 3145736 | tf_op jit(solution)/shard_map/ppermute | solution.py:272
  322.3 294.0 %reduce-scatter.8.cloned.1.call-start = ((), (), s32[]{:S(2)}) async-start(), calls=%async_computation.14 | async-start | bytes 7864320 | tf_op jit(solution)/shard_map/reduce_scatter | solution.py:340
  364.9 23.6 %collective-permute-start.29 = (bf16[1024,2048]{1,0:T(8,128)(2,1)}, bf16[1024,2048]{1,0:T(8,128)(2,1)S(1)}, u32[]{:S(2)}, u32[]{:S(2)}) collective-permute-start(bf16[1024,2048]{1,0:T(8,128)(2,1)} %shard_map.213), channel_id=1, source_target_pairs={{0,2},{2,0},{1,3},{3,1},{4,6},{6,4},{5,7},{7,5},{8,10},{10,8},{9,1... | collective-permute-start | bytes 12582920 | tf_op jit(solution)/shard_map/ppermute | solution.py:272
  394.4 25.5 %collective-permute-start.30 = (bf16[256,2048]{1,0:T(8,128)(2,1)}, bf16[256,2048]{1,0:T(8,128)(2,1)}, u32[]{:S(2)}, u32[]{:S(2)}) collective-permute-start(bf16[256,2048]{1,0:T(8,128)(2,1)} %pad_maximum_fusion.9), channel_id=1, source_target_pairs={{0,1},{1,0},{2,3},{3,2},{4,5},{5,4},{6,7},{7,6},{8,9},{9,8},{10,11... | collective-permute-start | bytes 3145736 | tf_op jit(solution)/shard_map/ppermute | solution.py:272
  395.6 25.4 %collective-permute-start.31 = (bf16[256,2048]{1,0:T(8,128)(2,1)}, bf16[256,2048]{1,0:T(8,128)(2,1)}, u32[]{:S(2)}, u32[]{:S(2)}) collective-permute-start(bf16[256,2048]{1,0:T(8,128)(2,1)} %pad_maximum_fusion.10), channel_id=1, source_target_pairs={{0,4},{4,0},{1,5},{5,1},{2,6},{6,2},{3,7},{7,3},{8,12},{12,8},{9,1... | collective-permute-start | bytes 3145736 | tf_op jit(solution)/shard_map/ppermute | solution.py:272
  448.8 24.3 %collective-permute-start.35 = (bf16[256,2048]{1,0:T(8,128)(2,1)S(1)}, bf16[256,2048]{1,0:T(8,128)(2,1)S(1)}, u32[]{:S(2)}, u32[]{:S(2)}) collective-permute-start(bf16[256,2048]{1,0:T(8,128)(2,1)S(1)} %get-tuple-element.244), channel_id=1, source_target_pairs={{0,4},{4,0},{1,5},{5,1},{2,6},{6,2},{3,7},{7,3},{8,12},{12,8},{9,1... | collective-permute-start | bytes 3145736 | tf_op jit(solution)/shard_map/ppermute | solution.py:272
  449.3 23.7 %collective-permute-start.34 = (bf16[256,2048]{1,0:T(8,128)(2,1)S(1)}, bf16[256,2048]{1,0:T(8,128)(2,1)S(1)}, u32[]{:S(2)}, u32[]{:S(2)}) collective-permute-start(bf16[256,2048]{1,0:T(8,128)(2,1)S(1)} %get-tuple-element.244), channel_id=1, source_target_pairs={{0,1},{1,0},{2,3},{3,2},{4,5},{5,4},{6,7},{7,6},{8,9},{9,8},{10,11... | collective-permute-start | bytes 3145736 | tf_op jit(solution)/shard_map/ppermute | solution.py:272
  473.2 22.0 %collective-permute-start.36 = (bf16[1024,2048]{1,0:T(8,128)(2,1)}, bf16[1024,2048]{1,0:T(8,128)(2,1)}, u32[]{:S(2)}, u32[]{:S(2)}) collective-permute-start(bf16[1024,2048]{1,0:T(8,128)(2,1)} %shard_map.216), channel_id=1, source_target_pairs={{0,2},{2,0},{1,3},{3,1},{4,6},{6,4},{5,7},{7,5},{8,10},{10,8},{9,1... | collective-permute-start | bytes 12582920 | tf_op jit(solution)/shard_map/ppermute | solution.py:272
  490.7 51.6 %all-to-all-start.3 = ((bf16[4,128,1536]{2,1,0:T(8,128)(2,1)}), bf16[4,128,1536]{2,1,0:T(8,128)(2,1)}, u32[]{:S(2)}, u32[]{:S(2)}) async-start(bf16[4,128,1536]{2,1,0:T(8,128)(2,1)} %bitcast.130), calls=%async_computation.4 | async-start | bytes 3145728 | tf_op jit(solution)/shard_map/all_to_all | solution.py:332
  495.1 150.9 %reduce-scatter.6.cloned.1.call-start = ((), (), s32[]{:S(2)}) async-start(), calls=%async_computation.13 | async-start | bytes 5242880 | tf_op jit(solution)/shard_map/reduce_scatter | solution.py:340
  498.3 31.9 %collective-permute-start.39 = (bf16[256,2048]{1,0:T(8,128)(2,1)S(1)}, bf16[256,2048]{1,0:T(8,128)(2,1)S(1)}, u32[]{:S(2)}, u32[]{:S(2)}) collective-permute-start(bf16[256,2048]{1,0:T(8,128)(2,1)S(1)} %pad_maximum_fusion.11), channel_id=1, source_target_pairs={{0,1},{1,0},{2,3},{3,2},{4,5},{5,4},{6,7},{7,6},{8,9},{9,8},{10,11... | collective-permute-start | bytes 3145736 | tf_op jit(solution)/shard_map/ppermute | solution.py:272
  499.8 37.9 %collective-permute-start.40 = (bf16[256,2048]{1,0:T(8,128)(2,1)S(1)}, bf16[256,2048]{1,0:T(8,128)(2,1)S(1)}, u32[]{:S(2)}, u32[]{:S(2)}) collective-permute-start(bf16[256,2048]{1,0:T(8,128)(2,1)S(1)} %pad_maximum_fusion.12), channel_id=1, source_target_pairs={{0,4},{4,0},{1,5},{5,1},{2,6},{6,2},{3,7},{7,3},{8,12},{12,8},{9,1... | collective-permute-start | bytes 3145736 | tf_op jit(solution)/shard_map/ppermute | solution.py:272
  516.1 48.5 %collective-permute-start.44 = (bf16[1024,2048]{1,0:T(8,128)(2,1)}, bf16[1024,2048]{1,0:T(8,128)(2,1)}, u32[]{:S(2)}, u32[]{:S(2)}) collective-permute-start(bf16[1024,2048]{1,0:T(8,128)(2,1)} %get-tuple-element.229), channel_id=1, source_target_pairs={{0,2},{2,0},{1,3},{3,1},{4,6},{6,4},{5,7},{7,5},{8,10},{10,8},{9,1... | collective-permute-start | bytes 12582920 | tf_op jit(solution)/shard_map/ppermute | solution.py:272
  567.8 24.5 %collective-permute-start.45 = (bf16[256,2048]{1,0:T(8,128)(2,1)S(1)}, bf16[256,2048]{1,0:T(8,128)(2,1)S(1)}, u32[]{:S(2)}, u32[]{:S(2)}) collective-permute-start(bf16[256,2048]{1,0:T(8,128)(2,1)S(1)} %pad_maximum_fusion.13), channel_id=1, source_target_pairs={{0,1},{1,0},{2,3},{3,2},{4,5},{5,4},{6,7},{7,6},{8,9},{9,8},{10,11... | collective-permute-start | bytes 3145736 | tf_op jit(solution)/shard_map/ppermute | solution.py:272
  568.4 24.2 %collective-permute-start.46 = (bf16[256,2048]{1,0:T(8,128)(2,1)S(1)}, bf16[256,2048]{1,0:T(8,128)(2,1)S(1)}, u32[]{:S(2)}, u32[]{:S(2)}) collective-permute-start(bf16[256,2048]{1,0:T(8,128)(2,1)S(1)} %pad_maximum_fusion.14), channel_id=1, source_target_pairs={{0,4},{4,0},{1,5},{5,1},{2,6},{6,2},{3,7},{7,3},{8,12},{12,8},{9,1... | collective-permute-start | bytes 3145736 | tf_op jit(solution)/shard_map/ppermute | solution.py:272
  616.3 24.5 %all-to-all-start.5 = ((bf16[4,128,1536]{2,1,0:T(8,128)(2,1)}), bf16[4,128,1536]{2,1,0:T(8,128)(2,1)}, u32[]{:S(2)}, u32[]{:S(2)}) async-start(bf16[4,128,1536]{2,1,0:T(8,128)(2,1)} %bitcast.129), calls=%async_computation.8 | async-start | bytes 3145728 | tf_op jit(solution)/shard_map/all_to_all | solution.py:332
  646.0 18.0 %all-to-all-start.4 = ((bf16[4,128,1024]{2,1,0:T(8,128)(2,1)}), bf16[4,128,1024]{2,1,0:T(8,128)(2,1)S(1)}, u32[]{:S(2)}, u32[]{:S(2)}) async-start(bf16[4,128,1024]{2,1,0:T(8,128)(2,1)} %bitcast.134), calls=%async_computation.6 | async-start | bytes 2097152 | tf_op jit(solution)/shard_map/all_to_all | solution.py:332
  (70 other events, 588.5 us)
Sparse Core Ops, SparseCore 0:
  29.4 81.7 all-gather.3
  112.8 113.7 all-gather.5
  228.2 113.5 all-gather.7
  344.0 108.9 reduce-scatter.3
  455.1 111.2 reduce-scatter.7
  568.6 77.3 reduce-scatter.5
